TPU v7x, 32 devices: a whole 2x2x4 slice. The times are simulated.
32 devices in a mesh: row: 8 (over z, y), col: 4 (over x, core).
Axes of the slice: x: 2, y: 2, z: 4, core: 2. Of those that a mesh axis runs over, the one named last changes fastest.
Arguments:
- features: bfloat16 [4096, 2048], P(('row', 'col')), may hold values from -6 to 6
- neighbours: int32 [4096, 64], P('row', 'col'), may hold values from 0 to 1023
- edge_mask: int32 [4096, 64], P('row', 'col'), may hold values from 0 to 1, as said below
- weight: bfloat16 [2048, 2048], replicated, may hold values from -0.25 to 0.25
- bias: float32 [2048], replicated, may hold values from -4 to 4
- cotangent: bfloat16 [4096, 2048], P(('row', 'col')), may hold values from -6 to 6
Outputs:
- activations: bfloat16 [4096, 2048], P(('row', 'col'))
- feature_grad: float32 [4096, 2048], P(('row', 'col'))
- weight_grad: float32 [2048, 2048], replicated
- bias_grad: float32 [2048], replicated
Inputs may be any that keep to these rules, and one draw needn't show every extreme that they name: `edge_mask`: in every row and column block the ones come first; in every draw some rows are full in every block (hubs).
All inputs are finite; a program needn't handle non-finite values.
Results may differ from a plain program's by a relative error of at most 0.012.
Values may be sent and summed in bfloat16 or wider, within the bound.
A program may use at most 128 MiB of HBM per device.

v0:
```python
import jax
import jax.numpy as jnp
from jax import lax
from jax.sharding import PartitionSpec as P


def slot_matrix(lists, mask_float, width):
    columns = jnp.arange(width, dtype=jnp.int32)
    total = jnp.zeros((lists.shape[0], width), jnp.float32)
    for slot_index in range(lists.shape[1]):
        total = total + jnp.where(
            lists[:, slot_index, None] == columns[None, :], mask_float[:, slot_index, None], 0.0
        )
    return total.astype(jnp.bfloat16)


def on_device(features, neighbours, edge_mask, weight, bias, cotangent):
    mask_float = edge_mask.astype(jnp.float32)
    column_rows = lax.all_gather(features, "row", axis=0, tiled=True)
    adjacency = slot_matrix(neighbours, mask_float, column_rows.shape[0])
    partial_value = jnp.dot(adjacency, column_rows, preferred_element_type=jnp.float32)
    edge_count = jnp.sum(mask_float, axis=1)
    summed, degree = (
        lax.psum_scatter(partial_value, "col", scatter_dimension=0, tiled=True),
        lax.psum_scatter(edge_count, "col", scatter_dimension=0, tiled=True),
    )
    row_scale = 1.0 / (degree + 1.0)
    inputs_f = features.astype(jnp.float32)
    aggregated = row_scale[:, None] * (summed + 2.0 * inputs_f)
    aggregated_low = aggregated.astype(jnp.bfloat16)
    preact = jnp.dot(aggregated_low, weight, preferred_element_type=jnp.float32) + bias[None, :]
    activated, gelu_back = jax.vjp(jax.nn.gelu, preact)
    activations = activated.astype(jnp.bfloat16)
    preact_grad = gelu_back(cotangent.astype(jnp.float32))[0].astype(jnp.bfloat16)
    grad_agg = lax.dot_general(
        preact_grad, weight, (((1,), (1,)), ((), ())), preferred_element_type=jnp.float32
    )
    combined_grad = (row_scale[:, None] * grad_agg).astype(jnp.bfloat16)
    again_rows = lax.all_gather(features, "row", axis=0, tiled=True)
    again_partial = jnp.dot(adjacency, again_rows, preferred_element_type=jnp.float32)
    again_summed = lax.psum_scatter(again_partial, "col", scatter_dimension=0, tiled=True)
    used_low = (row_scale[:, None] * (again_summed + 2.0 * inputs_f)).astype(jnp.bfloat16)
    weight_term = lax.dot_general(
        used_low, preact_grad, (((0,), (0,)), ((), ())), preferred_element_type=jnp.float32
    )
    bias_term = jnp.sum(preact_grad.astype(jnp.float32), axis=0)
    weight_grad, bias_grad = lax.psum((weight_term, bias_term), ("row", "col"))
    block_grads = lax.all_gather(combined_grad, "col", axis=0, tiled=True)
    target = lax.dot_general(
        adjacency, block_grads, (((0,), (0,)), ((), ())), preferred_element_type=jnp.float32
    )
    returned = lax.psum_scatter(
        target.astype(jnp.bfloat16), "row", scatter_dimension=0, tiled=True
    ).astype(jnp.float32)
    feature_grad = returned + 2.0 * combined_grad.astype(jnp.float32)
    return (activations, feature_grad, weight_grad, bias_grad)


def solution(mesh):
    placed = (
        P(("row", "col"), None),
        P("row", "col"),
        P("row", "col"),
        P(),
        P(),
        P(("row", "col"), None),
    )
    return jax.shard_map(
        on_device,
        mesh=mesh,
        in_specs=placed,
        out_specs=(P(("row", "col"), None), P(("row", "col"), None), P(), P()),
        check_vma=False,
    )
```

profile of v0, /device:TPU:0, one launch (start us, length us, event | category | flops | bytes accessed | tf_op | source)
XLA Modules:
  0.0 578.1 jit_solution(262155284403124506)
XLA Ops:
  7.2 0.0 all-gather.3.cloned.1.call-start
  7.2 0.7 all-gather.3.cloned.1.call-update
  7.9 0.0 reduce-scatter.3.cloned.1.call-start
  7.9 0.8 convert_element_type.37
  8.7 1.1 fusion.14
  9.8 76.4 %all-gather.3.cloned.1.call-done = bf16[1024,2048]{1,0:T(8,128)(2,1)} async-done(((bf16[128,2048]{1,0:T(8,128)(2,1)}), bf16[1024,2048]{1,0:T(8,128)(2,1)}) %all-gather.3.cloned.1.call-update) | async-done | bytes 4194320 | tf_op jit(solution)/shard_map/all_gather | solution.py:19
  86.3 11.1 %fusion.12 = f32[512,2048]{1,0:T(8,128)} fusion(bf16[1024,2048]{1,0:T(8,128)(2,1)} %all-gather.3.cloned.1.call-done, f32[512]{0:T(512)S(1)} %bitcast.73, s32[512]{0:T(512)S(1)} %bitcast.103, f32[512]{0:T(512)S(1)} %bitcast.45, s32[512]{0:T(512)S(1)} %bitcast.105, f32[512]{0:T(512)S(1)} %bitcast.47, s32[512]{0:T(512)S(1)} %bitcast.77, f32[512]{0:T(512)S(1)} %bitcast.49, ...), kind=kOutput, calls=%fused_computation.42 | convolution fusion | flops 2172649472 | bytes 8454144 | tf_op jit(solution)/shard_map/dot_general | solution.py:21
  97.3 0.0 copy-start.5
  97.3 0.0 copy-start.2
  97.3 0.0 copy-start.1
  97.3 0.0 reduce-scatter.3.cloned.1.call-update
  97.4 0.0 copy-start.3
  97.4 0.0 copy-start.4
  97.4 0.0 all-gather.5.cloned.1.call-start
  97.4 0.5 copy-done.5
  98.0 0.6 dynamic-slice
  99.2 0.0 copy-done.2
  99.2 5.7 all-reduce
  104.9 0.1 fusion.11
  105.0 35.3 %reduce-scatter.3.cloned.1.call-done = f32[128,2048]{1,0:T(8,128)} async-done(((f32[512,2048]{1,0:T(8,128)}), f32[128,2048]{1,0:T(8,128)}) %reduce-scatter.3.cloned.1.call-update) | async-done | bytes 1048592 | tf_op jit(solution)/shard_map/reduce_scatter | solution.py:24
  140.3 0.0 copy-done.1
  140.3 0.0 slice-start
  140.3 1.5 multiply_convert_fusion.1
  141.9 0.0 copy-done.3
  141.9 0.0 copy-done.4
  141.9 0.0 slice-start.1
  141.9 6.5 %convert_reduce_fusion = (f32[2048]{0:T(1024)S(1)}, bf16[128,2048]{1,0:T(8,128)(2,1)S(1)}, bf16[128,2048]{1,0:T(8,128)(2,1)}) fusion(bf16[128,2048]{1,0:T(8,128)(2,1)S(1)} %copy-done.3, f32[2048]{0:T(1024)S(1)} %copy-done.4, bf16[128,2048]{1,0:T(8,128)(2,1)S(1)} %multiply_convert_fusion.1, bf16[2048,2048]{1,0:T(8,128)(2,1)} %param.9), kind=kOutput, calls=%fused_computation.35 | convolution fusion | flops 1080555520 | bytes 10502144 | tf_op jit(solution)/shard_map/dot_general | solution.py:31
  148.5 0.0 slice-done
  148.5 0.0 slice-done.1
  148.5 3.7 fusion
  152.2 0.0 all-gather.5.cloned.1.call-update
  152.2 0.2 reduce-scatter.5.cloned.1.call-start
  152.4 22.5 %all-gather.5.cloned.1.call-done = bf16[512,2048]{1,0:T(8,128)(2,1)} async-done(((bf16[128,2048]{1,0:T(8,128)(2,1)}), bf16[512,2048]{1,0:T(8,128)(2,1)}) %all-gather.5.cloned.1.call-update) | async-done | bytes 2097168 | tf_op jit(solution)/shard_map/all_gather | solution.py:48
  175.0 10.8 %convolution_convert_fusion = bf16[1024,2048]{1,0:T(8,128)(2,1)} fusion(bf16[512,2048]{1,0:T(8,128)(2,1)} %all-gather.5.cloned.1.call-done, f32[512]{0:T(512)S(1)} %bitcast.74, s32[512]{0:T(512)S(1)} %bitcast.104, f32[512]{0:T(512)S(1)} %bitcast.46, s32[512]{0:T(512)S(1)} %bitcast.106, f32[512]{0:T(512)S(1)} %bitcast.48, s32[512]{0:T(512)S(1)} %bitcast.78, ...), kind=kOutput, calls=%fused_computation | convolution fusion | flops 2174746624 | bytes 6356992 | tf_op jit(solution)/shard_map/dot_general | solution.py:49
  185.8 0.0 reduce-scatter.5.cloned.1.call-update
  185.8 0.0 all-reduce.3.cloned.1.call-start
  185.8 8.5 %fusion.16 = f32[2048,2048]{1,0:T(8,128)} fusion(bf16[128,2048]{1,0:T(8,128)(2,1)S(1)} %multiply_convert_fusion.1, bf16[128,2048]{1,0:T(8,128)(2,1)S(1)} %get-tuple-element.5), kind=kOutput, calls=%fused_computation.45 | convolution fusion | flops 1073741824 | bytes 17825792 | tf_op jit(solution)/shard_map/dot_general | solution.py:43
  194.4 0.0 copy-start
  194.4 0.0 all-reduce.3.cloned.1.call-update
  194.4 41.7 %psum.15 = f32[2048]{0:T(1024)} all-reduce(f32[2048]{0:T(1024)S(1)} %get-tuple-element.4), channel_id=1, replica_groups=mesh['row'=8,'col'=4] {'row','col'}, use_global_device_ids=true, to_apply=%region_6.7 | all-reduce | flops 2048 | bytes 16384 | tf_op jit(solution)/shard_map/psum | solution.py:47
  236.1 39.5 %reduce-scatter.5.cloned.1.call-done = bf16[128,2048]{1,0:T(8,128)(2,1)} async-done(((bf16[1024,2048]{1,0:T(8,128)(2,1)}), bf16[128,2048]{1,0:T(8,128)(2,1)}) %reduce-scatter.5.cloned.1.call-update) | async-done | bytes 524304 | tf_op jit(solution)/shard_map/reduce_scatter | solution.py:52
  275.5 0.0 copy-done
  275.5 2.2 multiply_add_fusion
  277.7 282.0 %all-reduce.3.cloned.1.call-done = f32[2048,2048]{1,0:T(8,128)} async-done(((f32[2048,2048]{1,0:T(8,128)}), f32[2048,2048]{1,0:T(8,128)}) %all-reduce.3.cloned.1.call-update) | async-done | bytes 16777232 | tf_op jit(solution)/shard_map/psum | solution.py:47
  559.8 11.8 %copy.11 = f32[2048,2048]{1,0:T(8,128)} copy(f32[2048,2048]{1,0:T(8,128)} %all-reduce.3.cloned.1.call-done) | data formatting | bytes 33554432
  (3 shorter events, 0.0 us)
Async XLA Ops:
  7.2 79.1 %all-gather.3.cloned.1.call-start = ((), (), s32[]{:S(2)}) async-start(), calls=%async_computation.2 | async-start | bytes 4718592 | tf_op jit(solution)/shard_map/all_gather | solution.py:19
  7.9 132.4 %reduce-scatter.3.cloned.1.call-start = ((), (), s32[]{:S(2)}) async-start(), calls=%async_computation.3 | async-start | bytes 5242880 | tf_op jit(solution)/shard_map/reduce_scatter | solution.py:24
  97.3 0.7 copy-start.5
  97.3 1.9 copy-start.2
  97.3 43.0 %copy-start.1 = (bf16[128,2048]{1,0:T(8,128)(2,1)S(1)}, bf16[128,2048]{1,0:T(8,128)(2,1)}, u32[]{:S(2)}) copy-start(bf16[128,2048]{1,0:T(8,128)(2,1)} %param.6) | copy-start | bytes 1572868
  97.4 44.5 %copy-start.3 = (bf16[128,2048]{1,0:T(8,128)(2,1)S(1)}, bf16[128,2048]{1,0:T(8,128)(2,1)}, u32[]{:S(2)}) copy-start(bf16[128,2048]{1,0:T(8,128)(2,1)} %param.11) | copy-start | bytes 1572868
  97.4 44.5 %copy-start.4 = (f32[2048]{0:T(1024)S(1)}, f32[2048]{0:T(1024)}, u32[]{:S(2)}) copy-start(f32[2048]{0:T(1024)} %param.10) | copy-start | bytes 24580
  97.4 77.6 %all-gather.5.cloned.1.call-start = ((), (), s32[]{:S(2)}) async-start(), calls=%async_computation.4 | async-start | bytes 2621440 | tf_op jit(solution)/shard_map/all_gather | solution.py:48
  140.3 8.1 %slice-start = ((s8[8388608]{0:T(1024)(128)(4,1)}), s8[4194304]{0:T(1024)(128)(4,1)S(1)}, s32[]{:S(2)}) async-start(s8[8388608]{0:T(1024)(128)(4,1)} %bitcast.41), calls=%async_computation.7 | async-start | bytes 8388608
  141.9 6.5 %slice-start.1 = ((s8[8388608]{0:T(1024)(128)(4,1)}), s8[4194304]{0:T(1024)(128)(4,1)S(1)}, s32[]{:S(2)}) async-start(s8[8388608]{0:T(1024)(128)(4,1)} %bitcast.41), calls=%async_computation.8 | async-start | bytes 8388608
  152.2 123.3 %reduce-scatter.5.cloned.1.call-start = ((), (), s32[]{:S(2)}) async-start(), calls=%async_computation.5 | async-start | bytes 4718592 | tf_op jit(solution)/shard_map/reduce_scatter | solution.py:52
  185.8 374.0 %all-reduce.3.cloned.1.call-start = ((), (), s32[]{:S(2)}) async-start(), calls=%async_computation.6 | async-start | bytes 33554432 | tf_op jit(solution)/shard_map/psum | solution.py:47
  194.4 81.2 %copy-start = (bf16[128,2048]{1,0:T(8,128)(2,1)S(1)}, bf16[128,2048]{1,0:T(8,128)(2,1)}, u32[]{:S(2)}) copy-start(bf16[128,2048]{1,0:T(8,128)(2,1)} %fusion) | copy-start | bytes 1572868
Sparse Core Ops, SparseCore 0:
  10.1 76.0 all-gather.2
  97.5 42.8 reduce-scatter.2
  152.3 22.5 all-gather.4
  185.9 89.5 reduce-scatter.4
  282.0 277.6 all-reduce.2
where the time goes:
time: 579 us; the launch traced here: 578 us
  waiting for transfers between devices  457 us (79%)
  blocking collectives  47.3 us (8%)
  matrix products  40.7 us (7%)
  between operations  14.5 us (3%)
  local copies, waits for them, and re-layouts  14.1 us (2%)
    psum x1, waiting for transfers between devices, on_device(): weight_grad, bias_grad = lax.psum((weight_term, bias_term), ('row', 'col'))  282 us
    all_gather x1, waiting for transfers between devices, on_device(): column_rows = lax.all_gather(features, 'row', axis=0, tiled=True)  76.4 us
    psum x1, blocking collectives, on_device(): weight_grad, bias_grad = lax.psum((weight_term, bias_term), ('row', 'col'))  41.7 us
    reduce_scatter x1, waiting for transfers between devices, on_device(): lax.psum_scatter(target.astype(jnp.bfloat16), 'row', scatter_dimension=0,...  39.5 us
    reduce_scatter x1, waiting for transfers between devices, on_device(): lax.psum_scatter(partial_value, 'col', scatter_dimension=0, tiled=True)  35.3 us
    all_gather x1, waiting for transfers between devices, on_device(): block_grads = lax.all_gather(combined_grad, 'col', axis=0, tiled=True)  22.5 us
    unnamed x18, local copies, waits for them, and re-layouts  13 us
  transfers between devices with their start and end apart: 5, of which 5 were waited for; matrix products, arithmetic and copies ran while one was open for 2% of the time, Pallas kernels for 0%

commit v1 on v0

--- a/solution.py
+++ b/solution.py
@@ -21,7 +21,7 @@
     partial_value = jnp.dot(adjacency, column_rows, preferred_element_type=jnp.float32)
     edge_count = jnp.sum(mask_float, axis=1)
     summed, degree = (
-        lax.psum_scatter(partial_value, "col", scatter_dimension=0, tiled=True),
+        lax.psum_scatter(partial_value.astype(jnp.bfloat16), "col", scatter_dimension=0, tiled=True).astype(jnp.float32),
         lax.psum_scatter(edge_count, "col", scatter_dimension=0, tiled=True),
     )
     row_scale = 1.0 / (degree + 1.0)
@@ -32,19 +32,15 @@
     activated, gelu_back = jax.vjp(jax.nn.gelu, preact)
     activations = activated.astype(jnp.bfloat16)
     preact_grad = gelu_back(cotangent.astype(jnp.float32))[0].astype(jnp.bfloat16)
+    weight_term = lax.dot_general(
+        aggregated_low, preact_grad, (((0,), (0,)), ((), ())), preferred_element_type=jnp.float32
+    )
+    weight_grad = lax.psum(weight_term.astype(jnp.bfloat16), ("row", "col")).astype(jnp.float32)
+    bias_grad = lax.psum(jnp.sum(preact_grad.astype(jnp.float32), axis=0), ("row", "col"))
     grad_agg = lax.dot_general(
         preact_grad, weight, (((1,), (1,)), ((), ())), preferred_element_type=jnp.float32
     )
     combined_grad = (row_scale[:, None] * grad_agg).astype(jnp.bfloat16)
-    again_rows = lax.all_gather(features, "row", axis=0, tiled=True)
-    again_partial = jnp.dot(adjacency, again_rows, preferred_element_type=jnp.float32)
-    again_summed = lax.psum_scatter(again_partial, "col", scatter_dimension=0, tiled=True)
-    used_low = (row_scale[:, None] * (again_summed + 2.0 * inputs_f)).astype(jnp.bfloat16)
-    weight_term = lax.dot_general(
-        used_low, preact_grad, (((0,), (0,)), ((), ())), preferred_element_type=jnp.float32
-    )
-    bias_term = jnp.sum(preact_grad.astype(jnp.float32), axis=0)
-    weight_grad, bias_grad = lax.psum((weight_term, bias_term), ("row", "col"))
     block_grads = lax.all_gather(combined_grad, "col", axis=0, tiled=True)
     target = lax.dot_general(
         adjacency, block_grads, (((0,), (0,)), ((), ())), preferred_element_type=jnp.float32

time: 579 us -> 451 us (0.78)
  waiting for transfers between devices: 457 us -> 331 us
  local copies, waits for them, and re-layouts: 14.1 us -> 2.27 us
  other arithmetic: 4.58 us -> 14.7 us
    psum x1, waiting for transfers between devices: 282 us -> 135 us  [on_device(): lax.psum(weight_term.astype(jnp.bfloat16), ('row', 'col'))]
    reduce_scatter x1, waiting for transfers between devices: 39.5 us -> 80.2 us  [on_device(): lax.psum_scatter(target.astype(jnp.bfloat16), 'row', scatter_dimension=0,...]
    reduce_scatter x1, waiting for transfers between devices: 35.3 us -> 22.2 us  [on_device(): lax.psum_scatter(partial_value.astype(jnp.bfloat16), 'col', scatter_dimen...]
    unnamed x18 -> x15, local copies, waits for them, and re-layouts: 13 us -> 1.16 us
    convert_element_type x1, other arithmetic: 1.55 us -> 11.7 us  [on_device(): lax.psum(weight_term.astype(jnp.bfloat16), ('row', 'col'))]
    all_gather x1, waiting for transfers between devices: 22.5 us -> 16.6 us  [on_device(): block_grads = lax.all_gather(combined_grad, 'col', axis=0, tiled=True)]
  transfers between devices with their start and end apart: 5 -> 5, of which waited for: 5 -> 5; matrix products, arithmetic and copies ran while one was open for 2% -> 7% of each run, Pallas kernels for 0% -> 0%
where the time goes in v1:
time: 451 us
  waiting for transfers between devices  331 us (73%)
  blocking collectives  46.8 us (10%)
  matrix products  41.1 us (9%)
  other arithmetic  14.7 us (3%)
  between operations  14.5 us (3%)
    psum x1, waiting for transfers between devices, on_device(): lax.psum(weight_term.astype(jnp.bfloat16), ('row', 'col'))  135 us
    reduce_scatter x1, waiting for transfers between devices, on_device(): lax.psum_scatter(target.astype(jnp.bfloat16), 'row', scatter_dimension=0,...  80.2 us
    all_gather x1, waiting for transfers between devices, on_device(): column_rows = lax.all_gather(features, 'row', axis=0, tiled=True)  76.4 us
    psum x1, blocking collectives, on_device(): lax.psum(jnp.sum(preact_grad.astype(jnp.float32), axis=0), ('row', 'col'))  41.2 us
    reduce_scatter x1, waiting for transfers between devices, on_device(): lax.psum_scatter(partial_value.astype(jnp.bfloat16), 'col', scatter_dimen...  22.2 us
    all_gather x1, waiting for transfers between devices, on_device(): block_grads = lax.all_gather(combined_grad, 'col', axis=0, tiled=True)  16.6 us
    convert_element_type x1, other arithmetic, on_device(): lax.psum(weight_term.astype(jnp.bfloat16), ('row', 'col'))  11.7 us
    dot_general x1, matrix products, on_device(): lax.dot_general(adjacency, block_grads, (((0,), (0,)), ((), ())), preferr...  10.8 us
  transfers between devices with their start and end apart: 5, of which 5 were waited for; matrix products, arithmetic and copies ran while one was open for 7% of the time, Pallas kernels for 0%

profile of v1, /device:TPU:0, one launch (start us, length us, event | category | flops | bytes accessed | tf_op | source)
XLA Modules:
  0.0 450.7 jit_solution(6891400644419020358)
XLA Ops:
  7.2 0.0 all-gather.3.cloned.1.call-start
  7.2 0.7 all-gather.3.cloned.1.call-update
  7.9 0.0 reduce-scatter.3.cloned.1.call-start
  7.9 0.8 convert_element_type.48
  8.7 1.1 fusion.13
  9.8 76.4 %all-gather.3.cloned.1.call-done = bf16[1024,2048]{1,0:T(8,128)(2,1)} async-done(((bf16[128,2048]{1,0:T(8,128)(2,1)}), bf16[1024,2048]{1,0:T(8,128)(2,1)}) %all-gather.3.cloned.1.call-update) | async-done | bytes 4194320 | tf_op jit(solution)/shard_map/all_gather | solution.py:19
  86.3 10.7 %convolution_convert_fusion.2 = bf16[512,2048]{1,0:T(8,128)(2,1)} fusion(bf16[1024,2048]{1,0:T(8,128)(2,1)} %all-gather.3.cloned.1.call-done, f32[512]{0:T(512)S(1)} %bitcast.69, s32[512]{0:T(512)S(1)} %bitcast.99, f32[512]{0:T(512)S(1)} %bitcast.41, s32[512]{0:T(512)S(1)} %bitcast.101, f32[512]{0:T(512)S(1)} %bitcast.43, s32[512]{0:T(512)S(1)} %bitcast.73, ...), kind=kOutput, calls=%fused_computation.2 | convolution fusion | flops 2173698048 | bytes 6356992 | tf_op jit(solution)/shard_map/dot_general | solution.py:21
  97.0 0.0 copy-start.6
  97.0 0.0 copy-start.3
  97.0 0.0 copy-start.1
  97.0 0.0 copy-start.4
  97.0 0.0 copy-start.5
  97.0 0.0 reduce-scatter.3.cloned.1.call-update
  97.0 0.0 all-gather.5.cloned.1.call-start
  97.1 0.6 copy-done.6
  97.6 0.6 dynamic-slice
  98.9 0.0 copy-done.3
  98.9 5.7 %all-reduce = f32[512]{0:T(512)S(1)} all-reduce(f32[512]{0:T(512)S(1)} %convert_reduce_fusion.1), channel_id=2, replica_groups=mesh['row'=8,'col'=4] {'col'}, use_global_device_ids=true, to_apply=%region_1.2.clone | all-reduce | flops 512 | bytes 4096
  104.6 0.1 fusion.11
  104.7 22.2 %reduce-scatter.3.cloned.1.call-done = bf16[128,2048]{1,0:T(8,128)(2,1)} async-done(((bf16[512,2048]{1,0:T(8,128)(2,1)}), bf16[128,2048]{1,0:T(8,128)(2,1)}) %reduce-scatter.3.cloned.1.call-update) | async-done | bytes 524304 | tf_op jit(solution)/shard_map/reduce_scatter | solution.py:24
  126.9 0.0 copy-done.1
  126.9 0.0 copy-done.4
  126.9 0.0 copy-done.5
  126.9 6.6 %convert_reduce_fusion = (f32[2048]{0:T(1024)S(1)}, bf16[128,2048]{1,0:T(8,128)(2,1)S(1)}, bf16[128,2048]{1,0:T(8,128)(2,1)}) fusion(bf16[128,2048]{1,0:T(8,128)(2,1)S(1)} %copy-done.4, f32[2048]{0:T(1024)S(1)} %copy-done.5, bf16[2048,2048]{1,0:T(8,128)(2,1)} %param.9, bf16[128,2048]{1,0:T(8,128)(2,1)S(1)} %copy-done.1, ...), kind=kOutput, calls=%fused_computation.37 | convolution fusion | flops 1082128384 | bytes 11026944 | tf_op jit(solution)/shard_map/dot_general | solution.py:31
  133.5 0.0 copy-start.2
  133.5 7.1 %fusion = bf16[128,2048]{1,0:T(8,128)(2,1)} fusion(bf16[128,2048]{1,0:T(8,128)(2,1)S(1)} %get-tuple-element.5, bf16[2048,2048]{1,0:T(8,128)(2,1)} %param.9, f32[128]{0:T(128)S(1)} %fusion.11), kind=kOutput, calls=%fused_computation.5 | convolution fusion | flops 1074266112 | bytes 9437696 | tf_op jit(solution)/shard_map/dot_general | solution.py:40
  140.6 0.0 all-gather.5.cloned.1.call-update
  140.6 0.0 all-reduce.3.cloned.1.call-start
  140.7 0.0 copy-done.2
  140.7 5.9 %convolution_convert_fusion = bf16[2048,2048]{1,0:T(8,128)(2,1)} fusion(bf16[128,2048]{1,0:T(8,128)(2,1)S(1)} %get-tuple-element.5, bf16[128,2048]{1,0:T(8,128)(2,1)S(1)} %copy-done.1, bf16[128,2048]{1,0:T(8,128)(2,1)S(1)} %copy-done.2, f32[128]{0:T(128)S(1)} %fusion.11), kind=kOutput, calls=%fused_computation | convolution fusion | flops 1079508992 | bytes 9961984 | tf_op jit(solution)/shard_map/dot_general | solution.py:35
  146.5 0.0 all-reduce.3.cloned.1.call-update
  146.6 0.2 reduce-scatter.5.cloned.1.call-start
  146.8 16.6 %all-gather.5.cloned.1.call-done = bf16[512,2048]{1,0:T(8,128)(2,1)} async-done(((bf16[128,2048]{1,0:T(8,128)(2,1)}), bf16[512,2048]{1,0:T(8,128)(2,1)}) %all-gather.5.cloned.1.call-update) | async-done | bytes 2097168 | tf_op jit(solution)/shard_map/all_gather | solution.py:44
  163.4 10.8 %convolution_convert_fusion.1 = bf16[1024,2048]{1,0:T(8,128)(2,1)} fusion(bf16[512,2048]{1,0:T(8,128)(2,1)} %all-gather.5.cloned.1.call-done, f32[512]{0:T(512)S(1)} %bitcast.70, s32[512]{0:T(512)S(1)} %bitcast.100, f32[512]{0:T(512)S(1)} %bitcast.42, s32[512]{0:T(512)S(1)} %bitcast.102, f32[512]{0:T(512)S(1)} %bitcast.44, s32[512]{0:T(512)S(1)} %bitcast.74, ...), kind=kOutput, calls=%fused_computation.1 | convolution fusion | flops 2174746624 | bytes 6356992 | tf_op jit(solution)/shard_map/dot_general | solution.py:45
  174.2 0.0 reduce-scatter.5.cloned.1.call-update
  174.2 41.2 %psum.15 = f32[2048]{0:T(1024)} all-reduce(f32[2048]{0:T(1024)S(1)} %get-tuple-element.4), channel_id=1, replica_groups=mesh['row'=8,'col'=4] {'row','col'}, use_global_device_ids=true, to_apply=%region_6.7 | all-reduce | flops 2048 | bytes 16384 | tf_op jit(solution)/shard_map/psum | solution.py:39
  215.4 0.0 copy-start
  215.4 134.8 %all-reduce.3.cloned.1.call-done = bf16[2048,2048]{1,0:T(8,128)(2,1)} async-done(((bf16[2048,2048]{1,0:T(8,128)(2,1)}), bf16[2048,2048]{1,0:T(8,128)(2,1)}) %all-reduce.3.cloned.1.call-update) | async-done | bytes 8388624 | tf_op jit(solution)/shard_map/psum | solution.py:38
  350.1 11.7 %convert_element_type.62 = f32[2048,2048]{1,0:T(8,128)} convert(bf16[2048,2048]{1,0:T(8,128)(2,1)} %all-reduce.3.cloned.1.call-done) | non-fusion elementwise | flops 4194304 | bytes 25165824 | tf_op jit(solution)/shard_map/convert_element_type | solution.py:38
  361.8 80.2 %reduce-scatter.5.cloned.1.call-done = bf16[128,2048]{1,0:T(8,128)(2,1)} async-done(((bf16[1024,2048]{1,0:T(8,128)(2,1)}), bf16[128,2048]{1,0:T(8,128)(2,1)}) %reduce-scatter.5.cloned.1.call-update) | async-done | bytes 524304 | tf_op jit(solution)/shard_map/reduce_scatter | solution.py:48
  442.0 0.0 copy-done
  442.0 2.2 multiply_add_fusion
  (2 shorter events, 0.0 us)
Async XLA Ops:
  7.2 79.1 %all-gather.3.cloned.1.call-start = ((), (), s32[]{:S(2)}) async-start(), calls=%async_computation.2 | async-start | bytes 4718592 | tf_op jit(solution)/shard_map/all_gather | solution.py:19
  7.9 119.0 %reduce-scatter.3.cloned.1.call-start = ((), (), s32[]{:S(2)}) async-start(), calls=%async_computation.3 | async-start | bytes 2621440 | tf_op jit(solution)/shard_map/reduce_scatter | solution.py:24
  97.0 0.7 copy-start.6
  97.0 1.9 copy-start.3
  97.0 29.9 %copy-start.1 = (bf16[128,2048]{1,0:T(8,128)(2,1)S(1)}, bf16[128,2048]{1,0:T(8,128)(2,1)}, u32[]{:S(2)}) copy-start(bf16[128,2048]{1,0:T(8,128)(2,1)} %param.6) | copy-start | bytes 1572868
  97.0 29.9 %copy-start.4 = (bf16[128,2048]{1,0:T(8,128)(2,1)S(1)}, bf16[128,2048]{1,0:T(8,128)(2,1)}, u32[]{:S(2)}) copy-start(bf16[128,2048]{1,0:T(8,128)(2,1)} %param.11) | copy-start | bytes 1572868
  97.0 29.9 %copy-start.5 = (f32[2048]{0:T(1024)S(1)}, f32[2048]{0:T(1024)}, u32[]{:S(2)}) copy-start(f32[2048]{0:T(1024)} %param.10) | copy-start | bytes 24580
  97.0 66.3 %all-gather.5.cloned.1.call-start = ((), (), s32[]{:S(2)}) async-start(), calls=%async_computation.4 | async-start | bytes 2621440 | tf_op jit(solution)/shard_map/all_gather | solution.py:44
  133.5 7.2 %copy-start.2 = (bf16[128,2048]{1,0:T(8,128)(2,1)S(1)}, bf16[128,2048]{1,0:T(8,128)(2,1)}, u32[]{:S(2)}) copy-start(bf16[128,2048]{1,0:T(8,128)(2,1)} %reduce-scatter.3.cloned.1.call-done) | copy-start | bytes 1572868
  140.6 209.5 %all-reduce.3.cloned.1.call-start = ((), (), s32[]{:S(2)}) async-start(), calls=%async_computation.6 | async-start | bytes 16777216 | tf_op jit(solution)/shard_map/psum | solution.py:38
  146.6 295.5 %reduce-scatter.5.cloned.1.call-start = ((), (), s32[]{:S(2)}) async-start(), calls=%async_computation.5 | async-start | bytes 4718592 | tf_op jit(solution)/shard_map/reduce_scatter | solution.py:48
  215.4 226.7 %copy-start = (bf16[128,2048]{1,0:T(8,128)(2,1)S(1)}, bf16[128,2048]{1,0:T(8,128)(2,1)}, u32[]{:S(2)}) copy-start(bf16[128,2048]{1,0:T(8,128)(2,1)} %fusion) | copy-start | bytes 1572868
Sparse Core Ops, SparseCore 0:
  10.1 76.0 all-gather.2
  97.2 29.6 reduce-scatter.2
  140.7 22.5 all-gather.4
  170.4 179.6 all-reduce.2
  354.0 87.9 reduce-scatter.4

commit v2 on v1

v2 whole, which is shorter than its diff:
```python
import functools

import jax
import jax.numpy as jnp
from jax import lax
from jax.experimental import pallas as pl
from jax.experimental.pallas import tpu as pltpu
from jax.sharding import PartitionSpec as P

MESH = pl.DeviceIdType.MESH
BF16, F32, I32 = jnp.bfloat16, jnp.float32, jnp.int32
NODE = 128
SPLIT = 4
CORES = 2


class Plan:
    def __init__(self, mesh, feat):
        self.rows, self.cols = mesh.shape["row"], mesh.shape["col"]
        self.nz, self.ny = SPLIT, self.rows // SPLIT
        self.nx = self.cols // CORES
        self.feat = feat
        self.slice = feat // self.nz
        self.columns = self.rows * NODE
        self.block = self.cols * NODE
        self.line = self.nz * self.block

    def place(self):
        row, col = lax.axis_index("row"), lax.axis_index("col")
        return row // self.ny, lax.rem(row, self.ny), col // CORES, lax.rem(col, CORES)

    def device(self, z, y, x, k):
        return (z * self.ny + y, x * CORES + k)


class Sends:
    def __init__(self, sems):
        self.sems, self.started = sems, []

    def __call__(self, src, dst, recv, device):
        copy = pltpu.make_async_remote_copy(
            src_ref=src,
            dst_ref=dst,
            send_sem=self.sems.at[len(self.started)],
            recv_sem=recv,
            device_id=device,
            device_id_type=MESH,
        )
        copy.start()
        self.started.append(copy)

    def finish(self):
        for copy in self.started:
            copy.wait_send()


def arrived(ref, recv, device):
    pltpu.make_async_remote_copy(
        src_ref=ref, dst_ref=ref, send_sem=recv, recv_sem=recv, device_id=device, device_id_type=MESH
    ).wait_recv()


def others(index, count):
    return [lax.rem(index + step, count) for step in range(1, count)]


def at(start, size, align=None):
    return pl.ds(pl.multiple_of(start, align or size), size)


def greet(devices):
    barrier = pltpu.get_barrier_semaphore()
    for device in devices:
        pl.semaphore_signal(barrier, inc=1, device_id=device, device_id_type=MESH)
    pl.semaphore_wait(barrier, len(devices))


def forward_kernel(
    plan, chunks, x_ref, codes_ref, w_hbm, bias_ref, cot_ref,
    act_ref, pg_ref, scaled_ref, agg_ref, adj_ref, bias_sum_ref,
    x_t, gathered, codes, count, degrees, w_ref, half_send, half_recv, x_send, x_recv, own, total, summed, agg_rows,
    w_sem, sems, codes_sem, degree_sem, slice_sem, line_sem, half_sem, x_sem, back_sem,
):
    nz, ny, nx, fs = plan.nz, plan.ny, plan.nx, plan.slice
    z, y, x, k = plan.place()
    send = Sends(sems)
    width = fs // chunks
    zs, ys, xs = others(z, nz), others(y, ny), others(x, nx)
    here = plan.device(z, y, x, k)
    mates = [plan.device(z, y, a, k) for a in xs] + [plan.device(z, y, x, 1 - k)] + [plan.device(z, y, a, 1 - k) for a in xs]
    mate_cols = [a * CORES + k for a in xs] + [x * CORES + 1 - k] + [a * CORES + 1 - k for a in xs]

    w_copy = pltpu.make_async_copy(w_hbm, w_ref, w_sem)
    w_copy.start()

    def turn(step, carry):
        cols = at(step * NODE, NODE)
        x_t[cols, :] = x_ref[:, cols].astype(F32).T.astype(BF16)
        return carry

    lax.fori_loop(0, plan.feat // NODE, turn, 0)
    for c in range(plan.cols):
        part = codes_ref[:, c * NODE : (c + 1) * NODE]
        ones = jnp.sum(jnp.where(part >= 0, 1.0, 0.0), axis=0, keepdims=True)
        count[c] = jnp.broadcast_to(ones, (8, NODE))

    greet([plan.device(a, y, x, k) for a in zs] + [plan.device(z, a, x, k) for a in ys] + mates)

    mine = at((y * nz + z) * NODE, NODE)
    for a in zs:
        send(codes_ref, codes.at[z], codes_sem.at[z], plan.device(a, y, x, k))
    for chunk in range(chunks):
        for a in zs:
            send(
                x_t.at[at(a * fs + chunk * width, width)],
                gathered.at[pl.ds(chunk * width, width), mine],
                slice_sem.at[chunk, z],
                plan.device(a, y, x, k),
            )
        for b in ys:
            send(
                x_t.at[at(z * fs + chunk * width, width)],
                gathered.at[pl.ds(chunk * width, width), mine],
                line_sem.at[chunk, z, y],
                plan.device(z, b, x, k),
            )
    col = x * CORES + k
    for device, c in zip(mates, mate_cols):
        send(count.at[c], degrees.at[col], degree_sem.at[col], device)
    gathered[:, mine] = x_t[at(z * fs, fs), :]
    degrees[col] = count[col]

    groups = (plan.rows + 3) // 4
    strip = 64

    def build(a, source):
        for c in range(plan.cols):
            columns = at((((c % CORES) * nx + c // CORES) * nz + a) * NODE, NODE)
            part = source[:, c * NODE : (c + 1) * NODE]
            low = jnp.where(part >= 0, part % NODE, -1)
            high = jnp.where(part >= 0, part // NODE, -1)
            adds = [
                sum(jnp.where(high == 4 * g + i, 1 << (8 * i), 0) for i in range(4) if 4 * g + i < plan.rows)
                for g in range(groups)
            ]
            for start in range(0, NODE, strip):
                lanes = lax.broadcasted_iota(I32, (strip, NODE), 0) + start
                packed = [jnp.zeros((strip, NODE), I32) for _ in range(groups)]
                for s in range(part.shape[0]):
                    hit = low[s : s + 1, :] == lanes
                    packed = [p + jnp.where(hit, v[s : s + 1, :], 0) for p, v in zip(packed, adds)]
                for r in range(plan.rows):
                    row = ((r % ny) * nz + r // ny) * NODE + start
                    number = (packed[r // 4] >> (8 * (r % 4))) & 255
                    adj_ref[row : row + strip, columns] = number.astype(F32).astype(BF16)

    build(z, codes_ref)
    for a in zs:
        arrived(codes.at[a], codes_sem.at[a], here)
        build(a, codes.at[a])

    def block_of(a, b):
        return at((b * nz + a) * NODE, NODE)

    def pass_on(chunk):
        rows = pl.ds(chunk * width, width)
        for a in zs:
            piece = gathered.at[rows, block_of(a, y)]
            arrived(piece, slice_sem.at[chunk, a], here)
            for b in ys:
                send(piece, piece, line_sem.at[chunk, a, y], plan.device(z, b, x, k))

    tile = 256
    half = plan.line // 2
    third = half // nx

    def product(chunk, columns_from, count_, store):
        rows = pl.ds(chunk * width, width)

        def step(i, carry):
            offset = i * tile
            store(
                at(offset, tile),
                jnp.dot(gathered[rows, :], adj_ref[:, at(columns_from + offset, tile)], preferred_element_type=F32),
            )
            return carry

        lax.fori_loop(0, count_ // tile, step, 0)

    def first(chunk):
        rows = pl.ds(chunk * width, width)
        for a in range(nz):
            for b in ys:
                arrived(gathered.at[rows, block_of(a, b)], line_sem.at[chunk, a, b], here)

        def to_half(cols, value):
            half_send[chunk, :, cols] = value.astype(BF16)

        product(chunk, (1 - k) * half, half, to_half)
        send(half_send.at[chunk], half_recv.at[chunk], half_sem.at[chunk], plan.device(z, y, x, 1 - k))

        def to_own(cols, value):
            own[chunk, :, cols] = value

        product(chunk, k * half, half, to_own)

    def second(chunk):
        arrived(half_recv.at[chunk], half_sem.at[chunk], here)
        for a in xs:
            cols = at(a * third, third)
            x_send[chunk, :, cols] = (own[chunk, :, cols] + half_recv[chunk, :, cols].astype(F32)).astype(BF16)
            send(x_send.at[chunk, :, cols], x_recv.at[chunk, x], x_sem.at[chunk, x], plan.device(z, y, a, k))

    def last(chunk):
        cols = at(x * third, third)
        value = own[chunk, :, cols] + half_recv[chunk, :, cols].astype(F32)
        for a in xs:
            arrived(x_recv.at[chunk, a], x_sem.at[chunk, a], here)
            value = value + x_recv[chunk, a].astype(F32)
        total[chunk] = value.astype(BF16)
        rows = at(z * fs + chunk * width, width)
        for a in zs:
            send(total.at[chunk, :, at(a * NODE, NODE)], summed.at[rows], back_sem.at[chunk, z], plan.device(a, y, x, k))
        summed[rows, :] = total[chunk, :, at(z * NODE, NODE)]

    pass_on(0)
    for chunk in range(chunks):
        first(chunk)
        if chunk + 1 < chunks:
            pass_on(chunk + 1)
        second(chunk)
    for chunk in range(chunks):
        last(chunk)

    for device, c in zip(mates, mate_cols):
        arrived(degrees.at[c], degree_sem.at[c], here)
    degree = degrees[0]
    for c in range(1, plan.cols):
        degree = degree + degrees[c]
    scale = 1.0 / (degree[0:1, :] + 1.0)
    scale_col = jnp.broadcast_to(scale, (NODE, NODE)).T[:, 0:1]
    w_copy.wait()
    for chunk in range(chunks):
        for a in zs:
            rows = at(a * fs + chunk * width, width)
            arrived(summed.at[rows], back_sem.at[chunk, a], here)

    def combine(step, carry):
        rows = at(step * NODE, NODE)
        value = scale * (summed[rows, :].astype(F32) + 2.0 * x_t[rows, :].astype(F32))
        agg_ref[rows, :] = value.astype(BF16)
        agg_rows[:, rows] = value.T.astype(BF16)
        return carry

    lax.fori_loop(0, plan.feat // NODE, combine, 0)

    def layer(step, carry):
        cols = at(step * tile, tile)
        pre = jnp.dot(agg_rows[...], w_ref[:, cols], preferred_element_type=F32) + bias_ref[:, cols]
        square = pre * pre
        slope = 0.7978845608028654
        t = jnp.tanh(slope * pre * (1.0 + 0.044715 * square))
        act_ref[:, cols] = (0.5 * pre * (1.0 + t)).astype(BF16)
        grad = 0.5 * (1.0 + t) + 0.5 * pre * (1.0 - t * t) * (slope * (1.0 + 3.0 * 0.044715 * square))
        low = (cot_ref[:, cols].astype(F32) * grad).astype(BF16)
        pg_ref[:, cols] = low
        wide = low.astype(F32)
        scaled_ref[:, cols] = (scale_col * wide).astype(BF16)
        bias_sum_ref[:, cols] = jnp.sum(wide, axis=0, keepdims=True)
        return carry

    lax.fori_loop(0, plan.feat // tile, layer, 0)
    send.finish()


def forward_part(plan, features, codes, weight, bias, cotangent, chunks=2):
    feat, fs = plan.feat, plan.slice
    width = fs // chunks
    half = plan.line // 2
    third = half // plan.nx
    n_sends = (
        (plan.nz - 1) * (1 + 2 * chunks) + plan.cols - 1 + chunks * plan.nz * (plan.ny - 1) + chunks * plan.nx
    )
    dma = pltpu.SemaphoreType.DMA
    vmem = pl.BlockSpec(memory_space=pltpu.VMEM)
    return pl.pallas_call(
        functools.partial(forward_kernel, plan, chunks),
        name="forward",
        out_shape=(
            jax.ShapeDtypeStruct((NODE, feat), BF16),
            jax.ShapeDtypeStruct((NODE, feat), BF16),
            jax.ShapeDtypeStruct((NODE, feat), BF16),
            jax.ShapeDtypeStruct((feat, NODE), BF16),
            jax.ShapeDtypeStruct((plan.columns, plan.line), BF16),
            jax.ShapeDtypeStruct((1, feat), F32),
        ),
        in_specs=[vmem, vmem, pl.BlockSpec(memory_space=pl.ANY), vmem, vmem],
        out_specs=(vmem,) * 6,
        scratch_shapes=[
            pltpu.VMEM((feat, NODE), BF16),
            pltpu.VMEM((fs, plan.columns), BF16),
            pltpu.VMEM((plan.nz,) + codes.shape, I32),
            pltpu.VMEM((plan.cols, 8, NODE), F32),
            pltpu.VMEM((plan.cols, 8, NODE), F32),
            pltpu.VMEM(weight.shape, BF16),
            pltpu.VMEM((chunks, width, half), BF16),
            pltpu.VMEM((chunks, width, half), BF16),
            pltpu.VMEM((chunks, width, half), BF16),
            pltpu.VMEM((chunks, plan.nx, width, third), BF16),
            pltpu.VMEM((chunks, width, half), F32),
            pltpu.VMEM((chunks, width, third), BF16),
            pltpu.VMEM((feat, NODE), BF16),
            pltpu.VMEM((NODE, feat), BF16),
            dma(()),
            dma((n_sends,)),
            dma((plan.nz,)),
            dma((plan.cols,)),
            dma((chunks, plan.nz)),
            dma((chunks, plan.nz, plan.ny)),
            dma((chunks,)),
            dma((chunks, plan.nx)),
            dma((chunks, plan.nz)),
        ],
        compiler_params=pltpu.CompilerParams(
            collective_id=0, has_side_effects=True, vmem_limit_bytes=63 << 20
        ),
    )(features, codes, weight, bias, cotangent)


def backward_kernel(
    plan, wide_chunks, back_chunks, pg_ref, scaled_ref, agg_ref, adj_ref, bias_ref, w_hbm,
    fg_ref, low_hbm, bias_grad_ref,
    w_ref, agg_all, pg_all, grads, half_send, half_recv, own_tile, sum_send, sum_recv, final,
    y_send, y_recv, own_target, back, returned, bias_k, bias_x, bias_y, bias_z, bias_sums,
    local_sem, sems, agg_x_sem, agg_y_sem, pg_y_sem, pg_x_sem, slice_sem, grads_x_sem, grads_k_sem,
    half_sem, sum_sem, gather_sem, y_sem, back_sem, bias_k_sem, bias_x_sem, bias_y_sem, bias_z_sem,
):
    nz, ny, nx, fs, feat = plan.nz, plan.ny, plan.nx, plan.slice, plan.feat
    z, y, x, k = plan.place()
    send = Sends(sems)
    zs, ys, xs = others(z, nz), others(y, ny), others(x, nx)
    here, twin = plan.device(z, y, x, k), plan.device(z, y, x, 1 - k)
    fa, fp = feat // nx, feat // ny
    fh, fw = fa // CORES, fp // wide_chunks
    fz = fh // nz
    group = nz * NODE
    wb = fs // back_chunks

    w_copy = pltpu.make_async_copy(w_hbm, w_ref, local_sem.at[wide_chunks])
    w_copy.start()
    greet(
        [plan.device(a, y, x, k) for a in zs]
        + [plan.device(z, b, x, k) for b in ys]
        + [plan.device(z, y, a, k) for a in xs]
        + [twin]
    )

    def nodes(b, a):
        return at((b * nx + a) * NODE, NODE)

    for a in xs:
        send(agg_ref.at[at(a * fa, fa)], agg_all.at[:, nodes(y, x)], agg_x_sem.at[x], plan.device(z, y, a, k))
    for b in ys:
        send(pg_ref.at[:, at(b * fp, fp)], pg_all.at[nodes(y, x)], pg_y_sem.at[y], plan.device(z, b, x, k))
    for chunk in range(back_chunks):
        for a in zs:
            send(
                scaled_ref.at[:, at(a * fs + chunk * wb, wb)],
                grads.at[at(((k * nx + x) * nz + z) * NODE, NODE), pl.ds(chunk * wb, wb)],
                slice_sem.at[chunk, z],
                plan.device(a, y, x, k),
            )
    for b in ys:
        send(agg_ref.at[at(x * fa, fa)], agg_all.at[:, nodes(y, x)], agg_y_sem.at[y, x], plan.device(z, b, x, k))
    for a in xs:
        send(pg_ref.at[:, at(y * fp, fp)], pg_all.at[nodes(y, x)], pg_x_sem.at[y, x], plan.device(z, y, a, k))
    send(bias_ref, bias_k, bias_k_sem, twin)
    agg_all[:, nodes(y, x)] = agg_ref[at(x * fa, fa), :]
    pg_all[nodes(y, x), :] = pg_ref[:, at(y * fp, fp)]
    grads[at(((k * nx + x) * nz + z) * NODE, NODE), :] = scaled_ref[:, at(z * fs, fs)]

    for a in xs:
        ref = agg_all.at[:, nodes(y, a)]
        arrived(ref, agg_x_sem.at[a], here)
        for b in ys:
            send(ref, ref, agg_y_sem.at[y, a], plan.device(z, b, x, k))
    for b in ys:
        ref = pg_all.at[nodes(b, x)]
        arrived(ref, pg_y_sem.at[b], here)
        for a in xs:
            send(ref, ref, pg_x_sem.at[b, x], plan.device(z, y, a, k))

    arrived(bias_k, bias_k_sem, here)
    bias_sums[0] = bias_ref[...] + bias_k[...]
    for a in xs:
        send(bias_sums.at[0], bias_x.at[x], bias_x_sem.at[x], plan.device(z, y, a, k))
    bias_x[x] = bias_sums[0]

    def line_rows(c, a):
        return at((c * nx + a) * group, group)

    for chunk in range(back_chunks):
        cols = pl.ds(chunk * wb, wb)
        for a in zs:
            arrived(grads.at[at(((k * nx + x) * nz + a) * NODE, NODE), cols], slice_sem.at[chunk, a], here)
        ref = grads.at[line_rows(k, x), cols]
        for a in xs:
            send(ref, ref, grads_x_sem.at[chunk, x], plan.device(z, y, a, k))
        send(ref, ref, grads_k_sem.at[chunk, x], twin)

    for b in ys:
        for a in range(nx):
            arrived(agg_all.at[:, nodes(b, a)], agg_y_sem.at[b, a], here)
    for a in xs:
        for b in range(ny):
            arrived(pg_all.at[nodes(b, a)], pg_x_sem.at[b, a], here)

    tile = min(256, fh)

    def product(rows_from, chunk, store):
        def step(i, carry):
            rows = agg_all[at(rows_from + i * tile, tile), :]
            store(
                at(i * tile, tile),
                jnp.dot(rows, pg_all[:, chunk * fw : (chunk + 1) * fw], preferred_element_type=F32),
            )
            return carry

        lax.fori_loop(0, fh // tile, step, 0)

    for chunk in range(wide_chunks):
        def to_half(rows, value):
            half_send[chunk, rows, :] = value.astype(BF16)

        product((1 - k) * fh, chunk, to_half)
        send(half_send.at[chunk], half_recv.at[chunk], half_sem.at[chunk], twin)
    for chunk in range(wide_chunks):
        def to_own(rows, value):
            own_tile[chunk, rows, :] = value

        product(k * fh, chunk, to_own)
    for chunk in range(wide_chunks):
        arrived(half_recv.at[chunk], half_sem.at[chunk], here)
        for a in zs:
            rows = at(a * fz, fz)
            sum_send[chunk, rows, :] = (own_tile[chunk, rows, :] + half_recv[chunk, rows, :].astype(F32)).astype(BF16)
            send(sum_send.at[chunk, rows], sum_recv.at[chunk, z], sum_sem.at[chunk, z], plan.device(a, y, x, k))

    def bias_stage(ref, sem, count, peers, stage, onward):
        for a in peers:
            arrived(ref.at[a], sem.at[a], here)
        value = ref[0]
        for a in range(1, count):
            value = value + ref[a]
        if onward is None:
            bias_grad_ref[...] = value
        else:
            next_ref, next_sem, index, devices = onward
            bias_sums[stage] = value
            next_ref[index] = value
            for device in devices:
                send(bias_sums.at[stage], next_ref.at[index], next_sem.at[index], device)

    bias_stage(bias_x, bias_x_sem, nx, xs, 1, (bias_y, bias_y_sem, y, [plan.device(z, b, x, k) for b in ys]))

    for chunk in range(back_chunks):
        cols = pl.ds(chunk * wb, wb)
        for a in xs:
            ref = grads.at[line_rows(k, a), cols]
            arrived(ref, grads_x_sem.at[chunk, a], here)
            send(ref, ref, grads_k_sem.at[chunk, a], twin)
    for chunk in range(back_chunks):
        cols = pl.ds(chunk * wb, wb)
        for a in range(nx):
            arrived(grads.at[line_rows(1 - k, a), cols], grads_k_sem.at[chunk, a], here)

        def target(b, store):
            def step(i, carry):
                rows = adj_ref[at(b * group + i * tile, tile), :]
                store(at(i * tile, tile), jnp.dot(rows, grads[:, cols], preferred_element_type=F32))
                return carry

            lax.fori_loop(0, group // tile, step, 0)

        for i, b in enumerate(ys):
            def to_y(rows, value):
                y_send[chunk, i, rows, :] = value.astype(BF16)

            target(b, to_y)
            send(y_send.at[chunk, i], y_recv.at[chunk, ny - 2 - i], y_sem.at[chunk, ny - 2 - i], plan.device(z, b, x, k))

        def to_target(rows, value):
            own_target[chunk, rows, :] = value

        target(y, to_target)
    bias_stage(bias_y, bias_y_sem, ny, ys, 2, (bias_z, bias_z_sem, z, [plan.device(a, y, x, k) for a in zs]))

    def piece(chunk, a_z, a_y, a_x, a_k):
        return low_hbm.at[at(a_x * fa + a_k * fh + a_z * fz, fz), at(a_y * fp + chunk * fw, fw)]

    def gather(source, chunk, origin, devices):
        for device in devices:
            send(source, piece(chunk, *origin), gather_sem.at[(chunk,) + origin], device)

    def await_piece(chunk, *origin):
        arrived(piece(chunk, *origin), gather_sem.at[(chunk,) + origin], here)

    to_z = [plan.device(a, y, x, k) for a in zs]
    to_y_ = [plan.device(z, b, x, k) for b in ys]
    to_x = [plan.device(z, y, a, k) for a in xs]
    locals_ = []
    for chunk in range(wide_chunks):
        rows = at(z * fz, fz)
        value = own_tile[chunk, rows, :] + half_recv[chunk, rows, :].astype(F32)
        for a in zs:
            arrived(sum_recv.at[chunk, a], sum_sem.at[chunk, a], here)
            value = value + sum_recv[chunk, a].astype(F32)
        final[chunk] = value.astype(BF16)
        gather(final.at[chunk], chunk, (z, y, x, k), to_z + to_x + to_y_ + [twin])
        copy = pltpu.make_async_copy(final.at[chunk], piece(chunk, z, y, x, k), local_sem.at[chunk])
        copy.start()
        locals_.append(copy)

    for chunk in range(back_chunks):
        value = own_target[chunk]
        for i in range(ny - 1):
            arrived(y_recv.at[chunk, i], y_sem.at[chunk, i], here)
            value = value + y_recv[chunk, i].astype(F32)
        back[chunk] = value.astype(BF16)
        cols = at(z * fs + chunk * wb, wb)
        for a in zs:
            send(back.at[chunk, at(a * NODE, NODE)], returned.at[:, cols], back_sem.at[chunk, z], plan.device(a, y, x, k))
        returned[:, cols] = back[chunk, at(z * NODE, NODE), :]

    order = [z] + zs
    for chunk in range(wide_chunks):
        for a in zs:
            await_piece(chunk, a, y, x, k)
            gather(piece(chunk, a, y, x, k), chunk, (a, y, x, k), to_x + to_y_ + [twin])
        for step, a in enumerate(order):
            for a_x in xs:
                await_piece(chunk, a, y, a_x, k)
                gather(piece(chunk, a, y, a_x, k), chunk, (a, y, a_x, k), (to_y_ if step % 2 == 0 else []) + [twin])
            for a_y in ys:
                await_piece(chunk, a, a_y, x, k)
                gather(piece(chunk, a, a_y, x, k), chunk, (a, a_y, x, k), (to_x if step % 2 == 1 else []) + [twin])

    w_copy.wait()
    for chunk in range(back_chunks):
        for a in zs:
            cols = at(a * fs + chunk * wb, wb)
            arrived(returned.at[:, cols], back_sem.at[chunk, a], here)
    scaled_ref_value = (returned[...].astype(F32) + 2.0 * scaled_ref[...].astype(F32)).astype(BF16)
    returned[...] = scaled_ref_value

    def through(step, carry):
        rows = at(step * 256, 256)
        fg_ref[:, rows] = lax.dot_general(
            returned[...], w_ref[rows, :], (((1,), (1,)), ((), ())), preferred_element_type=F32
        )
        return carry

    lax.fori_loop(0, feat // 256, through, 0)
    bias_stage(bias_z, bias_z_sem, nz, zs, 3, None)

    for chunk in range(wide_chunks):
        for a in order:
            for a_x in xs:
                for a_y in ys:
                    await_piece(chunk, a, a_y, a_x, k)
                    gather(piece(chunk, a, a_y, a_x, k), chunk, (a, a_y, a_x, k), [twin])
    for chunk in range(wide_chunks):
        for a in range(nz):
            for a_y in range(ny):
                for a_x in range(nx):
                    await_piece(chunk, a, a_y, a_x, 1 - k)
    for copy in locals_:
        copy.wait()
    send.finish()


def backward_part(plan, preact_grad, scaled, agg_t, adjacency, bias_term, weight, wide_chunks=2, back_chunks=2):
    nz, ny, nx, fs, feat = plan.nz, plan.ny, plan.nx, plan.slice, plan.feat
    fa, fp = feat // nx, feat // ny
    fh, fw = fa // CORES, fp // wide_chunks
    fz = fh // nz
    group, wb, depth = nz * NODE, fs // back_chunks, ny * nx * NODE
    dz, dy, dx = nz - 1, ny - 1, nx - 1
    n_sends = (
        dx + dy + back_chunks * dz + dy + dx + 1 + 2 * dx * dy + dx + back_chunks * (dx + 1)
        + wide_chunks * (1 + dz) + dy + back_chunks * dx + back_chunks * dy + dz
        + wide_chunks * (dz + dx + dy + 1) + back_chunks * dz
        + wide_chunks * (dz * (dx + dy + 1) + nz * (dx + dy) + 2 * nz * dx * dy + nz * dx * dy)
    )
    dma = pltpu.SemaphoreType.DMA
    vmem = pl.BlockSpec(memory_space=pltpu.VMEM)
    hbm = pl.BlockSpec(memory_space=pl.ANY)
    return pl.pallas_call(
        functools.partial(backward_kernel, plan, wide_chunks, back_chunks),
        name="backward",
        out_shape=(
            jax.ShapeDtypeStruct((NODE, feat), F32),
            jax.ShapeDtypeStruct((feat, feat), BF16),
            jax.ShapeDtypeStruct((1, feat), F32),
        ),
        in_specs=[vmem] * 5 + [hbm],
        out_specs=(vmem, hbm, vmem),
        scratch_shapes=[
            pltpu.VMEM(weight.shape, BF16),
            pltpu.VMEM((fa, depth), BF16),
            pltpu.VMEM((depth, fp), BF16),
            pltpu.VMEM((plan.line, fs), BF16),
            pltpu.VMEM((wide_chunks, fh, fw), BF16),
            pltpu.VMEM((wide_chunks, fh, fw), BF16),
            pltpu.VMEM((wide_chunks, fh, fw), F32),
            pltpu.VMEM((wide_chunks, fh, fw), BF16),
            pltpu.VMEM((wide_chunks, nz, fz, fw), BF16),
            pltpu.VMEM((wide_chunks, fz, fw), BF16),
            pltpu.VMEM((back_chunks, ny - 1, group, wb), BF16),
            pltpu.VMEM((back_chunks, ny - 1, group, wb), BF16),
            pltpu.VMEM((back_chunks, group, wb), F32),
            pltpu.VMEM((back_chunks, group, wb), BF16),
            pltpu.VMEM((NODE, feat), BF16),
            pltpu.VMEM((1, feat), F32),
            pltpu.VMEM((nx, 1, feat), F32),
            pltpu.VMEM((ny, 1, feat), F32),
            pltpu.VMEM((nz, 1, feat), F32),
            pltpu.VMEM((3, 1, feat), F32),
            dma((wide_chunks + 1,)),
            dma((n_sends,)),
            dma((nx,)),
            dma((ny, nx)),
            dma((ny,)),
            dma((ny, nx)),
            dma((back_chunks, nz)),
            dma((back_chunks, nx)),
            dma((back_chunks, nx)),
            dma((wide_chunks,)),
            dma((wide_chunks, nz)),
            dma((wide_chunks, nz, ny, nx, CORES)),
            dma((back_chunks, ny - 1)),
            dma((back_chunks, nz)),
            dma(()),
            dma((nx,)),
            dma((ny,)),
            dma((nz,)),
        ],
        compiler_params=pltpu.CompilerParams(
            collective_id=1, has_side_effects=True, vmem_limit_bytes=127 << 19
        ),
    )(preact_grad, scaled, agg_t, adjacency, bias_term, weight)


def on_device(plan, features, neighbours, edge_mask, weight, bias, cotangent):
    codes = jnp.where(edge_mask > 0, neighbours, -1).T
    activations, preact_grad, scaled, agg_t, adjacency, bias_term = forward_part(
        plan, features, codes, weight, bias.reshape(1, -1), cotangent
    )
    feature_grad, weight_low, bias_grad = backward_part(
        plan, preact_grad, scaled, agg_t, adjacency, bias_term, weight
    )
    return activations, feature_grad, weight_low.astype(F32), bias_grad.reshape(-1)


def solution(mesh):
    placed = (
        P(("row", "col"), None),
        P("row", "col"),
        P("row", "col"),
        P(),
        P(),
        P(("row", "col"), None),
    )

    def run(*args):
        plan = Plan(mesh, args[0].shape[1])
        return jax.shard_map(
            functools.partial(on_device, plan),
            mesh=mesh,
            in_specs=placed,
            out_specs=(P(("row", "col"), None), P(("row", "col"), None), P(), P()),
            check_vma=False,
        )(*args)

    return run
```

time: 451 us -> 182 us (0.40)
  the two profiles are of different devices: /device:TPU:0 before, /device:TPU:9 now
where the time goes in v2:
time: 182 us
  Pallas kernels  165 us (91%)
  other arithmetic  13.2 us (7%)
  local copies, waits for them, and re-layouts  2.38 us (1%)
    pallas_call x1, Pallas kernels, backward_part(): pl.pallas_call(functools.partial(backward_kernel, plan, wide_chunks, back...  108 us
    pallas_call x1, Pallas kernels, forward_part(): pl.pallas_call(functools.partial(forward_kernel, plan, chunks), name='for...  56.9 us
    convert_element_type x1, other arithmetic, on_device(): weight_low.astype(F32)  11.8 us

profile of v2, /device:TPU:9, one launch (start us, length us, event | category | flops | bytes accessed | tf_op | source)
XLA Modules:
  0.0 181.5 jit_solution(9449636373298060518)
XLA Ops:
  0.6 1.4 select_bitcast_fusion.codes_ref
  2.0 56.9 %forward.1 = (bf16[128,2048]{1,0:T(8,128)(2,1)}, bf16[128,2048]{1,0:T(8,128)(2,1)}, bf16[128,2048]{1,0:T(8,128)(2,1)}, bf16[2048,128]{1,0:T(8,128)(2,1)}, bf16[1024,2048]{1,0:T(8,128)(2,1)}, /*index=5*/f32[1,2048]{1,0:T(1,128)}) custom-call(bf16[128,2048]{1,0:T(8,128)(2,1)} %x_ref.1, s32[16,512]{1,0:T(8,128)} %select_bitcast_fusion.codes_ref, ...), custom_call_target="tpu_custom_call" | custom-call | tf_op jit(solution)/shard_map/forward/pallas_call | solution.py:286
  58.9 108.4 %backward.1 = (f32[128,2048]{1,0:T(8,128)}, bf16[2048,2048]{1,0:T(8,128)(2,1)}, f32[1,2048]{1,0:T(1,128)}) custom-call(bf16[128,2048]{1,0:T(8,128)(2,1)} %get-tuple-element.14.pg_ref, bf16[128,2048]{1,0:T(8,128)(2,1)} %get-tuple-element.15.scaled_ref, bf16[2048,128]{1,0:T(8,128)(2,1)} %get-tuple-element.16.agg_ref, ...), custom_call_target="tpu_custom_call" | custom-call | tf_op jit(solution)/shard_map/backward/pallas_call | solution.py:598
  167.3 0.0 copy-start.1
  167.3 0.0 copy-start
  167.4 0.0 copy-start.2
  167.4 11.8 %convert_element_type.3 = f32[2048,2048]{1,0:T(8,128)} convert(bf16[2048,2048]{1,0:T(8,128)(2,1)} %get-tuple-element.20) | non-fusion elementwise | flops 4194304 | bytes 25165824 | tf_op jit(solution)/shard_map/convert_element_type | solution.py:662
  179.2 0.0 copy-done.1
  179.2 0.8 copy.13
  179.9 0.0 copy-done
  179.9 1.0 copy.14
  180.9 0.0 copy-done.2
  180.9 0.6 copy.15
Async XLA Ops:
  167.3 11.8 %copy-start.1 = (bf16[128,2048]{1,0:T(8,128)(2,1)S(1)}, bf16[128,2048]{1,0:T(8,128)(2,1)}, u32[]{:S(2)}) copy-start(bf16[128,2048]{1,0:T(8,128)(2,1)} %get-tuple-element.26) | copy-start | bytes 1572868
  167.3 12.6 %copy-start = (f32[128,2048]{1,0:T(8,128)S(1)}, f32[128,2048]{1,0:T(8,128)}, u32[]{:S(2)}) copy-start(f32[128,2048]{1,0:T(8,128)} %get-tuple-element.27) | copy-start | bytes 3145732
  167.4 13.6 %copy-start.2 = (f32[1,2048]{1,0:T(1,128)S(1)}, f32[1,2048]{1,0:T(1,128)}, u32[]{:S(2)}) copy-start(f32[1,2048]{1,0:T(1,128)} %get-tuple-element.21) | copy-start | bytes 24580

commit v3 on v1

v3 whole, which is shorter than its diff:
```python
import functools

import jax
import jax.numpy as jnp
from jax import lax
from jax.experimental import pallas as pl
from jax.experimental.pallas import tpu as pltpu
from jax.sharding import PartitionSpec as P

MESH = pl.DeviceIdType.MESH
BF16, F32, I32 = jnp.bfloat16, jnp.float32, jnp.int32
DMA = pltpu.SemaphoreType.DMA
NODE = 128
SPLIT = 4
CORES = 2
CHUNKS = 4
WIDE = 2
BACK = 2


class Plan:
    def __init__(self, mesh, feat, slots):
        rows, cols = mesh.shape["row"], mesh.shape["col"]
        self.rows, self.cols, self.feat, self.slots = rows, cols, feat, slots
        self.nz, self.ny, self.nx = SPLIT, rows // SPLIT, cols // CORES
        self.slice = feat // self.nz
        self.width = self.slice // CHUNKS
        self.columns = rows * NODE
        self.block = cols * NODE
        self.line = self.nz * self.block
        self.half = self.line // CORES
        self.third = self.half // self.nx
        self.fa, self.fp = feat // self.nx, feat // self.ny
        self.fh, self.fw = self.fa // CORES, self.fp // WIDE
        self.fz = self.fh // self.nz
        self.group = self.nz * NODE
        self.wb = self.slice // BACK
        self.depth = self.ny * self.nx * NODE
        self.merged = self.columns * self.line <= 1 << 22

    def place(self):
        row, col = lax.axis_index("row"), lax.axis_index("col")
        return row // self.ny, lax.rem(row, self.ny), col // CORES, lax.rem(col, CORES)

    def device(self, z, y, x, k):
        return (z * self.ny + y, x * CORES + k)


class Refs:
    def __init__(self, names, refs):
        self.__dict__.update(zip(names, refs, strict=True))


def guarded(when, act):
    if when is None:
        act()
    else:
        pl.when(when)(act)


class Sends:
    def __init__(self, sems):
        self.sems, self.started = sems, []

    def __call__(self, src, dst, recv, device, when=None):
        copy = pltpu.make_async_remote_copy(
            src_ref=src,
            dst_ref=dst,
            send_sem=self.sems.at[len(self.started)],
            recv_sem=recv,
            device_id=device,
            device_id_type=MESH,
        )
        guarded(when, copy.start)
        self.started.append((copy, when))

    def finish(self):
        for copy, when in self.started:
            guarded(when, copy.wait_send)


def others(index, count):
    return [lax.rem(index + step, count) for step in range(1, count)]


def at(start, size):
    return pl.ds(pl.multiple_of(start, size), size)


def loop(count, step):
    if count <= 4:
        for i in range(count):
            step(i)
    else:

        def body(i, carry):
            step(i)
            return carry

        lax.fori_loop(0, count, body, 0)


def greet(devices):
    barrier = pltpu.get_barrier_semaphore()
    for device in devices:
        pl.semaphore_signal(barrier, inc=1, device_id=device, device_id_type=MESH)
    pl.semaphore_wait(barrier, len(devices))


class Step:
    def __init__(self, plan, refs):
        self.plan, self.r = plan, refs
        self.z, self.y, self.x, self.k = z, y, x, k = plan.place()
        self.zs, self.ys, self.xs = others(z, plan.nz), others(y, plan.ny), others(x, plan.nx)
        self.here, self.twin = plan.device(z, y, x, k), plan.device(z, y, x, 1 - k)
        self.to_z = [plan.device(a, y, x, k) for a in self.zs]
        self.to_y = [plan.device(z, b, x, k) for b in self.ys]
        self.to_x = [plan.device(z, y, a, k) for a in self.xs]
        self.to_far = [plan.device(z, y, a, 1 - k) for a in self.xs]
        self.send = Sends(refs.sems)

    def arrived(self, ref, sem):
        pltpu.make_async_remote_copy(
            src_ref=ref, dst_ref=ref, send_sem=sem, recv_sem=sem, device_id=self.here, device_id_type=MESH
        ).wait_recv()

    def weight_copies(self):
        plan, r = self.plan, self.r
        copies = []
        for chunk in range(CHUNKS):
            for a in range(plan.nz):
                i = chunk * plan.nz + a
                copies.append(
                    pltpu.make_async_copy(
                        r.w_hbm.at[pl.ds(a * plan.slice + chunk * plan.width, plan.width)],
                        r.w.at[pl.ds(i * plan.width, plan.width)],
                        r.w_sem.at[i],
                    )
                )
        return copies


def forward_half(s, w_copies, agg_ready, pg_ready):
    plan, r, send = s.plan, s.r, s.send
    nz, ny, nx, fs, width = plan.nz, plan.ny, plan.nx, plan.slice, plan.width
    half, third = plan.half, plan.third
    z, y, x, k = s.z, s.y, s.x, s.k

    mates = s.to_x + [s.twin] + s.to_far
    mate_cols = [a * CORES + k for a in s.xs] + [x * CORES + 1 - k] + [a * CORES + 1 - k for a in s.xs]
    col = x * CORES + k
    mine = at((y * nz + z) * NODE, NODE)

    for device in s.to_z:
        send(r.codes, r.line_codes.at[z], r.codes_sem.at[z], device)
    for chunk in range(CHUNKS):
        rows = pl.ds(chunk * width, width)
        for a, device in zip(s.zs, s.to_z):
            send(r.x_t.at[at(a * fs + chunk * width, width)], r.gathered.at[rows, mine], r.slice_sem.at[chunk, z], device)
        for device in s.to_y:
            send(r.x_t.at[at(z * fs + chunk * width, width)], r.gathered.at[rows, mine], r.line_sem.at[chunk, z, y], device)
    for device, c in zip(mates, mate_cols):
        send(r.count.at[c], r.degrees.at[col], r.degree_sem.at[col], device)
    r.gathered[:, mine] = r.x_t[at(z * fs, fs), :]
    r.degrees[col] = r.count[col]

    groups = (plan.rows + 3) // 4
    strip = 32

    def build(a, source):
        for c in range(plan.cols):
            columns = at((((c % CORES) * nx + c // CORES) * nz + a) * NODE, NODE)
            part = source[:, c * NODE : (c + 1) * NODE]
            low = jnp.where(part >= 0, part % NODE, -1)
            high = jnp.where(part >= 0, part // NODE, -1)
            adds = [
                sum(jnp.where(high == 4 * g + i, 1 << (8 * i), 0) for i in range(4) if 4 * g + i < plan.rows)
                for g in range(groups)
            ]
            for start in range(0, NODE, strip):
                lanes = lax.broadcasted_iota(I32, (strip, NODE), 0) + start
                packed = [jnp.zeros((strip, NODE), I32) for _ in range(groups)]
                for slot in range(plan.slots):
                    hit = low[slot : slot + 1, :] == lanes
                    packed = [p + jnp.where(hit, v[slot : slot + 1, :], 0) for p, v in zip(packed, adds)]
                for row in range(plan.rows):
                    start_row = ((row % ny) * nz + row // ny) * NODE + start
                    number = (packed[row // 4] >> (8 * (row % 4))) & 255
                    r.adj[start_row : start_row + strip, columns] = number.astype(F32).astype(BF16)

    def build_from(a):
        s.arrived(r.line_codes.at[a], r.codes_sem.at[a])
        build(a, r.line_codes.at[a])

    def block_of(a, b):
        return at((b * nz + a) * NODE, NODE)

    def pass_on(chunk):
        rows = pl.ds(chunk * width, width)
        for a in s.zs:
            piece = r.gathered.at[rows, block_of(a, y)]
            s.arrived(piece, r.slice_sem.at[chunk, a])
            for device in s.to_y:
                send(piece, piece, r.line_sem.at[chunk, a, y], device)

    tile = 256

    def product(chunk, columns_from, store):
        rows = pl.ds(chunk * width, width)

        def step(i):
            columns = r.adj[:, at(columns_from + i * tile, tile)]
            store(at(i * tile, tile), jnp.dot(r.gathered[rows, :], columns, preferred_element_type=F32))

        loop(half // tile, step)

    def first(chunk):
        rows = pl.ds(chunk * width, width)
        for a in range(nz):
            for b in s.ys:
                s.arrived(r.gathered.at[rows, block_of(a, b)], r.line_sem.at[chunk, a, b])

        def to_half(cols, value):
            r.half_send[chunk, :, cols] = value.astype(BF16)

        product(chunk, (1 - k) * half, to_half)
        send(r.half_send.at[chunk], r.half_recv.at[chunk], r.half_sem.at[chunk], s.twin)

        def to_own(cols, value):
            r.own[chunk, :, cols] = value

        product(chunk, k * half, to_own)

    def second(chunk):
        s.arrived(r.half_recv.at[chunk], r.half_sem.at[chunk])
        for a, device in zip(s.xs, s.to_x):
            cols = at(a * third, third)
            r.x_send[chunk, :, cols] = (r.own[chunk, :, cols] + r.half_recv[chunk, :, cols].astype(F32)).astype(BF16)
            send(r.x_send.at[chunk, :, cols], r.x_recv.at[chunk, x], r.x_sem.at[chunk, x], device)

    def last(chunk):
        cols = at(x * third, third)
        value = r.own[chunk, :, cols] + r.half_recv[chunk, :, cols].astype(F32)
        for a in s.xs:
            s.arrived(r.x_recv.at[chunk, a], r.x_sem.at[chunk, a])
            value = value + r.x_recv[chunk, a].astype(F32)
        r.total[chunk] = value.astype(BF16)
        rows = at(z * fs + chunk * width, width)
        for a, device in zip(s.zs, s.to_z):
            send(r.total.at[chunk, :, at(a * NODE, NODE)], r.summed.at[rows], r.back_sem.at[chunk, z], device)
        r.summed[rows, :] = r.total[chunk, :, at(z * NODE, NODE)]

    build(z, r.codes)
    build_from(s.zs[0])
    build_from(s.zs[1])
    pass_on(0)
    build_from(s.zs[2])
    pass_on(1)
    pass_on(2)
    first(0)
    pass_on(3)
    second(0)
    first(1)
    first(2)
    second(1)
    last(0)
    first(3)
    second(2)
    second(3)
    last(1)

    for device, c in zip(mates, mate_cols):
        s.arrived(r.degrees.at[c], r.degree_sem.at[c])
    degree = r.degrees[0]
    for c in range(1, plan.cols):
        degree = degree + r.degrees[c]
    scale = 1.0 / (degree[0:1, :] + 1.0)
    scale_col = jnp.broadcast_to(scale, (NODE, NODE)).T[:, 0:1]

    def combine(chunk):
        for a in s.zs:
            s.arrived(r.summed.at[at(a * fs + chunk * width, width)], r.back_sem.at[chunk, a])
        for a in range(nz):
            rows = pl.ds(a * fs + chunk * width, width)
            value = scale * (r.summed[rows, :].astype(F32) + 2.0 * r.x_t[rows, :].astype(F32))
            r.agg[rows, :] = value.astype(BF16)
            r.agg_rows[:, (chunk * nz + a) * width : (chunk * nz + a + 1) * width] = value.T.astype(BF16)

    def part_of(chunk, cols):
        rows = pl.ds(chunk * fs, fs)
        return jnp.dot(r.agg_rows[:, rows], r.w[rows, cols], preferred_element_type=F32)

    def add_chunk(chunk):
        for i in range(chunk * nz, (chunk + 1) * nz):
            w_copies[i].wait()

        def step(i):
            cols = at(i * 512, 512)
            if chunk == 0:
                r.preact[:, cols] = part_of(chunk, cols)
            else:
                r.preact[:, cols] += part_of(chunk, cols)

        loop(plan.feat // 512, step)

    combine(0)
    last(2)
    add_chunk(0)
    combine(1)
    last(3)
    add_chunk(1)
    combine(2)
    add_chunk(2)
    combine(3)
    agg_ready()
    for i in range(3 * nz, 4 * nz):
        w_copies[i].wait()
    r.cot_copy.wait()

    def layer(cols):
        pre = r.preact[:, cols] + part_of(3, cols) + r.bias[:, cols]
        square = pre * pre
        slope = 0.7978845608028654
        t = jnp.tanh(slope * pre * (1.0 + 0.044715 * square))
        r.act[:, cols] = (0.5 * pre * (1.0 + t)).astype(BF16)
        grad = 0.5 * (1.0 + t) + 0.5 * pre * (1.0 - t * t) * (slope * (1.0 + 3.0 * 0.044715 * square))
        low = (r.cot[:, cols].astype(F32) * grad).astype(BF16)
        r.pg[:, cols] = low
        wide = low.astype(F32)
        r.scaled[:, cols] = (scale_col * wide).astype(BF16)
        r.bias_sum[:, cols] = jnp.sum(wide, axis=0, keepdims=True)

    for part in range(WIDE):
        loop(ny, lambda b: layer(at(b * plan.fp + part * plan.fw, plan.fw)))
        pg_ready(part)


class BackwardHalf:
    def __init__(self, s, w_copies):
        self.s, self.w_copies = s, w_copies
        plan = s.plan
        self.pair = s.z + 1 - 2 * lax.rem(s.z, 2)
        self.other = plan.nz - 1 - s.z
        self.middle = lax.rem(s.z, 3) > 0
        self.end = lax.rem(s.z, 3) == 0
        self.tile = min(256, plan.fh)
        self.copies = []

    def nodes(self, b, a):
        return at((b * self.s.plan.nx + a) * NODE, NODE)

    def line_rows(self, c, a):
        return at((c * self.s.plan.nx + a) * self.s.plan.group, self.s.plan.group)

    def wide_cols(self, b, part):
        return at(b * self.s.plan.fp + part * self.s.plan.fw, self.s.plan.fw)

    def agg_ready(self):
        s, r, fa = self.s, self.s.r, self.s.plan.fa
        mine = self.nodes(s.y, s.x)
        for a, device in zip(s.xs, s.to_x):
            s.send(r.agg.at[at(a * fa, fa)], r.agg_all.at[:, mine], r.agg_x_sem.at[s.x], device)
        for device in s.to_y:
            s.send(r.agg.at[at(s.x * fa, fa)], r.agg_all.at[:, mine], r.agg_y_sem.at[s.y, s.x], device)
        r.agg_all[:, mine] = r.agg[at(s.x * fa, fa), :]

    def pg_ready(self, part):
        s, r, fw = self.s, self.s.r, self.s.plan.fw
        mine, cols = self.nodes(s.y, s.x), pl.ds(part * fw, fw)
        for b, device in zip(s.ys, s.to_y):
            s.send(r.pg.at[:, self.wide_cols(b, part)], r.pg_all.at[mine, cols], r.pg_y_sem.at[part, s.y], device)
        for device in s.to_x:
            s.send(
                r.pg.at[:, self.wide_cols(s.y, part)], r.pg_all.at[mine, cols], r.pg_x_sem.at[part, s.y, s.x], device
            )
        r.pg_all[mine, cols] = r.pg[:, self.wide_cols(s.y, part)]

    def pass_agg(self):
        s, r = self.s, self.s.r
        for a in s.xs:
            ref = r.agg_all.at[:, self.nodes(s.y, a)]
            s.arrived(ref, r.agg_x_sem.at[a])
            for device in s.to_y:
                s.send(ref, ref, r.agg_y_sem.at[s.y, a], device)

    def pass_pg(self, part):
        s, r, fw = self.s, self.s.r, self.s.plan.fw
        for b in s.ys:
            ref = r.pg_all.at[self.nodes(b, s.x), pl.ds(part * fw, fw)]
            s.arrived(ref, r.pg_y_sem.at[part, b])
            for device in s.to_x:
                s.send(ref, ref, r.pg_x_sem.at[part, b, s.x], device)

    def await_agg(self):
        s, r = self.s, self.s.r
        for b in s.ys:
            for a in range(s.plan.nx):
                s.arrived(r.agg_all.at[:, self.nodes(b, a)], r.agg_y_sem.at[b, a])

    def tile_part(self, part):
        s, r, plan = self.s, self.s.r, self.s.plan
        fw, fh, tile = plan.fw, plan.fh, self.tile
        cols = pl.ds(part * fw, fw)
        for a in s.xs:
            for b in range(plan.ny):
                s.arrived(r.pg_all.at[self.nodes(b, a), cols], r.pg_x_sem.at[part, b, a])

        def product(rows_from, store):
            def step(i):
                rows = r.agg_all[at(rows_from + i * tile, tile), :]
                store(at(i * tile, tile), jnp.dot(rows, r.pg_all[:, cols], preferred_element_type=F32))

            loop(fh // tile, step)

        def to_half(rows, value):
            r.tile_send[part, rows, :] = value.astype(BF16)

        product((1 - s.k) * fh, to_half)
        s.send(r.tile_send.at[part], r.tile_recv.at[part], r.tile_sem.at[part], s.twin)

        def to_own(rows, value):
            r.tile[part, rows, :] = value

        product(s.k * fh, to_own)

    def own_part(self, part, a):
        r, fz = self.s.r, self.s.plan.fz
        rows = at(a * fz, fz)
        return r.tile[part, rows, :] + r.tile_recv[part, rows, :].astype(F32)

    def sum_start(self, part):
        s, r = self.s, self.s.r
        s.arrived(r.tile_recv.at[part], r.tile_sem.at[part])
        pair, other = self.pair, self.other
        targets = [other, s.plan.nz - 1 - pair, pair]

        @pl.when(self.end)
        def _():
            for i, a in enumerate(targets):
                r.sum_send[part, i] = self.own_part(part, a).astype(BF16)

        for i in range(3):
            s.send(
                r.sum_send.at[part, i], r.sum_recv.at[part, i], r.sum_sem.at[part, i],
                s.plan.device(pair, s.y, s.x, s.k), self.end,
            )

    def sum_step(self, part, i, into, a, to):
        s, r = self.s, self.s.r

        @pl.when(self.middle)
        def _():
            s.arrived(r.sum_recv.at[part, i], r.sum_sem.at[part, i])
            r.sum_send[part, into - 3] = (self.own_part(part, a) + r.sum_recv[part, i].astype(F32)).astype(BF16)

        s.send(
            r.sum_send.at[part, into - 3], r.sum_recv.at[part, into], r.sum_sem.at[part, into],
            s.plan.device(to, s.y, s.x, s.k), self.middle,
        )

    def sum_across(self, part):
        far = self.s.plan.nz - 1 - self.pair
        self.sum_step(part, 0, 3, far, self.other)
        self.sum_step(part, 1, 4, self.other, self.other)

    def sum_out(self, part):
        self.sum_step(part, 3, 5, self.pair, self.pair)

    def sum_end(self, part):
        s, r = self.s, self.s.r
        mine = self.own_part(part, s.z)

        @pl.when(self.middle)
        def _():
            s.arrived(r.sum_recv.at[part, 2], r.sum_sem.at[part, 2])
            s.arrived(r.sum_recv.at[part, 4], r.sum_sem.at[part, 4])
            r.final[part] = (mine + r.sum_recv[part, 2].astype(F32) + r.sum_recv[part, 4].astype(F32)).astype(BF16)

        @pl.when(self.end)
        def _():
            s.arrived(r.sum_recv.at[part, 5], r.sum_sem.at[part, 5])
            r.final[part] = (mine + r.sum_recv[part, 5].astype(F32)).astype(BF16)

        here = (s.z, s.y, s.x, s.k)
        self.spread(r.final.at[part], part, here, s.to_x + s.to_y + [s.twin])
        pair, other = s.plan.device(self.pair, s.y, s.x, s.k), s.plan.device(self.other, s.y, s.x, s.k)
        self.spread(r.final.at[part], part, here, [pair])
        self.spread(r.final.at[part], part, here, [other], self.middle)
        copy = pltpu.make_async_copy(r.final.at[part], self.piece(part, *here), r.local_sem.at[part])
        copy.start()
        self.copies.append(copy)

    def piece(self, part, a_z, a_y, a_x, a_k):
        plan = self.s.plan
        return self.s.r.low.at[at(a_x * plan.fa + a_k * plan.fh + a_z * plan.fz, plan.fz), self.wide_cols(a_y, part)]

    def spread(self, source, part, origin, devices, when=None):
        for device in devices:
            self.s.send(source, self.piece(part, *origin), self.s.r.gather_sem.at[(part,) + origin], device, when)

    def take(self, part, *origin):
        self.s.arrived(self.piece(part, *origin), self.s.r.gather_sem.at[(part,) + origin])

    def line_order(self):
        return [self.s.z, self.pair, 2 - self.s.z // 2, 3 - 3 * (self.s.z // 2)]

    def gather_line(self, part, i):
        s = self.s
        origin = (self.line_order()[i], s.y, s.x, s.k)
        self.take(part, *origin)
        onward = s.plan.device(self.other if i == 1 else self.pair, s.y, s.x, s.k)
        self.spread(self.piece(part, *origin), part, origin, [onward], self.middle)
        self.spread(self.piece(part, *origin), part, origin, s.to_x + s.to_y + [s.twin])

    def gather_plane(self, part, i):
        s = self.s
        a_z = self.line_order()[i]
        even = lax.rem(a_z, 2) == 0
        odd = lax.rem(a_z, 2) == 1
        for a_x in s.xs:
            origin = (a_z, s.y, a_x, s.k)
            self.take(part, *origin)
            self.spread(self.piece(part, *origin), part, origin, s.to_y, even)
            self.spread(self.piece(part, *origin), part, origin, [s.twin])
        for a_y in s.ys:
            origin = (a_z, a_y, s.x, s.k)
            self.take(part, *origin)
            self.spread(self.piece(part, *origin), part, origin, s.to_x, odd)
            self.spread(self.piece(part, *origin), part, origin, [s.twin])

    def gather_corner(self, part, i):
        s = self.s
        for a_x in s.xs:
            for a_y in s.ys:
                origin = (self.line_order()[i], a_y, a_x, s.k)
                self.take(part, *origin)
                self.spread(self.piece(part, *origin), part, origin, [s.twin])

    def gather_twin(self, part):
        s, plan = self.s, self.s.plan
        for a_z in range(plan.nz):
            for a_y in range(plan.ny):
                for a_x in range(plan.nx):
                    self.take(part, a_z, a_y, a_x, 1 - s.k)

    def grads_start(self):
        s, r, plan = self.s, self.s.r, self.s.plan
        fs, wb = plan.slice, plan.wb
        mine = at(((s.k * plan.nx + s.x) * plan.nz + s.z) * NODE, NODE)
        for part in range(BACK):
            for a, device in zip(s.zs, s.to_z):
                s.send(
                    r.scaled.at[:, at(a * fs + part * wb, wb)], r.grads.at[mine, pl.ds(part * wb, wb)],
                    r.grads_z_sem.at[part, s.z], device,
                )
        r.grads[mine, :] = r.scaled[:, at(s.z * fs, fs)]

    def grads_x(self, part):
        s, r, plan = self.s, self.s.r, self.s.plan
        cols = pl.ds(part * plan.wb, plan.wb)
        for a in s.zs:
            s.arrived(
                r.grads.at[at(((s.k * plan.nx + s.x) * plan.nz + a) * NODE, NODE), cols], r.grads_z_sem.at[part, a]
            )
        ref = r.grads.at[self.line_rows(s.k, s.x), cols]
        for device in s.to_x:
            s.send(ref, ref, r.grads_x_sem.at[part, s.x], device)
        s.send(ref, ref, r.grads_k_sem.at[part, s.x], s.twin)

    def grads_twin(self, part):
        s, r, plan = self.s, self.s.r, self.s.plan
        for a in s.xs:
            ref = r.grads.at[self.line_rows(s.k, a), pl.ds(part * plan.wb, plan.wb)]
            s.arrived(ref, r.grads_x_sem.at[part, a])
            s.send(ref, ref, r.grads_k_sem.at[part, a], s.twin)

    def target(self, part):
        s, r, plan = self.s, self.s.r, self.s.plan
        cols = pl.ds(part * plan.wb, plan.wb)
        for a in range(plan.nx):
            s.arrived(r.grads.at[self.line_rows(1 - s.k, a), cols], r.grads_k_sem.at[part, a])

        def product(b, store):
            def step(i):
                rows = r.adj[at(b * plan.group + i * 256, 256), :]
                store(at(i * 256, 256), jnp.dot(rows, r.grads[:, cols], preferred_element_type=F32))

            loop(plan.group // 256, step)

        for i, (b, device) in enumerate(zip(s.ys, s.to_y)):

            def to_y(rows, value):
                r.y_send[part, i, rows, :] = value.astype(BF16)

            product(b, to_y)
            there = plan.ny - 2 - i
            s.send(r.y_send.at[part, i], r.y_recv.at[part, there], r.y_sem.at[part, there], device)

        def to_target(rows, value):
            r.target[part, rows, :] = value

        product(s.y, to_target)

    def back(self, part):
        s, r, plan = self.s, self.s.r, self.s.plan
        value = r.target[part]
        for i in range(plan.ny - 1):
            s.arrived(r.y_recv.at[part, i], r.y_sem.at[part, i])
            value = value + r.y_recv[part, i].astype(F32)
        r.back[part] = value.astype(BF16)
        cols = at(s.z * plan.slice + part * plan.wb, plan.wb)
        for a, device in zip(s.zs, s.to_z):
            s.send(r.back.at[part, at(a * NODE, NODE)], r.returned.at[:, cols], r.returned_sem.at[part, s.z], device)
        r.returned[:, cols] = r.back[part, at(s.z * NODE, NODE), :]

    def through(self):
        s, r, plan = self.s, self.s.r, self.s.plan
        for part in range(BACK):
            for a in s.zs:
                cols = at(a * plan.slice + part * plan.wb, plan.wb)
                s.arrived(r.returned.at[:, cols], r.returned_sem.at[part, a])
        r.returned[...] = (r.returned[...].astype(F32) + 2.0 * r.scaled[...].astype(F32)).astype(BF16)
        for chunk in range(CHUNKS):
            rows = pl.ds(chunk * plan.slice, plan.slice)
            value = lax.dot_general(
                r.returned[...], r.w[rows, :], (((1,), (1,)), ((), ())), preferred_element_type=F32
            )
            for a in range(plan.nz):
                cols = pl.ds(a * plan.slice + chunk * plan.width, plan.width)
                r.fg[:, cols] = value[:, a * plan.width : (a + 1) * plan.width]

    def bias_start(self):
        s, r = self.s, self.s.r
        s.send(r.bias_sum, r.bias_k.at[s.k], r.bias_k_sem.at[s.k], s.twin)
        r.bias_k[s.k] = r.bias_sum[...]

    def bias_stage(self, stage):
        s, r, plan = self.s, self.s.r, self.s.plan
        ref, sem, peers, count = (
            (r.bias_k, r.bias_k_sem, [1 - s.k], CORES),
            (r.bias_x, r.bias_x_sem, s.xs, plan.nx),
            (r.bias_y, r.bias_y_sem, s.ys, plan.ny),
            (r.bias_z, r.bias_z_sem, s.zs, plan.nz),
        )[stage]
        for a in peers:
            s.arrived(ref.at[a], sem.at[a])
        value = ref[0]
        for a in range(1, count):
            value = value + ref[a]
        if stage == 3:
            r.bias_grad[...] = value
            return
        ref, sem, index, devices = (
            (r.bias_x, r.bias_x_sem, s.x, s.to_x),
            (r.bias_y, r.bias_y_sem, s.y, s.to_y),
            (r.bias_z, r.bias_z_sem, s.z, s.to_z),
        )[stage]
        ref[index] = value
        for device in devices:
            s.send(ref.at[index], ref.at[index], sem.at[index], device)

    def run(self):
        self.bias_start()
        self.pass_agg()
        self.pass_pg(0)
        self.grads_start()
        self.bias_stage(0)
        self.pass_pg(1)
        self.await_agg()
        self.tile_part(0)
        self.grads_x(0)
        self.sum_start(0)
        self.tile_part(1)
        self.grads_x(1)
        self.sum_start(1)
        self.sum_across(0)
        self.grads_twin(0)
        self.bias_stage(1)
        self.target(0)
        self.sum_out(0)
        self.sum_end(0)
        self.sum_across(1)
        self.grads_twin(1)
        self.target(1)
        self.gather_line(0, 1)
        self.sum_out(1)
        self.sum_end(1)
        self.back(0)
        self.bias_stage(2)
        self.gather_plane(0, 0)
        self.gather_line(0, 2)
        self.gather_plane(0, 1)
        self.gather_line(0, 3)
        self.back(1)
        self.gather_plane(0, 2)
        self.gather_line(1, 1)
        self.gather_plane(0, 3)
        self.gather_plane(1, 0)
        self.gather_line(1, 2)
        self.gather_plane(1, 1)
        self.gather_line(1, 3)
        self.gather_plane(1, 2)
        self.gather_plane(1, 3)
        self.bias_stage(3)
        self.through()
        for part in range(WIDE):
            for i in range(self.s.plan.nz):
                self.gather_corner(part, i)
        for part in range(WIDE):
            self.gather_twin(part)
        for copy in self.copies:
            copy.wait()


def prepare(s):
    plan, r = s.plan, s.r
    for start in range(0, plan.feat, NODE):
        r.x_t[start : start + NODE, :] = r.x[:, start : start + NODE].T
    for c in range(plan.cols):
        part = r.codes[:, c * NODE : (c + 1) * NODE]
        ones = jnp.sum(jnp.where(part >= 0, 1.0, 0.0), axis=0, keepdims=True)
        r.count[c] = jnp.broadcast_to(ones, (8, NODE))


def whole_kernel(plan, names, *refs):
    s = Step(plan, Refs(names, refs))
    w_copies = s.weight_copies()
    s.r.cot_copy = pltpu.make_async_copy(s.r.cot_hbm, s.r.cot, s.r.cot_sem)
    for copy in w_copies + [s.r.cot_copy]:
        copy.start()
    prepare(s)
    greet(s.to_z + s.to_y + s.to_x + [s.twin] + s.to_far)
    backward = BackwardHalf(s, [])
    forward_half(s, w_copies, backward.agg_ready, backward.pg_ready)
    backward.run()
    s.send.finish()


def forward_kernel(plan, names, *refs):
    s = Step(plan, Refs(names, refs))
    w_copies = s.weight_copies()
    s.r.cot_copy = pltpu.make_async_copy(s.r.cot_hbm, s.r.cot, s.r.cot_sem)
    for copy in w_copies + [s.r.cot_copy]:
        copy.start()
    prepare(s)
    greet(s.to_z + s.to_y + s.to_x + [s.twin] + s.to_far)
    forward_half(s, w_copies, lambda: None, lambda part: None)
    s.send.finish()


def backward_kernel(plan, names, *refs):
    s = Step(plan, Refs(names, refs))
    w_copies = s.weight_copies()
    for copy in w_copies:
        copy.start()
    greet(s.to_z + s.to_y + s.to_x + [s.twin])
    backward = BackwardHalf(s, w_copies)
    backward.agg_ready()
    for part in range(WIDE):
        backward.pg_ready(part)
    for copy in w_copies:
        copy.wait()
    backward.run()
    s.send.finish()


def cast_kernel(low, act_in, fg_in, bias_in, out, act_out, fg_out, bias_out, wide, sems):
    copies = [
        pltpu.make_async_copy(src, dst, sems.at[i])
        for i, (src, dst) in enumerate(((act_in, act_out), (fg_in, fg_out), (bias_in, bias_out)))
    ]
    for copy in copies:
        copy.start()
    count, rows, _ = wide.shape
    for i in range(count):
        wide[i] = low[i * rows : (i + 1) * rows, :].astype(F32)
        copy = pltpu.make_async_copy(wide.at[i], out.at[pl.ds(i * rows, rows)], sems.at[3 + i])
        copy.start()
        copies.append(copy)
    for copy in copies:
        copy.wait()


def shaped(*items):
    return jax.ShapeDtypeStruct(*items)


def forward_scratch(plan):
    c, nz = CHUNKS, plan.nz
    v = pltpu.VMEM
    return dict(
        x_t=v((plan.feat, NODE), BF16),
        cot=v((NODE, plan.feat), BF16),
        gathered=v((plan.slice, plan.columns), BF16),
        line_codes=v((nz, plan.slots, plan.block), I32),
        count=v((plan.cols, 8, NODE), F32),
        degrees=v((plan.cols, 8, NODE), F32),
        half_send=v((c, plan.width, plan.half), BF16),
        half_recv=v((c, plan.width, plan.half), BF16),
        x_send=v((c, plan.width, plan.half), BF16),
        x_recv=v((c, plan.nx, plan.width, plan.third), BF16),
        own=v((c, plan.width, plan.half), F32),
        total=v((c, plan.width, plan.third), BF16),
        summed=v((plan.feat, NODE), BF16),
        agg_rows=v((NODE, plan.feat), BF16),
        preact=v((NODE, plan.feat), F32),
        cot_sem=DMA(()),
        codes_sem=DMA((nz,)),
        degree_sem=DMA((plan.cols,)),
        slice_sem=DMA((c, nz)),
        line_sem=DMA((c, nz, plan.ny)),
        half_sem=DMA((c,)),
        x_sem=DMA((c, plan.nx)),
        back_sem=DMA((c, nz)),
    )


def forward_sends(plan):
    dz, dy, dx = plan.nz - 1, plan.ny - 1, plan.nx - 1
    return dz + CHUNKS * (dz + dy) + plan.cols - 1 + CHUNKS * dz * dy + CHUNKS * (1 + dx + dz)


def backward_scratch(plan):
    nz, ny, nx, w = plan.nz, plan.ny, plan.nx, WIDE
    v = pltpu.VMEM
    return dict(
        agg_all=v((plan.fa, plan.depth), BF16),
        pg_all=v((plan.depth, plan.fp), BF16),
        grads=v((plan.line, plan.slice), BF16),
        tile_send=v((w, plan.fh, plan.fw), BF16),
        tile_recv=v((w, plan.fh, plan.fw), BF16),
        tile=v((w, plan.fh, plan.fw), F32),
        sum_send=v((w, 3, plan.fz, plan.fw), BF16),
        sum_recv=v((w, 6, plan.fz, plan.fw), BF16),
        final=v((w, plan.fz, plan.fw), BF16),
        y_send=v((BACK, ny - 1, plan.group, plan.wb), BF16),
        y_recv=v((BACK, ny - 1, plan.group, plan.wb), BF16),
        target=v((BACK, plan.group, plan.wb), F32),
        back=v((BACK, plan.group, plan.wb), BF16),
        returned=v((NODE, plan.feat), BF16),
        bias_k=v((CORES, 1, plan.feat), F32),
        bias_x=v((nx, 1, plan.feat), F32),
        bias_y=v((ny, 1, plan.feat), F32),
        bias_z=v((nz, 1, plan.feat), F32),
        local_sem=DMA((w,)),
        agg_x_sem=DMA((nx,)),
        agg_y_sem=DMA((ny, nx)),
        pg_y_sem=DMA((w, ny)),
        pg_x_sem=DMA((w, ny, nx)),
        grads_z_sem=DMA((BACK, nz)),
        grads_x_sem=DMA((BACK, nx)),
        grads_k_sem=DMA((BACK, nx)),
        tile_sem=DMA((w,)),
        sum_sem=DMA((w, 6)),
        gather_sem=DMA((w, nz, ny, nx, CORES)),
        y_sem=DMA((BACK, ny - 1)),
        returned_sem=DMA((BACK, nz)),
        bias_k_sem=DMA((CORES,)),
        bias_x_sem=DMA((nx,)),
        bias_y_sem=DMA((ny,)),
        bias_z_sem=DMA((nz,)),
    )


def backward_sends(plan):
    dz, dy, dx = plan.nz - 1, plan.ny - 1, plan.nx - 1
    factors = dx + dy + WIDE * (dx + dy) + dx * dy + WIDE * dx * dy
    tiles = WIDE * (1 + 3 + 3)
    gathers = WIDE * (dx + dy + 3 + 3 * (dx + dy + 2) + 4 * (2 * dx * dy + dx + dy) + 4 * dx * dy)
    grads = BACK * (dz + 2 * dx + 1 + dy + dz)
    return factors + tiles + gathers + grads + 1 + dx + dy + dz


def call(body, plan, name, identity, inputs, outputs, scratch, n_sends, vmem=127 << 19):
    scratch = dict(scratch, w=pltpu.VMEM((plan.feat, plan.feat), BF16), w_sem=DMA((CHUNKS * plan.nz,)), sems=DMA((n_sends,)))
    names = list(inputs) + list(outputs) + list(scratch)
    return pl.pallas_call(
        functools.partial(body, plan, names),
        name=name,
        out_shape=[pltpu.VMEM(shape, kind) if plan.merged else shaped(shape, kind) for shape, kind, _ in outputs.values()],
        in_specs=[pl.BlockSpec(memory_space=space) for _, space in inputs.values()],
        out_specs=[pl.BlockSpec(memory_space=space) for _, _, space in outputs.values()],
        scratch_shapes=list(scratch.values()),
        compiler_params=pltpu.CompilerParams(
            collective_id=identity, has_side_effects=True, vmem_limit_bytes=vmem
        ),
    )(*[array for array, _ in inputs.values()])


def on_device(plan, features, neighbours, edge_mask, weight, bias, cotangent):
    codes = jnp.where(edge_mask > 0, neighbours, -1).T
    feat, v, far = plan.feat, pltpu.VMEM, pl.ANY
    arguments = dict(x=(features, v), codes=(codes, v), w_hbm=(weight, far), bias=(bias.reshape(1, -1), v), cot_hbm=(cotangent, far))
    between = dict(
        pg=((NODE, feat), BF16),
        scaled=((NODE, feat), BF16),
        agg=((feat, NODE), BF16),
        adj=((plan.columns, plan.line), BF16),
        bias_sum=((1, feat), F32),
    )
    act = dict(act=((NODE, feat), BF16, v))
    results = dict(fg=((NODE, feat), F32, v), low=((feat, feat), BF16, far), bias_grad=((1, feat), F32, v))
    if plan.merged:
        scratch = dict(forward_scratch(plan), **backward_scratch(plan))
        scratch.update({name: v(*item) for name, item in between.items()})
        activations, feature_grad, low, bias_grad = call(
            whole_kernel, plan, "layer", 0, arguments, dict(act, **results), scratch,
            forward_sends(plan) + backward_sends(plan), 46 << 20,
        )
    else:
        activations, *kept = call(
            forward_kernel, plan, "forward", 0, arguments,
            dict(act, **{name: item + (v,) for name, item in between.items()}),
            forward_scratch(plan), forward_sends(plan),
        )
        feature_grad, low, bias_grad = call(
            backward_kernel, plan, "backward", 1,
            dict({name: (array, v) for name, array in zip(between, kept)}, w_hbm=(weight, far)),
            results, backward_scratch(plan), backward_sends(plan),
        )
    parts = 8
    vmem, hbm = pl.BlockSpec(memory_space=v), pl.BlockSpec(memory_space=far)
    weight_grad, activations, feature_grad, bias_grad = pl.pallas_call(
        cast_kernel,
        name="cast",
        out_shape=[shaped(low.shape, F32)] + [shaped(a.shape, a.dtype) for a in (activations, feature_grad, bias_grad)],
        in_specs=[vmem] * 4,
        out_specs=[hbm] * 4,
        scratch_shapes=[v((parts, feat // parts, feat), F32), DMA((3 + parts,))],
        compiler_params=pltpu.CompilerParams(vmem_limit_bytes=30 << 20),
    )(low, activations, feature_grad, bias_grad)
    return activations, feature_grad, weight_grad, bias_grad.reshape(-1)


def solution(mesh):
    placed = (
        P(("row", "col"), None),
        P("row", "col"),
        P("row", "col"),
        P(),
        P(),
        P(("row", "col"), None),
    )

    def run(*args):
        plan = Plan(mesh, args[0].shape[1], args[1].shape[1] // mesh.shape["col"])
        return jax.shard_map(
            functools.partial(on_device, plan),
            mesh=mesh,
            in_specs=placed,
            out_specs=(P(("row", "col"), None), P(("row", "col"), None), P(), P()),
            check_vma=False,
        )(*args)

    return run
```

time: 451 us -> 141 us (0.31)
  waiting for transfers between devices: 331 us -> 0 us
  Pallas kernels: 0 us -> 137 us
  blocking collectives: 46.8 us -> 0 us
  matrix products: 41.1 us -> 0 us
  between operations: 14.5 us -> 0.8 us
  other arithmetic: 14.7 us -> 1.39 us
    pallas_call x0 -> x2, Pallas kernels: none -> 137 us  [the longest x1 130 us: call(): pl.pallas_call(functools.partial(body, plan, names), name=name, out_shape...]
    psum x1 -> x0, waiting for transfers between devices: 135 us -> none  [on_device(): lax.psum(weight_term.astype(jnp.bfloat16), ('row', 'col'))]
    reduce_scatter x2 -> x0, waiting for transfers between devices: 102 us -> none  [the longest x1 80.2 us: on_device(): lax.psum_scatter(target.astype(jnp.bfloat16), 'row', scatter_dimension=0,...]
    all_gather x2 -> x0, waiting for transfers between devices: 93 us -> none  [the longest x1 76.4 us: on_device(): column_rows = lax.all_gather(features, 'row', axis=0, tiled=True)]
    psum x1 -> x0, blocking collectives: 41.2 us -> none  [on_device(): lax.psum(jnp.sum(preact_grad.astype(jnp.float32), axis=0), ('row', 'col'))]
    dot_general x5 -> x0, matrix products: 41.1 us -> none  [the longest x1 10.8 us: on_device(): lax.dot_general(adjacency, block_grads, (((0,), (0,)), ((), ())), preferr...]
    convert_element_type x2 -> x0, other arithmetic: 12.4 us -> none  [the longest x1 11.7 us: on_device(): lax.psum(weight_term.astype(jnp.bfloat16), ('row', 'col'))]
    unnamed x1 -> x0, blocking collectives: 5.66 us -> none
  transfers between devices with their start and end apart: 5 -> 0, of which waited for: 5 -> 0; matrix products, arithmetic and copies ran while one was open for 7% -> 0% of each run, Pallas kernels for 0% -> 0%
where the time goes in v3:
time: 141 us; the launch traced here: 139 us
  Pallas kernels  137 us (97%)
    pallas_call x1, Pallas kernels, call(): pl.pallas_call(functools.partial(body, plan, names), name=name, out_shape...  130 us
    pallas_call x1, Pallas kernels, on_device(): pl.pallas_call(cast_kernel, name='cast', out_shape=[shaped(low.shape, F32...  6.47 us

profile of v3, /device:TPU:0, one launch (start us, length us, event | category | flops | bytes accessed | tf_op | source)
XLA Modules:
  0.0 138.7 jit_solution(5693394067895272801)
XLA Ops:
  0.6 1.4 %select_bitcast_fusion.refs_1_ = s32[16,512]{1,0:T(8,128)} fusion(s32[512,16]{0,1:T(8,128)} %param.7, s32[512,16]{0,1:T(8,128)} %param.8), kind=kLoop, calls=%fused_computation | loop fusion | flops 16384 | bytes 98304 | tf_op jit(solution)/shard_map/transpose | solution.py:891
  2.0 130.1 %layer.1 = (bf16[128,2048]{1,0:T(8,128)(2,1)S(1)}, f32[128,2048]{1,0:T(8,128)S(1)}, bf16[2048,2048]{1,0:T(8,128)(2,1)S(1)}, f32[1,2048]{1,0:T(1,128)S(1)}) custom-call(bf16[128,2048]{1,0:T(8,128)(2,1)} %refs_0_.1, s32[16,512]{1,0:T(8,128)} %select_bitcast_fusion.refs_1_, bf16[2048,2048]{1,0:T(8,128)(2,1)} %refs_2_.1, f32[1,2048]{1,0:T(1,128)} %bitcast.4, ...), custom_call_target="tpu_custom_call" | custom-call | tf_op jit(solution)/shard_map/layer/pallas_call | solution.py:877
  132.1 6.5 %cast.1 = (f32[2048,2048]{1,0:T(8,128)}, bf16[128,2048]{1,0:T(8,128)(2,1)}, f32[128,2048]{1,0:T(8,128)}, f32[1,2048]{1,0:T(1,128)}) custom-call(bf16[2048,2048]{1,0:T(8,128)(2,1)S(1)} %get-tuple-element.12.low, bf16[128,2048]{1,0:T(8,128)(2,1)S(1)} %get-tuple-element.13.act_in, f32[128,2048]{1,0:T(8,128)S(1)} %get-tuple-element.14.fg_in, ...), custom_call_target="tpu_custom_call" | custom-call | tf_op jit(solution)/shard_map/cast/pallas_call | solution.py:923

commit v4 on v3

--- a/solution.py
+++ b/solution.py
@@ -14,7 +14,7 @@
 SPLIT = 4
 CORES = 2
 CHUNKS = 4
-WIDE = 2
+WIDE = 4
 BACK = 2
 
 
@@ -31,7 +31,8 @@
         self.half = self.line // CORES
         self.third = self.half // self.nx
         self.fa, self.fp = feat // self.nx, feat // self.ny
-        self.fh, self.fw = self.fa // CORES, self.fp // WIDE
+        self.wide = min(WIDE, self.fp // NODE)
+        self.fh, self.fw = self.fa // CORES, self.fp // self.wide
         self.fz = self.fh // self.nz
         self.group = self.nz * NODE
         self.wb = self.slice // BACK
@@ -104,7 +105,7 @@
     barrier = pltpu.get_barrier_semaphore()
     for device in devices:
         pl.semaphore_signal(barrier, inc=1, device_id=device, device_id_type=MESH)
-    pl.semaphore_wait(barrier, len(devices))
+    return lambda: pl.semaphore_wait(barrier, len(devices))
 
 
 class Step:
@@ -140,7 +141,7 @@
         return copies
 
 
-def forward_half(s, w_copies, agg_ready, pg_ready):
+def forward_half(s, w_copies, agg_ready, pass_agg, pg_ready):
     plan, r, send = s.plan, s.r, s.send
     nz, ny, nx, fs, width = plan.nz, plan.ny, plan.nx, plan.slice, plan.width
     half, third = plan.half, plan.third
@@ -236,13 +237,13 @@
         for a, device in zip(s.xs, s.to_x):
             cols = at(a * third, third)
             r.x_send[chunk, :, cols] = (r.own[chunk, :, cols] + r.half_recv[chunk, :, cols].astype(F32)).astype(BF16)
-            send(r.x_send.at[chunk, :, cols], r.x_recv.at[chunk, x], r.x_sem.at[chunk, x], device)
+            send(r.x_send.at[chunk, :, cols], r.x_recv.at[chunk, x], r.third_sem.at[chunk, x], device)
 
     def last(chunk):
         cols = at(x * third, third)
         value = r.own[chunk, :, cols] + r.half_recv[chunk, :, cols].astype(F32)
         for a in s.xs:
-            s.arrived(r.x_recv.at[chunk, a], r.x_sem.at[chunk, a])
+            s.arrived(r.x_recv.at[chunk, a], r.third_sem.at[chunk, a])
             value = value + r.x_recv[chunk, a].astype(F32)
         r.total[chunk] = value.astype(BF16)
         rows = at(z * fs + chunk * width, width)
@@ -285,6 +286,7 @@
             value = scale * (r.summed[rows, :].astype(F32) + 2.0 * r.x_t[rows, :].astype(F32))
             r.agg[rows, :] = value.astype(BF16)
             r.agg_rows[:, (chunk * nz + a) * width : (chunk * nz + a + 1) * width] = value.T.astype(BF16)
+        agg_ready(chunk)
 
     def part_of(chunk, cols):
         rows = pl.ds(chunk * fs, fs)
@@ -309,10 +311,12 @@
     combine(1)
     last(3)
     add_chunk(1)
+    pass_agg(0)
     combine(2)
     add_chunk(2)
+    pass_agg(1)
     combine(3)
-    agg_ready()
+    pass_agg(2)
     for i in range(3 * nz, 4 * nz):
         w_copies[i].wait()
     r.cot_copy.wait()
@@ -330,14 +334,14 @@
         r.scaled[:, cols] = (scale_col * wide).astype(BF16)
         r.bias_sum[:, cols] = jnp.sum(wide, axis=0, keepdims=True)
 
-    for part in range(WIDE):
+    for part in range(plan.wide):
         loop(ny, lambda b: layer(at(b * plan.fp + part * plan.fw, plan.fw)))
         pg_ready(part)
 
 
 class BackwardHalf:
-    def __init__(self, s, w_copies):
-        self.s, self.w_copies = s, w_copies
+    def __init__(self, s):
+        self.s = s
         plan = s.plan
         self.pair = s.z + 1 - 2 * lax.rem(s.z, 2)
         self.other = plan.nz - 1 - s.z
@@ -355,33 +359,50 @@
     def wide_cols(self, b, part):
         return at(b * self.s.plan.fp + part * self.s.plan.fw, self.s.plan.fw)
 
-    def agg_ready(self):
-        s, r, fa = self.s, self.s.r, self.s.plan.fa
+    def agg_blocks(self, chunk, part):
+        plan = self.s.plan
+        for i in range(plan.nz // plan.nx):
+            start = i * plan.slice + chunk * plan.width
+            yield at(part * plan.fa + start, plan.width), pl.ds(start, plan.width)
+
+    def agg_ready(self, chunk):
+        s, r = self.s, self.s.r
         mine = self.nodes(s.y, s.x)
         for a, device in zip(s.xs, s.to_x):
-            s.send(r.agg.at[at(a * fa, fa)], r.agg_all.at[:, mine], r.agg_x_sem.at[s.x], device)
-        for device in s.to_y:
-            s.send(r.agg.at[at(s.x * fa, fa)], r.agg_all.at[:, mine], r.agg_y_sem.at[s.y, s.x], device)
-        r.agg_all[:, mine] = r.agg[at(s.x * fa, fa), :]
-
-    def pg_ready(self, part):
+            for i, (source, rows) in enumerate(self.agg_blocks(chunk, a)):
+                s.send(r.agg.at[source], r.agg_all.at[rows, mine], r.agg_x_sem.at[chunk, i, s.x], device)
+        for i, (source, rows) in enumerate(self.agg_blocks(chunk, s.x)):
+            for device in s.to_y:
+                s.send(r.agg.at[source], r.agg_all.at[rows, mine], r.agg_y_sem.at[chunk, i, s.y, s.x], device)
+            r.agg_all[rows, mine] = r.agg[source, :]
+
+    def pg_x(self, part):
         s, r, fw = self.s, self.s.r, self.s.plan.fw
         mine, cols = self.nodes(s.y, s.x), pl.ds(part * fw, fw)
-        for b, device in zip(s.ys, s.to_y):
-            s.send(r.pg.at[:, self.wide_cols(b, part)], r.pg_all.at[mine, cols], r.pg_y_sem.at[part, s.y], device)
         for device in s.to_x:
             s.send(
                 r.pg.at[:, self.wide_cols(s.y, part)], r.pg_all.at[mine, cols], r.pg_x_sem.at[part, s.y, s.x], device
             )
         r.pg_all[mine, cols] = r.pg[:, self.wide_cols(s.y, part)]
 
-    def pass_agg(self):
+    def pg_y(self, part):
+        s, r, fw = self.s, self.s.r, self.s.plan.fw
+        mine, cols = self.nodes(s.y, s.x), pl.ds(part * fw, fw)
+        for b, device in zip(s.ys, s.to_y):
+            s.send(r.pg.at[:, self.wide_cols(b, part)], r.pg_all.at[mine, cols], r.pg_y_sem.at[part, s.y], device)
+
+    def pg_ready(self, part):
+        self.pg_y(part)
+        self.pg_x(part)
+
+    def pass_agg(self, chunk):
         s, r = self.s, self.s.r
-        for a in s.xs:
-            ref = r.agg_all.at[:, self.nodes(s.y, a)]
-            s.arrived(ref, r.agg_x_sem.at[a])
-            for device in s.to_y:
-                s.send(ref, ref, r.agg_y_sem.at[s.y, a], device)
+        for i, (_, rows) in enumerate(self.agg_blocks(chunk, s.x)):
+            for a in s.xs:
+                ref = r.agg_all.at[rows, self.nodes(s.y, a)]
+                s.arrived(ref, r.agg_x_sem.at[chunk, i, a])
+                for device in s.to_y:
+                    s.send(ref, ref, r.agg_y_sem.at[chunk, i, s.y, a], device)
 
     def pass_pg(self, part):
         s, r, fw = self.s, self.s.r, self.s.plan.fw
@@ -393,9 +414,11 @@
 
     def await_agg(self):
         s, r = self.s, self.s.r
-        for b in s.ys:
-            for a in range(s.plan.nx):
-                s.arrived(r.agg_all.at[:, self.nodes(b, a)], r.agg_y_sem.at[b, a])
+        for chunk in range(CHUNKS):
+            for i, (_, rows) in enumerate(self.agg_blocks(chunk, s.x)):
+                for b in s.ys:
+                    for a in range(s.plan.nx):
+                        s.arrived(r.agg_all.at[rows, self.nodes(b, a)], r.agg_y_sem.at[chunk, i, b, a])
 
     def tile_part(self, part):
         s, r, plan = self.s, self.s.r, self.s.plan
@@ -660,91 +683,83 @@
             s.send(ref.at[index], ref.at[index], sem.at[index], device)
 
     def run(self):
+        wide, nz = self.s.plan.wide, self.s.plan.nz
         self.bias_start()
-        self.pass_agg()
-        self.pass_pg(0)
         self.grads_start()
-        self.bias_stage(0)
-        self.pass_pg(1)
+        self.pass_agg(3)
+        for part in range(wide):
+            self.pass_pg(part)
         self.await_agg()
-        self.tile_part(0)
-        self.grads_x(0)
-        self.sum_start(0)
-        self.tile_part(1)
-        self.grads_x(1)
-        self.sum_start(1)
-        self.sum_across(0)
-        self.grads_twin(0)
-        self.bias_stage(1)
-        self.target(0)
-        self.sum_out(0)
-        self.sum_end(0)
-        self.sum_across(1)
-        self.grads_twin(1)
-        self.target(1)
-        self.gather_line(0, 1)
-        self.sum_out(1)
-        self.sum_end(1)
-        self.back(0)
-        self.bias_stage(2)
-        self.gather_plane(0, 0)
-        self.gather_line(0, 2)
-        self.gather_plane(0, 1)
-        self.gather_line(0, 3)
-        self.back(1)
-        self.gather_plane(0, 2)
-        self.gather_line(1, 1)
-        self.gather_plane(0, 3)
-        self.gather_plane(1, 0)
-        self.gather_line(1, 2)
-        self.gather_plane(1, 1)
-        self.gather_line(1, 3)
-        self.gather_plane(1, 2)
-        self.gather_plane(1, 3)
-        self.bias_stage(3)
-        self.through()
-        for part in range(WIDE):
-            for i in range(self.s.plan.nz):
-                self.gather_corner(part, i)
-        for part in range(WIDE):
+        stages = [
+            lambda p: (self.tile_part(p), self.sum_start(p)),
+            self.sum_across,
+            self.sum_out,
+            self.sum_end,
+            lambda p: (self.gather_line(p, 1), self.gather_plane(p, 0)),
+            lambda p: (self.gather_line(p, 2), self.gather_plane(p, 1)),
+            lambda p: (self.gather_line(p, 3), self.gather_plane(p, 2)),
+            lambda p: self.gather_plane(p, 3),
+            lambda p: [self.gather_corner(p, i) for i in range(nz)],
+        ]
+        between = {0: (lambda: self.bias_stage(0), lambda: self.grads_x(0),), 1: (lambda: self.grads_x(1), lambda: self.bias_stage(1),), 2: (lambda: self.grads_twin(0), lambda: self.target(0),), 3: (lambda: self.grads_twin(1), lambda: self.target(1),), 5: (lambda: self.bias_stage(2),), 6: (lambda: self.back(0),), 7: (lambda: self.back(1),), 10: (lambda: self.bias_stage(3),), 11: (lambda: self.through(),)}
+        for tick in range(max(len(stages) + wide - 1, 1 + max(between))):
+            for part in reversed(range(wide)):
+                if 0 <= tick - part < len(stages):
+                    stages[tick - part](part)
+            for act in between.get(tick, ()):
+                act()
+        for part in range(wide):
             self.gather_twin(part)
         for copy in self.copies:
             copy.wait()
 
 
+def fetch(s, names):
+    copies = [pltpu.make_async_copy(getattr(s.r, name + "_far"), getattr(s.r, name), getattr(s.r, name + "_sem")) for name in names]
+    for copy in copies:
+        copy.start()
+    return copies
+
+
 def prepare(s):
     plan, r = s.plan, s.r
+    for c in range(plan.cols):
+        cols = pl.ds(c * NODE, NODE)
+        part = jnp.where(r.mask[:, cols] > 0, r.lists[:, cols], -1)
+        r.codes[:, cols] = part
+        ones = jnp.sum(jnp.where(part >= 0, 1.0, 0.0), axis=0, keepdims=True)
+        r.count[c] = jnp.broadcast_to(ones, (8, NODE))
     for start in range(0, plan.feat, NODE):
         r.x_t[start : start + NODE, :] = r.x[:, start : start + NODE].T
-    for c in range(plan.cols):
-        part = r.codes[:, c * NODE : (c + 1) * NODE]
-        ones = jnp.sum(jnp.where(part >= 0, 1.0, 0.0), axis=0, keepdims=True)
-        r.count[c] = jnp.broadcast_to(ones, (8, NODE))
+
+
+def opening(s):
+    met = greet(s.to_z + s.to_y + s.to_x + [s.twin] + s.to_far)
+    lists, mask, x, bias, s.r.cot_copy = fetch(s, ("lists", "mask", "x", "bias", "cot"))
+    w_copies = s.weight_copies()
+    for copy in w_copies:
+        copy.start()
+    for copy in (lists, mask, x, bias):
+        copy.wait()
+    prepare(s)
+    met()
+    return w_copies
 
 
 def whole_kernel(plan, names, *refs):
     s = Step(plan, Refs(names, refs))
-    w_copies = s.weight_copies()
-    s.r.cot_copy = pltpu.make_async_copy(s.r.cot_hbm, s.r.cot, s.r.cot_sem)
-    for copy in w_copies + [s.r.cot_copy]:
-        copy.start()
-    prepare(s)
-    greet(s.to_z + s.to_y + s.to_x + [s.twin] + s.to_far)
-    backward = BackwardHalf(s, [])
-    forward_half(s, w_copies, backward.agg_ready, backward.pg_ready)
+    w_copies = opening(s)
+    backward = BackwardHalf(s)
+    forward_half(s, w_copies, backward.agg_ready, backward.pass_agg, backward.pg_ready)
     backward.run()
     s.send.finish()
 
 
 def forward_kernel(plan, names, *refs):
     s = Step(plan, Refs(names, refs))
-    w_copies = s.weight_copies()
-    s.r.cot_copy = pltpu.make_async_copy(s.r.cot_hbm, s.r.cot, s.r.cot_sem)
-    for copy in w_copies + [s.r.cot_copy]:
-        copy.start()
-    prepare(s)
-    greet(s.to_z + s.to_y + s.to_x + [s.twin] + s.to_far)
-    forward_half(s, w_copies, lambda: None, lambda part: None)
+    w_copies = opening(s)
+    skip = lambda part: None
+    forward_half(s, w_copies, skip, skip, skip)
     s.send.finish()
 
 
@@ -753,13 +768,16 @@
     w_copies = s.weight_copies()
     for copy in w_copies:
         copy.start()
-    greet(s.to_z + s.to_y + s.to_x + [s.twin])
-    backward = BackwardHalf(s, w_copies)
-    backward.agg_ready()
-    for part in range(WIDE):
+    greet(s.to_z + s.to_y + s.to_x + [s.twin])()
+    backward = BackwardHalf(s)
+    for chunk in range(CHUNKS):
+        backward.agg_ready(chunk)
+    for part in range(plan.wide):
         backward.pg_ready(part)
     for copy in w_copies:
         copy.wait()
+    for chunk in range(CHUNKS - 1):
+        backward.pass_agg(chunk)
     backward.run()
     s.send.finish()
 
@@ -789,8 +807,17 @@
     c, nz = CHUNKS, plan.nz
     v = pltpu.VMEM
     return dict(
+        x=v((NODE, plan.feat), BF16),
+        x_sem=DMA(()),
+        lists=v((plan.slots, plan.block), I32),
+        lists_sem=DMA(()),
+        mask=v((plan.slots, plan.block), I32),
+        mask_sem=DMA(()),
+        bias=v((1, plan.feat), F32),
+        bias_sem=DMA(()),
+        cot=v((NODE, plan.feat), BF16),
+        codes=v((plan.slots, plan.block), I32),
         x_t=v((plan.feat, NODE), BF16),
-        cot=v((NODE, plan.feat), BF16),
         gathered=v((plan.slice, plan.columns), BF16),
         line_codes=v((nz, plan.slots, plan.block), I32),
         count=v((plan.cols, 8, NODE), F32),
@@ -810,7 +837,7 @@
         slice_sem=DMA((c, nz)),
         line_sem=DMA((c, nz, plan.ny)),
         half_sem=DMA((c,)),
-        x_sem=DMA((c, plan.nx)),
+        third_sem=DMA((c, plan.nx)),
         back_sem=DMA((c, nz)),
     )
 
@@ -821,7 +848,7 @@
 
 
 def backward_scratch(plan):
-    nz, ny, nx, w = plan.nz, plan.ny, plan.nx, WIDE
+    nz, ny, nx, w = plan.nz, plan.ny, plan.nx, plan.wide
     v = pltpu.VMEM
     return dict(
         agg_all=v((plan.fa, plan.depth), BF16),
@@ -843,8 +870,8 @@
         bias_y=v((ny, 1, plan.feat), F32),
         bias_z=v((nz, 1, plan.feat), F32),
         local_sem=DMA((w,)),
-        agg_x_sem=DMA((nx,)),
-        agg_y_sem=DMA((ny, nx)),
+        agg_x_sem=DMA((CHUNKS, nz // nx, nx)),
+        agg_y_sem=DMA((CHUNKS, nz // nx, ny, nx)),
         pg_y_sem=DMA((w, ny)),
         pg_x_sem=DMA((w, ny, nx)),
         grads_z_sem=DMA((BACK, nz)),
@@ -863,10 +890,10 @@
 
 
 def backward_sends(plan):
-    dz, dy, dx = plan.nz - 1, plan.ny - 1, plan.nx - 1
-    factors = dx + dy + WIDE * (dx + dy) + dx * dy + WIDE * dx * dy
-    tiles = WIDE * (1 + 3 + 3)
-    gathers = WIDE * (dx + dy + 3 + 3 * (dx + dy + 2) + 4 * (2 * dx * dy + dx + dy) + 4 * dx * dy)
+    dz, dy, dx, wide = plan.nz - 1, plan.ny - 1, plan.nx - 1, plan.wide
+    factors = (CHUNKS * plan.nz // plan.nx + wide) * (dx + dy + dx * dy)
+    tiles = wide * (1 + 3 + 3)
+    gathers = wide * (dx + dy + 3 + 3 * (dx + dy + 2) + 4 * (2 * dx * dy + dx + dy) + 4 * dx * dy)
     grads = BACK * (dz + 2 * dx + 1 + dy + dz)
     return factors + tiles + gathers + grads + 1 + dx + dy + dz
 
@@ -888,9 +915,15 @@
 
 
 def on_device(plan, features, neighbours, edge_mask, weight, bias, cotangent):
-    codes = jnp.where(edge_mask > 0, neighbours, -1).T
     feat, v, far = plan.feat, pltpu.VMEM, pl.ANY
-    arguments = dict(x=(features, v), codes=(codes, v), w_hbm=(weight, far), bias=(bias.reshape(1, -1), v), cot_hbm=(cotangent, far))
+    arguments = dict(
+        x_far=(features, far),
+        lists_far=(neighbours.T, far),
+        mask_far=(edge_mask.T, far),
+        w_hbm=(weight, far),
+        bias_far=(bias.reshape(1, -1), far),
+        cot_far=(cotangent, far),
+    )
     between = dict(
         pg=((NODE, feat), BF16),
         scaled=((NODE, feat), BF16),

time: 141 us -> 132 us (0.936); the launches traced: 139 us -> 132 us
  Pallas kernels: 137 us -> 131 us
    pallas_call x1, Pallas kernels: 130 us -> 125 us  [call(): pl.pallas_call(functools.partial(body, plan, names), name=name, out_shape...]
where the time goes in v4:
time: 132 us
  Pallas kernels  131 us (99%)
    pallas_call x1, Pallas kernels, call(): pl.pallas_call(functools.partial(body, plan, names), name=name, out_shape...  125 us
    pallas_call x1, Pallas kernels, on_device(): pl.pallas_call(cast_kernel, name='cast', out_shape=[shaped(low.shape, F32...  6.47 us

profile of v4, /device:TPU:0, one launch (start us, length us, event | category | flops | bytes accessed | tf_op | source)
XLA Modules:
  0.0 131.9 jit_solution(6795146228131640032)
XLA Ops:
  0.6 124.6 %layer.1 = (bf16[128,2048]{1,0:T(8,128)(2,1)S(1)}, f32[128,2048]{1,0:T(8,128)S(1)}, bf16[2048,2048]{1,0:T(8,128)(2,1)S(1)}, f32[1,2048]{1,0:T(1,128)S(1)}) custom-call(bf16[128,2048]{1,0:T(8,128)(2,1)} %refs_0_.1, s32[16,512]{1,0:T(8,128)} %bitcast.4, s32[16,512]{1,0:T(8,128)} %bitcast.5, bf16[2048,2048]{1,0:T(8,128)(2,1)} %refs_3_.1, f32[1,2048]{1,0:T(1,128)} %bitcast.6, ...), custom_call_target="tpu_custom_call" | custom-call | tf_op jit(solution)/shard_map/layer/pallas_call | solution.py:904
  125.3 6.5 %cast.1 = (f32[2048,2048]{1,0:T(8,128)}, bf16[128,2048]{1,0:T(8,128)(2,1)}, f32[128,2048]{1,0:T(8,128)}, f32[1,2048]{1,0:T(1,128)}) custom-call(bf16[2048,2048]{1,0:T(8,128)(2,1)S(1)} %get-tuple-element.12.low, bf16[128,2048]{1,0:T(8,128)(2,1)S(1)} %get-tuple-element.13.act_in, f32[128,2048]{1,0:T(8,128)S(1)} %get-tuple-element.14.fg_in, ...), custom_call_target="tpu_custom_call" | custom-call | tf_op jit(solution)/shard_map/cast/pallas_call | solution.py:956

commit v5 on v4

v5 whole, which is shorter than its diff:
```python
import functools

import jax
import jax.numpy as jnp
from jax import lax
from jax.experimental import pallas as pl
from jax.experimental.pallas import tpu as pltpu
from jax.sharding import PartitionSpec as P

MESH = pl.DeviceIdType.MESH
BF16, F32, I32 = jnp.bfloat16, jnp.float32, jnp.int32
DMA = pltpu.SemaphoreType.DMA
NODE = 128
SPLIT = 4
CORES = 2
CHUNKS = 4
FINE = (4, 4, 4, 4)
WIDE = 4
BACK = 4
RING = 96


class Plan:
    def __init__(self, mesh, feat, slots):
        rows, cols = mesh.shape["row"], mesh.shape["col"]
        self.rows, self.cols, self.feat, self.slots = rows, cols, feat, slots
        self.nz, self.ny, self.nx = SPLIT, rows // SPLIT, cols // CORES
        self.slice = feat // self.nz
        self.width = self.slice // CHUNKS
        sizes = [self.slice // share for share in FINE]
        self.fine = [(sum(sizes[:i]), size) for i, size in enumerate(sizes)]
        self.columns = rows * NODE
        self.block = cols * NODE
        self.line = self.nz * self.block
        self.half = self.line // CORES
        self.third = self.half // self.nx
        self.fa, self.fp = feat // self.nx, feat // self.ny
        self.wide = min(WIDE, self.fp // NODE)
        self.fh, self.fw = self.fa // CORES, self.fp // self.wide
        self.fz = self.fh // self.nz
        self.group = self.nz * NODE
        self.wb = self.slice // BACK
        self.depth = self.ny * self.nx * NODE
        self.merged = self.columns * self.line <= 1 << 22

    def place(self):
        row, col = lax.axis_index("row"), lax.axis_index("col")
        return row // self.ny, lax.rem(row, self.ny), col // CORES, lax.rem(col, CORES)

    def device(self, z, y, x, k):
        return (z * self.ny + y, x * CORES + k)


class Refs:
    def __init__(self, names, refs):
        self.__dict__.update(zip(names, refs, strict=True))


def guarded(when, act):
    if when is None:
        act()
    else:
        pl.when(when)(act)


class Sends:
    def __init__(self, sems):
        self.sems, self.started, self.settled = sems, [], 0

    def __call__(self, src, dst, recv, device, when=None):
        self.settle(RING - 1)
        copy = pltpu.make_async_remote_copy(
            src_ref=src,
            dst_ref=dst,
            send_sem=self.sems.at[len(self.started) % RING],
            recv_sem=recv,
            device_id=device,
            device_id_type=MESH,
        )
        guarded(when, copy.start)
        self.started.append((copy, when))

    def settle(self, keep):
        while len(self.started) - self.settled > keep:
            copy, when = self.started[self.settled]
            guarded(when, copy.wait_send)
            self.settled += 1


def others(index, count):
    return [lax.rem(index + step, count) for step in range(1, count)]


def seen(i, count):
    return count - 2 - i


def at(start, size):
    return pl.ds(pl.multiple_of(start, size), size)


def span(start, size):
    return pl.ds(pl.multiple_of(start, 16), size)


def loop(count, step):
    if count <= 4:
        for i in range(count):
            step(i)
    else:

        def body(i, carry):
            step(i)
            return carry

        lax.fori_loop(0, count, body, 0)


def greet(devices):
    barrier = pltpu.get_barrier_semaphore()
    for device in devices:
        pl.semaphore_signal(barrier, inc=1, device_id=device, device_id_type=MESH)
    return lambda: pl.semaphore_wait(barrier, len(devices))


class Step:
    def __init__(self, plan, refs):
        self.plan, self.r = plan, refs
        self.z, self.y, self.x, self.k = z, y, x, k = plan.place()
        self.zs, self.ys, self.xs = others(z, plan.nz), others(y, plan.ny), others(x, plan.nx)
        self.here, self.twin = plan.device(z, y, x, k), plan.device(z, y, x, 1 - k)
        self.to_z = [plan.device(a, y, x, k) for a in self.zs]
        self.to_y = [plan.device(z, b, x, k) for b in self.ys]
        self.to_x = [plan.device(z, y, a, k) for a in self.xs]
        self.to_far = [plan.device(z, y, a, 1 - k) for a in self.xs]
        self.send = Sends(refs.sems)

    def arrived(self, ref, sem):
        pltpu.make_async_remote_copy(
            src_ref=ref, dst_ref=ref, send_sem=sem, recv_sem=sem, device_id=self.here, device_id_type=MESH
        ).wait_recv()

    def weight_copies(self):
        plan, r = self.plan, self.r
        copies = []
        for chunk in range(CHUNKS):
            for a in range(plan.nz):
                i = chunk * plan.nz + a
                copies.append(
                    pltpu.make_async_copy(
                        r.w_hbm.at[pl.ds(a * plan.slice + chunk * plan.width, plan.width)],
                        r.w.at[pl.ds(i * plan.width, plan.width)],
                        r.w_sem.at[chunk],
                    )
                )
        return copies


def of_part(task):
    def run(half, part, *where):
        if part < half.s.plan.wide:
            task(half, part, *where)

    return run


class ForwardHalf:
    def __init__(self, s):
        self.s = s
        plan, r, x, k = s.plan, s.r, s.x, s.k
        self.mates = s.to_x + [s.twin] + s.to_far
        self.mate_cols = [a * CORES + k for a in s.xs] + [x * CORES + 1 - k] + [a * CORES + 1 - k for a in s.xs]
        self.start()

    def block_of(self, a, b):
        return at((b * self.s.plan.nz + a) * NODE, NODE)

    def start(self):
        s = self.s
        plan, r, send, z, y, x, k = s.plan, s.r, s.send, s.z, s.y, s.x, s.k
        fs = plan.slice
        col, mine = x * CORES + k, self.block_of(z, y)
        for device in s.to_z:
            send(r.codes, r.line_codes.at[z], r.codes_sem.at[z], device)
        for chunk, (start, size) in enumerate(plan.fine):
            rows = pl.ds(start, size)
            for a, device in zip(s.zs, s.to_z):
                source = r.x_t.at[span(a * fs + start, size)]
                send(source, r.gathered.at[rows, mine], r.slice_sem.at[chunk, z], device)
            for i, device in enumerate(s.to_y):
                source = r.x_t.at[span(z * fs + start, size)]
                send(source, r.gathered.at[rows, mine], r.line_sem.at[chunk, seen(i, plan.ny)], device)
        for device, c in zip(self.mates, self.mate_cols):
            send(r.count.at[c], r.degrees.at[col], r.degree_sem, device)
        r.gathered[:, mine] = r.x_t[at(z * fs, fs), :]
        r.degrees[col] = r.count[col]

    def build(self, i):
        s = self.s
        plan, r, nz, ny = s.plan, s.r, s.plan.nz, s.plan.ny
        a = ([s.z] + s.zs)[i]
        source = r.codes if i == 0 else r.line_codes.at[a]
        if i > 0:
            s.arrived(source, r.codes_sem.at[a])
        groups, strip = (plan.rows + 3) // 4, 32
        for c in range(plan.cols):
            columns = at((((c % CORES) * plan.nx + c // CORES) * nz + a) * NODE, NODE)
            part = source[:, c * NODE : (c + 1) * NODE]
            low = jnp.where(part >= 0, part % NODE, -1)
            high = jnp.where(part >= 0, part // NODE, -1)
            adds = [
                sum(jnp.where(high == 4 * g + j, 1 << (8 * j), 0) for j in range(4) if 4 * g + j < plan.rows)
                for g in range(groups)
            ]
            for start in range(0, NODE, strip):
                lanes = lax.broadcasted_iota(I32, (strip, NODE), 0) + start
                packed = [jnp.zeros((strip, NODE), I32) for _ in range(groups)]
                for slot in range(plan.slots):
                    hit = low[slot : slot + 1, :] == lanes
                    packed = [p + jnp.where(hit, v[slot : slot + 1, :], 0) for p, v in zip(packed, adds)]
                for row in range(plan.rows):
                    start_row = ((row % ny) * nz + row // ny) * NODE + start
                    number = (packed[row // 4] >> (8 * (row % 4))) & 255
                    r.adj[start_row : start_row + strip, columns] = number.astype(F32).astype(BF16)

    def pass_on(self, chunk, i):
        s, r, a = self.s, self.s.r, self.s.zs[i]
        piece = r.gathered.at[pl.ds(*s.plan.fine[chunk]), self.block_of(a, s.y)]
        s.arrived(piece, r.slice_sem.at[chunk, a])
        for j, device in enumerate(s.to_y):
            s.send(piece, piece, r.line_sem.at[chunk, seen(j, s.plan.ny)], device)

    def product(self, chunk, columns_from, store):
        r, plan, tile = self.s.r, self.s.plan, 256
        rows = pl.ds(*plan.fine[chunk])

        def step(i):
            columns = r.adj[:, at(columns_from + i * tile, tile)]
            store(at(i * tile, tile), jnp.dot(r.gathered[rows, :], columns, preferred_element_type=F32))

        loop(plan.half // tile, step)

    def first(self, chunk):
        s, r, plan = self.s, self.s.r, self.s.plan
        rows = pl.ds(*plan.fine[chunk])
        for i in range(plan.ny - 1):
            s.arrived(r.gathered.at[rows, pl.ds(0, plan.group)], r.line_sem.at[chunk, i])

        def to_half(cols, value):
            r.half_send[rows, cols] = value.astype(BF16)

        self.product(chunk, (1 - s.k) * plan.half, to_half)
        s.send(r.half_send.at[rows], r.half_recv.at[rows], r.half_sem.at[chunk], s.twin)

    def own(self, chunk):
        r, rows = self.s.r, pl.ds(*self.s.plan.fine[chunk])

        def to_own(cols, value):
            r.own[rows, cols] = value

        self.product(chunk, self.s.k * self.s.plan.half, to_own)

    def second(self, chunk):
        s, r, third = self.s, self.s.r, self.s.plan.third
        rows = pl.ds(*s.plan.fine[chunk])
        s.arrived(r.half_recv.at[rows], r.half_sem.at[chunk])
        for i, (a, device) in enumerate(zip(s.xs, s.to_x)):
            cols, there = at(a * third, third), seen(i, s.plan.nx)
            r.x_send[rows, cols] = (r.own[rows, cols] + r.half_recv[rows, cols].astype(F32)).astype(BF16)
            s.send(r.x_send.at[rows, cols], r.x_recv.at[there, rows], r.third_sem.at[chunk, there], device)

    def last(self, chunk):
        s, r, plan = self.s, self.s.r, self.s.plan
        start, size = plan.fine[chunk]
        rows, cols = pl.ds(start, size), at(s.x * plan.third, plan.third)
        value = r.own[rows, cols] + r.half_recv[rows, cols].astype(F32)
        for i in range(plan.nx - 1):
            s.arrived(r.x_recv.at[i, rows], r.third_sem.at[chunk, i])
            value = value + r.x_recv[i, rows].astype(F32)
        r.total[rows] = value.astype(BF16)
        there = span(s.z * plan.slice + start, size)
        for a, device in zip(s.zs, s.to_z):
            s.send(r.total.at[rows, at(a * NODE, NODE)], r.summed.at[there], r.back_sem.at[chunk], device)
        r.summed[there, :] = r.total[rows, at(s.z * NODE, NODE)]

    def scale(self):
        s, r = self.s, self.s.r
        s.arrived(r.degrees.at[pl.ds(0, s.plan.cols - 1)], r.degree_sem)
        degree = r.degrees[0]
        for c in range(1, s.plan.cols):
            degree = degree + r.degrees[c]
        self.row = 1.0 / (degree[0:1, :] + 1.0)
        self.column = jnp.broadcast_to(self.row, (NODE, NODE)).T[:, 0:1]

    def combine(self, chunk):
        s, r, plan = self.s, self.s.r, self.s.plan
        nz, fs, width = plan.nz, plan.slice, plan.width
        start, size = plan.fine[chunk]
        s.arrived(r.summed.at[pl.ds(0, (nz - 1) * size)], r.back_sem.at[chunk])
        for a in range(nz):
            rows = pl.ds(a * fs + start, size)
            value = self.row * (r.summed[rows, :].astype(F32) + 2.0 * r.x_t[rows, :].astype(F32))
            r.agg[rows, :] = value.astype(BF16)
        end = start + size
        for begin in range(end // width * width - (width if end % width == 0 else 0), end - width + 1, width):
            for a in range(nz):
                place = begin * nz + a * width
                r.agg_rows[:, place : place + width] = r.agg[a * fs + begin : a * fs + begin + width, :].T

    def await_weight(self, chunk):
        r = self.s.r
        rows = r.w.at[pl.ds(chunk * self.s.plan.slice, self.s.plan.slice)]
        pltpu.make_async_copy(rows, rows, r.w_sem.at[chunk]).wait()

    def part_of(self, chunk, cols):
        r = self.s.r
        rows = pl.ds(chunk * self.s.plan.slice, self.s.plan.slice)
        return jnp.dot(r.agg_rows[:, rows], r.w[rows, cols], preferred_element_type=F32)

    def add(self, chunk):
        r = self.s.r
        self.await_weight(chunk)

        def step(i):
            cols = at(i * 512, 512)
            if chunk == 0:
                r.preact[:, cols] = self.part_of(chunk, cols)
            else:
                r.preact[:, cols] += self.part_of(chunk, cols)

        loop(self.s.plan.feat // 512, step)

    @of_part
    def layer(self, part):
        plan = self.s.plan
        if part == 0:
            self.await_weight(CHUNKS - 1)
            self.s.r.cot_copy.wait()
        loop(plan.ny, lambda b: self.layer_columns(at(b * plan.fp + part * plan.fw, plan.fw)))

    def layer_columns(self, cols):
        r = self.s.r
        pre = r.preact[:, cols] + self.part_of(CHUNKS - 1, cols) + r.bias[:, cols]
        square = pre * pre
        slope = 0.7978845608028654
        t = jnp.tanh(slope * pre * (1.0 + 0.044715 * square))
        r.act[:, cols] = (0.5 * pre * (1.0 + t)).astype(BF16)
        grad = 0.5 * (1.0 + t) + 0.5 * pre * (1.0 - t * t) * (slope * (1.0 + 3.0 * 0.044715 * square))
        low = (r.cot[:, cols].astype(F32) * grad).astype(BF16)
        r.pg[:, cols] = low
        wide = low.astype(F32)
        r.scaled[:, cols] = (self.column * wide).astype(BF16)
        r.bias_sum[:, cols] = jnp.sum(wide, axis=0, keepdims=True)


class BackwardHalf:
    def __init__(self, s):
        self.s = s
        plan = s.plan
        self.pair = s.z + 1 - 2 * lax.rem(s.z, 2)
        self.other = plan.nz - 1 - s.z
        self.middle = lax.rem(s.z, 3) > 0
        self.end = lax.rem(s.z, 3) == 0
        self.tile = min(256, plan.fh)
        self.copies = {}

    def nodes(self, b, a):
        return at((b * self.s.plan.nx + a) * NODE, NODE)

    def line_rows(self, c, a):
        return at((c * self.s.plan.nx + a) * self.s.plan.group, self.s.plan.group)

    def wide_cols(self, b, part):
        return at(b * self.s.plan.fp + part * self.s.plan.fw, self.s.plan.fw)

    def agg_blocks(self, chunk, part):
        plan = self.s.plan
        begin, size = plan.fine[chunk]
        for i in range(plan.nz // plan.nx):
            start = i * plan.slice + begin
            yield span(part * plan.fa + start, size), pl.ds(start, size)

    def agg_send(self, chunk):
        s, r = self.s, self.s.r
        mine = self.nodes(s.y, s.x)
        for j, (a, device) in enumerate(zip(s.xs, s.to_x)):
            for source, rows in self.agg_blocks(chunk, a):
                s.send(r.agg.at[source], r.agg_all.at[rows, mine], r.agg_x_sem.at[chunk, seen(j, s.plan.nx)], device)
        for source, rows in self.agg_blocks(chunk, s.x):
            for j, device in enumerate(s.to_y):
                s.send(r.agg.at[source], r.agg_all.at[rows, mine], r.agg_y_sem.at[seen(j, s.plan.ny)], device)
            r.agg_all[rows, mine] = r.agg[source, :]

    @of_part
    def pg_x(self, part):
        s, r, fw = self.s, self.s.r, self.s.plan.fw
        mine, cols = self.nodes(s.y, s.x), pl.ds(part * fw, fw)
        for j, device in enumerate(s.to_x):
            source = r.pg.at[:, self.wide_cols(s.y, part)]
            s.send(source, r.pg_all.at[mine, cols], r.pg_x_sem.at[part, seen(j, s.plan.nx)], device)
        r.pg_all[mine, cols] = r.pg[:, self.wide_cols(s.y, part)]

    @of_part
    def pg_y(self, part):
        s, r, fw = self.s, self.s.r, self.s.plan.fw
        mine, cols = self.nodes(s.y, s.x), pl.ds(part * fw, fw)
        for j, (b, device) in enumerate(zip(s.ys, s.to_y)):
            source = r.pg.at[:, self.wide_cols(b, part)]
            s.send(source, r.pg_all.at[mine, cols], r.pg_y_sem.at[part, seen(j, s.plan.ny)], device)

    def pass_agg(self, chunk):
        s, r, plan = self.s, self.s.r, self.s.plan
        size = plan.fine[chunk][1] * (plan.nz // plan.nx)
        for i, a in enumerate(s.xs):
            s.arrived(r.agg_all.at[pl.ds(0, size), self.nodes(s.y, a)], r.agg_x_sem.at[chunk, i])
            for _, rows in self.agg_blocks(chunk, s.x):
                ref = r.agg_all.at[rows, self.nodes(s.y, a)]
                for j, device in enumerate(s.to_y):
                    s.send(ref, ref, r.agg_y_sem.at[seen(j, plan.ny)], device)

    @of_part
    def pass_pg(self, part):
        s, r, plan = self.s, self.s.r, self.s.plan
        for i, b in enumerate(s.ys):
            ref = r.pg_all.at[self.nodes(b, s.x), pl.ds(part * plan.fw, plan.fw)]
            s.arrived(ref, r.pg_y_sem.at[part, i])
            for j, device in enumerate(s.to_x):
                s.send(ref, ref, r.pg_x_sem.at[part, seen(j, plan.nx)], device)

    def await_agg(self):
        s, r = self.s, self.s.r
        for i in range(s.plan.ny - 1):
            s.arrived(r.agg_all.at[:, pl.ds(0, s.plan.nx * NODE)], r.agg_y_sem.at[i])

    def tile_product(self, part, rows_from, store):
        r, plan, tile = self.s.r, self.s.plan, self.tile
        cols = pl.ds(part * plan.fw, plan.fw)

        def step(i):
            rows = r.agg_all[at(rows_from + i * tile, tile), :]
            store(at(i * tile, tile), jnp.dot(rows, r.pg_all[:, cols], preferred_element_type=F32))

        loop(plan.fh // tile, step)

    @of_part
    def tile_part(self, part):
        s, r, plan = self.s, self.s.r, self.s.plan
        for i in range(plan.nx - 1):
            s.arrived(r.pg_all.at[pl.ds(0, plan.ny * NODE), pl.ds(part * plan.fw, plan.fw)], r.pg_x_sem.at[part, i])

        def to_half(rows, value):
            r.tile_send[part, rows, :] = value.astype(BF16)

        self.tile_product(part, (1 - s.k) * plan.fh, to_half)
        s.send(r.tile_send.at[part], r.tile_recv.at[part], r.tile_sem.at[part], s.twin)

    @of_part
    def tile_own(self, part):
        r = self.s.r

        def to_own(rows, value):
            r.tile[part, rows, :] = value

        self.tile_product(part, self.s.k * self.s.plan.fh, to_own)

    def own_part(self, part, a):
        r, fz = self.s.r, self.s.plan.fz
        rows = at(a * fz, fz)
        return r.tile[part, rows, :] + r.tile_recv[part, rows, :].astype(F32)

    @of_part
    def sum_start(self, part):
        s, r = self.s, self.s.r
        s.arrived(r.tile_recv.at[part], r.tile_sem.at[part])
        pair, other = self.pair, self.other
        targets = [other, s.plan.nz - 1 - pair, pair]

        @pl.when(self.end)
        def _():
            for i, a in enumerate(targets):
                r.sum_send[part, i] = self.own_part(part, a).astype(BF16)

        for i in range(3):
            s.send(
                r.sum_send.at[part, i], r.sum_recv.at[part, i], r.sum_sem.at[part, i],
                s.plan.device(pair, s.y, s.x, s.k), self.end,
            )

    def sum_step(self, part, i, into, slot, a, to):
        s, r = self.s, self.s.r

        @pl.when(self.middle)
        def _():
            s.arrived(r.sum_recv.at[part, i], r.sum_sem.at[part, i])
            r.sum_send[part, slot] = (self.own_part(part, a) + r.sum_recv[part, i].astype(F32)).astype(BF16)

        s.send(
            r.sum_send.at[part, slot], r.sum_recv.at[part, into], r.sum_sem.at[part, into],
            s.plan.device(to, s.y, s.x, s.k), self.middle,
        )

    @of_part
    def sum_far(self, part):
        self.sum_step(part, 0, 3, 0, self.s.plan.nz - 1 - self.pair, self.other)

    @of_part
    def sum_other(self, part):
        self.sum_step(part, 1, 4, 1, self.other, self.other)

    @of_part
    def sum_out(self, part):
        self.sum_step(part, 3, 0, 2, self.pair, self.pair)

    @of_part
    def sum_end(self, part):
        s, r = self.s, self.s.r
        mine = self.own_part(part, s.z)

        @pl.when(self.middle)
        def _():
            s.arrived(r.sum_recv.at[part, 2], r.sum_sem.at[part, 2])
            s.arrived(r.sum_recv.at[part, 4], r.sum_sem.at[part, 4])
            r.final[part] = (mine + r.sum_recv[part, 2].astype(F32) + r.sum_recv[part, 4].astype(F32)).astype(BF16)

        @pl.when(self.end)
        def _():
            s.arrived(r.sum_recv.at[part, 0], r.sum_sem.at[part, 0])
            r.final[part] = (mine + r.sum_recv[part, 0].astype(F32)).astype(BF16)

        copy = pltpu.make_async_copy(r.final.at[part], self.piece(part, s.z, s.y, s.x), r.local_sem.at[part])
        copy.start()
        self.copies[part] = copy
        self.spread(r.final.at[part], part, s.z)
        self.along(r.final.at[part], part, s.z, self.pair, None)
        self.along(r.final.at[part], part, s.z, self.other, self.middle)

    def block(self, part, a_y, a_x):
        plan = self.s.plan
        return self.s.r.low.at[at(a_x * plan.fa + self.s.k * plan.fh, plan.fh), self.wide_cols(a_y, part)]

    def piece(self, part, a_z, a_y, a_x):
        plan = self.s.plan
        rows = at(a_x * plan.fa + self.s.k * plan.fh + a_z * plan.fz, plan.fz)
        return self.s.r.low.at[rows, self.wide_cols(a_y, part)]

    def along(self, source, part, a_z, to, when):
        s = self.s
        device = s.plan.device(to, s.y, s.x, s.k)
        s.send(source, self.piece(part, a_z, s.y, s.x), s.r.gather_z_sem.at[part, a_z], device, when)

    def spread(self, source, part, a_z):
        s, r = self.s, self.s.r
        target = self.piece(part, a_z, s.y, s.x)
        for i, device in enumerate(s.to_x):
            s.send(source, target, r.gather_x_sem.at[part, a_z, seen(i, s.plan.nx)], device)
        for i, device in enumerate(s.to_y):
            s.send(source, target, r.gather_y_sem.at[part, a_z, seen(i, s.plan.ny)], device)

    def line_order(self):
        return [self.s.z, self.pair, 2 - self.s.z // 2, 3 - 3 * (self.s.z // 2)]

    @of_part
    def gather_line(self, part, i):
        s = self.s
        a_z = self.line_order()[i]
        piece = self.piece(part, a_z, s.y, s.x)
        s.arrived(piece, s.r.gather_z_sem.at[part, a_z])
        self.along(piece, part, a_z, self.other if i == 1 else self.pair, self.middle)
        self.spread(piece, part, a_z)

    @of_part
    def gather_x(self, part, i):
        s, r, plan = self.s, self.s.r, self.s.plan
        a_z = self.line_order()[i]
        for j, a_x in enumerate(s.xs):
            piece = self.piece(part, a_z, s.y, a_x)
            s.arrived(piece, r.gather_x_sem.at[part, a_z, j])
            for m, device in enumerate(s.to_y):
                s.send(piece, piece, r.corner_sem.at[part, seen(m, plan.ny), j], device, lax.rem(a_z, 2) == 0)

    @of_part
    def gather_y(self, part, i):
        s, r, plan = self.s, self.s.r, self.s.plan
        a_z = self.line_order()[i]
        for j, a_y in enumerate(s.ys):
            piece = self.piece(part, a_z, a_y, s.x)
            s.arrived(piece, r.gather_y_sem.at[part, a_z, j])
            for m, device in enumerate(s.to_x):
                s.send(piece, piece, r.corner_sem.at[part, j, seen(m, plan.nx)], device, lax.rem(a_z, 2) == 1)

    def to_twin(self, part, a_y, a_x):
        s = self.s
        block = self.block(part, a_y, a_x)
        s.send(block, block, s.r.twin_sem, s.twin)

    @of_part
    def twin_own(self, part):
        self.copies[part].wait()
        self.to_twin(part, self.s.y, self.s.x)

    @of_part
    def twin_x(self, part):
        for a_x in self.s.xs:
            self.to_twin(part, self.s.y, a_x)

    @of_part
    def twin_y(self, part):
        for a_y in self.s.ys:
            self.to_twin(part, a_y, self.s.x)

    @of_part
    def twin_corner(self, part):
        s = self.s
        for j, a_y in enumerate(s.ys):
            for i, a_x in enumerate(s.xs):
                s.arrived(self.block(part, a_y, a_x), s.r.corner_sem.at[part, j, i])
                self.to_twin(part, a_y, a_x)

    def gather_twin(self):
        s, feat = self.s, self.s.plan.feat
        s.send.settle(16)
        s.arrived(s.r.low.at[pl.ds(0, feat // CORES)], s.r.twin_sem)

    def grads_start(self, part):
        s, r, plan = self.s, self.s.r, self.s.plan
        fs, wb = plan.slice, plan.wb
        mine, cols = at(((s.k * plan.nx + s.x) * plan.nz + s.z) * NODE, NODE), pl.ds(part * wb, wb)
        for a, device in zip(s.zs, s.to_z):
            s.send(r.scaled.at[:, at(a * fs + part * wb, wb)], r.grads.at[mine, cols], r.grads_z_sem.at[part], device)
        r.grads[mine, cols] = r.scaled[:, at(s.z * fs + part * wb, wb)]

    def grads_x(self, part):
        s, r, plan = self.s, self.s.r, self.s.plan
        cols = pl.ds(part * plan.wb, plan.wb)
        s.arrived(r.grads.at[pl.ds(0, (plan.nz - 1) * NODE), cols], r.grads_z_sem.at[part])
        ref = r.grads.at[self.line_rows(s.k, s.x), cols]
        for i, device in enumerate(s.to_x):
            s.send(ref, ref, r.grads_x_sem.at[part, seen(i, plan.nx)], device)
        s.send(ref, ref, r.grads_k_sem.at[part], s.twin)

    def grads_twin(self, part):
        s, r, plan = self.s, self.s.r, self.s.plan
        for i, a in enumerate(s.xs):
            ref = r.grads.at[self.line_rows(s.k, a), pl.ds(part * plan.wb, plan.wb)]
            s.arrived(ref, r.grads_x_sem.at[part, i])
            s.send(ref, ref, r.grads_k_sem.at[part], s.twin)

    def target_product(self, part, b, store):
        r, plan = self.s.r, self.s.plan
        cols = pl.ds(part * plan.wb, plan.wb)

        def step(i):
            rows = r.adj[at(b * plan.group + i * 256, 256), :]
            store(at(i * 256, 256), jnp.dot(rows, r.grads[:, cols], preferred_element_type=F32))

        loop(plan.group // 256, step)

    def target(self, part):
        s, r, plan = self.s, self.s.r, self.s.plan
        s.arrived(r.grads.at[pl.ds(0, plan.line // CORES), pl.ds(part * plan.wb, plan.wb)], r.grads_k_sem.at[part])
        for i, (b, device) in enumerate(zip(s.ys, s.to_y)):

            def to_y(rows, value):
                r.y_send[part, i, rows, :] = value.astype(BF16)

            self.target_product(part, b, to_y)
            there = seen(i, plan.ny)
            s.send(r.y_send.at[part, i], r.y_recv.at[part, there], r.y_sem.at[part, there], device)

    def target_own(self, part):
        r = self.s.r

        def to_target(rows, value):
            r.target[part, rows, :] = value

        self.target_product(part, self.s.y, to_target)

    def back(self, part):
        s, r, plan = self.s, self.s.r, self.s.plan
        value = r.target[part]
        for i in range(plan.ny - 1):
            s.arrived(r.y_recv.at[part, i], r.y_sem.at[part, i])
            value = value + r.y_recv[part, i].astype(F32)
        r.back[part] = value.astype(BF16)
        cols = at(s.z * plan.slice + part * plan.wb, plan.wb)
        for a, device in zip(s.zs, s.to_z):
            s.send(r.back.at[part, at(a * NODE, NODE)], r.returned.at[:, cols], r.returned_sem.at[part], device)
        r.returned[:, cols] = r.back[part, at(s.z * NODE, NODE), :]

    def through(self):
        s, r, plan = self.s, self.s.r, self.s.plan
        for part in range(BACK):
            s.arrived(r.returned.at[:, pl.ds(0, (plan.nz - 1) * plan.wb)], r.returned_sem.at[part])
        r.returned[...] = (r.returned[...].astype(F32) + 2.0 * r.scaled[...].astype(F32)).astype(BF16)
        for chunk in range(CHUNKS):
            rows = pl.ds(chunk * plan.slice, plan.slice)
            value = lax.dot_general(
                r.returned[...], r.w[rows, :], (((1,), (1,)), ((), ())), preferred_element_type=F32
            )
            for a in range(plan.nz):
                cols = pl.ds(a * plan.slice + chunk * plan.width, plan.width)
                r.fg[:, cols] = value[:, a * plan.width : (a + 1) * plan.width]

    def bias_start(self):
        s, r = self.s, self.s.r
        s.send(r.bias_sum, r.bias_k.at[s.k], r.total_sem.at[0], s.twin)
        r.bias_k[s.k] = r.bias_sum[...]

    def bias_stage(self, stage):
        s, r, plan = self.s, self.s.r, self.s.plan
        ref, count = ((r.bias_k, CORES), (r.bias_x, plan.nx), (r.bias_y, plan.ny), (r.bias_z, plan.nz))[stage]
        s.arrived(ref.at[pl.ds(0, count - 1)], r.total_sem.at[stage])
        value = ref[0]
        for a in range(1, count):
            value = value + ref[a]
        if stage == 3:
            r.bias_grad[...] = value
            return
        ref, index, devices = ((r.bias_x, s.x, s.to_x), (r.bias_y, s.y, s.to_y), (r.bias_z, s.z, s.to_z))[stage]
        ref[index] = value
        for device in devices:
            s.send(ref.at[index], ref.at[index], r.total_sem.at[stage + 1], device)


class Skip:
    def __getattr__(self, name):
        return lambda *where: None


def schedule(f, b):
    f.build(0)
    f.build(3)
    f.pass_on(0, 2)
    f.pass_on(0, 1)
    f.pass_on(0, 0)
    f.build(2)
    f.pass_on(1, 2)
    f.build(1)
    f.pass_on(1, 0)
    f.pass_on(1, 1)
    f.first(0)
    f.scale()
    f.pass_on(2, 2)
    f.own(0)
    f.pass_on(2, 0)
    f.pass_on(2, 1)
    f.second(0)
    f.first(1)
    f.pass_on(3, 0)
    f.own(1)
    f.pass_on(3, 1)
    f.second(1)
    f.pass_on(3, 2)
    f.first(2)
    f.last(0)
    f.own(2)
    f.second(2)
    f.first(3)
    f.last(1)
    f.own(3)
    f.second(3)
    f.last(2)
    f.combine(0)
    b.agg_send(0)
    f.add(0)
    f.combine(1)
    b.agg_send(1)
    f.last(3)
    f.add(1)
    b.pass_agg(0)
    f.combine(2)
    b.agg_send(2)
    f.add(2)
    f.combine(3)
    b.agg_send(3)
    f.layer(0)
    b.pg_y(0)
    b.pg_x(0)
    f.layer(1)
    b.pg_y(1)
    f.layer(2)
    b.pg_x(2)
    f.layer(3)
    b.bias_start()
    b.pass_agg(2)
    b.grads_start(0)
    b.pass_agg(3)
    b.pass_agg(1)
    b.pg_y(2)
    b.pg_x(1)
    b.grads_start(2)
    b.grads_start(3)
    b.pass_pg(0)
    b.grads_start(1)
    b.pass_pg(1)
    b.grads_x(0)
    b.await_agg()
    b.tile_part(1)
    b.tile_own(1)
    b.grads_x(2)
    b.pg_y(3)
    b.sum_start(1)
    b.grads_twin(0)
    b.pass_pg(2)
    b.tile_part(0)
    b.tile_own(0)
    b.grads_x(3)
    b.pass_pg(3)
    b.sum_start(0)
    b.target(0)
    b.sum_far(1)
    b.pg_x(3)
    b.grads_x(1)
    b.grads_twin(2)
    b.tile_part(2)
    b.sum_other(1)
    b.tile_own(2)
    b.target(2)
    b.sum_out(1)
    b.sum_start(2)
    b.grads_twin(3)
    b.sum_far(0)
    b.target(3)
    b.bias_stage(0)
    b.sum_other(0)
    b.target_own(0)
    b.sum_out(0)
    b.sum_far(2)
    b.sum_end(1)
    b.tile_part(3)
    b.tile_own(3)
    b.grads_twin(1)
    b.sum_other(2)
    b.bias_stage(1)
    b.sum_end(0)
    b.sum_start(3)
    b.sum_out(2)
    b.target(1)
    b.gather_line(1, 1)
    b.gather_line(1, 2)
    b.sum_end(2)
    b.target_own(2)
    b.gather_x(0, 0)
    b.gather_line(0, 2)
    b.sum_far(3)
    b.sum_other(3)
    b.gather_line(1, 3)
    b.gather_line(0, 1)
    b.gather_line(2, 2)
    b.sum_out(3)
    b.gather_y(1, 2)
    b.gather_line(2, 1)
    b.sum_end(3)
    b.gather_x(1, 3)
    b.gather_line(0, 3)
    b.gather_y(1, 0)
    b.gather_line(2, 3)
    b.gather_y(0, 0)
    b.back(0)
    b.gather_line(3, 2)
    b.gather_x(1, 0)
    b.gather_line(3, 1)
    b.gather_x(1, 2)
    b.gather_y(1, 1)
    b.target_own(1)
    b.gather_x(1, 1)
    b.gather_x(0, 3)
    b.gather_y(1, 3)
    b.bias_stage(2)
    b.back(2)
    b.back(1)
    b.gather_y(2, 1)
    b.gather_y(0, 1)
    b.gather_y(0, 2)
    b.target_own(3)
    b.gather_line(3, 3)
    b.gather_y(3, 0)
    b.gather_x(0, 1)
    b.twin_own(2)
    b.gather_x(2, 2)
    b.twin_own(1)
    b.twin_own(3)
    b.gather_x(2, 0)
    b.gather_y(0, 3)
    b.gather_x(0, 2)
    b.gather_x(2, 3)
    b.back(3)
    b.gather_x(2, 1)
    b.gather_y(2, 0)
    b.twin_x(0)
    b.gather_x(3, 2)
    b.gather_x(3, 0)
    b.twin_x(1)
    b.gather_y(2, 3)
    b.gather_y(2, 2)
    b.twin_y(0)
    b.gather_y(3, 2)
    b.gather_y(3, 3)
    b.twin_corner(1)
    b.gather_x(3, 3)
    b.twin_y(1)
    b.twin_y(2)
    b.twin_x(2)
    b.gather_y(3, 1)
    b.twin_y(3)
    b.gather_x(3, 1)
    b.through()
    b.twin_x(3)
    b.twin_corner(0)
    b.twin_corner(2)
    b.twin_own(0)
    b.twin_corner(3)
    b.bias_stage(3)
    b.gather_twin()


def fetch(s, names):
    copies = [pltpu.make_async_copy(getattr(s.r, name + "_far"), getattr(s.r, name), getattr(s.r, name + "_sem")) for name in names]
    for copy in copies:
        copy.start()
    return copies


def prepare(s):
    plan, r = s.plan, s.r
    for c in range(plan.cols):
        cols = pl.ds(c * NODE, NODE)
        part = jnp.where(r.mask[:, cols] > 0, r.lists[:, cols], -1)
        r.codes[:, cols] = part
        ones = jnp.sum(jnp.where(part >= 0, 1.0, 0.0), axis=0, keepdims=True)
        r.count[c] = jnp.broadcast_to(ones, (8, NODE))
    for start in range(0, plan.feat, NODE):
        r.x_t[start : start + NODE, :] = r.x[:, start : start + NODE].T


def opening(s):
    met = greet(s.to_z + s.to_y + s.to_x + [s.twin] + s.to_far)
    lists, mask, x, bias, s.r.cot_copy = fetch(s, ("lists", "mask", "x", "bias", "cot"))
    for copy in s.weight_copies():
        copy.start()
    for copy in (lists, mask, x, bias):
        copy.wait()
    prepare(s)
    met()


def whole_kernel(plan, names, *refs):
    s = Step(plan, Refs(names, refs))
    opening(s)
    schedule(ForwardHalf(s), BackwardHalf(s))
    s.send.settle(0)


def forward_kernel(plan, names, *refs):
    s = Step(plan, Refs(names, refs))
    opening(s)
    schedule(ForwardHalf(s), Skip())
    s.send.settle(0)


def backward_kernel(plan, names, *refs):
    s = Step(plan, Refs(names, refs))
    for copy in s.weight_copies():
        copy.start()
    greet(s.to_z + s.to_y + s.to_x + [s.twin])()
    half = BackwardHalf(s)
    for chunk in range(CHUNKS):
        rows = s.r.w.at[pl.ds(chunk * plan.slice, plan.slice)]
        pltpu.make_async_copy(rows, rows, s.r.w_sem.at[chunk]).wait()
    schedule(Skip(), half)
    s.send.settle(0)


def cast_kernel(low, act_in, fg_in, bias_in, out, act_out, fg_out, bias_out, wide, sems):
    copies = [
        pltpu.make_async_copy(src, dst, sems.at[i])
        for i, (src, dst) in enumerate(((act_in, act_out), (fg_in, fg_out), (bias_in, bias_out)))
    ]
    for copy in copies:
        copy.start()
    count, rows, _ = wide.shape
    for i in range(count):
        wide[i] = low[i * rows : (i + 1) * rows, :].astype(F32)
        copy = pltpu.make_async_copy(wide.at[i], out.at[pl.ds(i * rows, rows)], sems.at[3 + i])
        copy.start()
        copies.append(copy)
    for copy in copies:
        copy.wait()


def shaped(*items):
    return jax.ShapeDtypeStruct(*items)


def forward_scratch(plan):
    c, nz, fs = len(FINE), plan.nz, plan.slice
    v = pltpu.VMEM
    return dict(
        x=v((NODE, plan.feat), BF16),
        x_sem=DMA(()),
        lists=v((plan.slots, plan.block), I32),
        lists_sem=DMA(()),
        mask=v((plan.slots, plan.block), I32),
        mask_sem=DMA(()),
        bias=v((1, plan.feat), F32),
        bias_sem=DMA(()),
        cot=v((NODE, plan.feat), BF16),
        codes=v((plan.slots, plan.block), I32),
        x_t=v((plan.feat, NODE), BF16),
        gathered=v((plan.slice, plan.columns), BF16),
        line_codes=v((nz, plan.slots, plan.block), I32),
        count=v((plan.cols, 8, NODE), F32),
        degrees=v((plan.cols, 8, NODE), F32),
        half_send=v((fs, plan.half), BF16),
        half_recv=v((fs, plan.half), BF16),
        x_send=v((fs, plan.half), BF16),
        x_recv=v((plan.nx - 1, fs, plan.third), BF16),
        own=v((fs, plan.half), F32),
        total=v((fs, plan.third), BF16),
        summed=v((plan.feat, NODE), BF16),
        agg_rows=v((NODE, plan.feat), BF16),
        preact=v((NODE, plan.feat), F32),
        cot_sem=DMA(()),
        codes_sem=DMA((nz,)),
        degree_sem=DMA(()),
        slice_sem=DMA((c, nz)),
        line_sem=DMA((c, plan.ny - 1)),
        half_sem=DMA((c,)),
        third_sem=DMA((c, plan.nx - 1)),
        back_sem=DMA((c,)),
    )


def backward_scratch(plan):
    nz, ny, nx, w = plan.nz, plan.ny, plan.nx, plan.wide
    v = pltpu.VMEM
    return dict(
        agg_all=v((plan.fa, plan.depth), BF16),
        pg_all=v((plan.depth, plan.fp), BF16),
        grads=v((plan.line, plan.slice), BF16),
        tile_send=v((w, plan.fh, plan.fw), BF16),
        tile_recv=v((w, plan.fh, plan.fw), BF16),
        tile=v((w, plan.fh, plan.fw), F32),
        sum_send=v((w, 3, plan.fz, plan.fw), BF16),
        sum_recv=v((w, 5, plan.fz, plan.fw), BF16),
        final=v((w, plan.fz, plan.fw), BF16),
        y_send=v((BACK, ny - 1, plan.group, plan.wb), BF16),
        y_recv=v((BACK, ny - 1, plan.group, plan.wb), BF16),
        target=v((BACK, plan.group, plan.wb), F32),
        back=v((BACK, plan.group, plan.wb), BF16),
        returned=v((NODE, plan.feat), BF16),
        bias_k=v((CORES, 1, plan.feat), F32),
        bias_x=v((nx, 1, plan.feat), F32),
        bias_y=v((ny, 1, plan.feat), F32),
        bias_z=v((nz, 1, plan.feat), F32),
        local_sem=DMA((w,)),
        agg_x_sem=DMA((len(FINE), nx - 1)),
        agg_y_sem=DMA((ny - 1,)),
        pg_y_sem=DMA((w, ny - 1)),
        pg_x_sem=DMA((w, nx - 1)),
        grads_z_sem=DMA((BACK,)),
        grads_x_sem=DMA((BACK, nx - 1)),
        grads_k_sem=DMA((BACK,)),
        tile_sem=DMA((w,)),
        sum_sem=DMA((w, 5)),
        gather_z_sem=DMA((w, nz)),
        gather_x_sem=DMA((w, nz, nx - 1)),
        gather_y_sem=DMA((w, nz, ny - 1)),
        corner_sem=DMA((w, ny - 1, nx - 1)),
        twin_sem=DMA(()),
        y_sem=DMA((BACK, ny - 1)),
        returned_sem=DMA((BACK,)),
        total_sem=DMA((4,)),
    )


def call(body, plan, name, identity, inputs, outputs, scratch, vmem=127 << 19):
    scratch = dict(scratch, w=pltpu.VMEM((plan.feat, plan.feat), BF16), w_sem=DMA((CHUNKS,)), sems=DMA((RING,)))
    names = list(inputs) + list(outputs) + list(scratch)
    return pl.pallas_call(
        functools.partial(body, plan, names),
        name=name,
        out_shape=[pltpu.VMEM(shape, kind) if plan.merged else shaped(shape, kind) for shape, kind, _ in outputs.values()],
        in_specs=[pl.BlockSpec(memory_space=space) for _, space in inputs.values()],
        out_specs=[pl.BlockSpec(memory_space=space) for _, _, space in outputs.values()],
        scratch_shapes=list(scratch.values()),
        compiler_params=pltpu.CompilerParams(
            collective_id=identity, has_side_effects=True, vmem_limit_bytes=vmem
        ),
    )(*[array for array, _ in inputs.values()])


def on_device(plan, features, neighbours, edge_mask, weight, bias, cotangent):
    feat, v, far = plan.feat, pltpu.VMEM, pl.ANY
    arguments = dict(
        x_far=(features, far),
        lists_far=(neighbours.T, far),
        mask_far=(edge_mask.T, far),
        w_hbm=(weight, far),
        bias_far=(bias.reshape(1, -1), far),
        cot_far=(cotangent, far),
    )
    between = dict(
        pg=((NODE, feat), BF16),
        scaled=((NODE, feat), BF16),
        agg=((feat, NODE), BF16),
        adj=((plan.columns, plan.line), BF16),
        bias_sum=((1, feat), F32),
    )
    act = dict(act=((NODE, feat), BF16, v))
    results = dict(fg=((NODE, feat), F32, v), low=((feat, feat), BF16, far), bias_grad=((1, feat), F32, v))
    if plan.merged:
        scratch = dict(forward_scratch(plan), **backward_scratch(plan))
        scratch.update({name: v(*item) for name, item in between.items()})
        activations, feature_grad, low, bias_grad = call(
            whole_kernel, plan, "layer", 0, arguments, dict(act, **results), scratch,
            46 << 20,
        )
    else:
        activations, *kept = call(
            forward_kernel, plan, "forward", 0, arguments,
            dict(act, **{name: item + (v,) for name, item in between.items()}),
            forward_scratch(plan),
        )
        feature_grad, low, bias_grad = call(
            backward_kernel, plan, "backward", 1,
            dict({name: (array, v) for name, array in zip(between, kept)}, w_hbm=(weight, far)),
            results, backward_scratch(plan),
        )
    parts = 8
    vmem, hbm = pl.BlockSpec(memory_space=v), pl.BlockSpec(memory_space=far)
    weight_grad, activations, feature_grad, bias_grad = pl.pallas_call(
        cast_kernel,
        name="cast",
        out_shape=[shaped(low.shape, F32)] + [shaped(a.shape, a.dtype) for a in (activations, feature_grad, bias_grad)],
        in_specs=[vmem] * 4,
        out_specs=[hbm] * 4,
        scratch_shapes=[v((parts, feat // parts, feat), F32), DMA((3 + parts,))],
        compiler_params=pltpu.CompilerParams(vmem_limit_bytes=30 << 20),
    )(low, activations, feature_grad, bias_grad)
    return activations, feature_grad, weight_grad, bias_grad.reshape(-1)


def solution(mesh):
    placed = (
        P(("row", "col"), None),
        P("row", "col"),
        P("row", "col"),
        P(),
        P(),
        P(("row", "col"), None),
    )

    def run(*args):
        plan = Plan(mesh, args[0].shape[1], args[1].shape[1] // mesh.shape["col"])
        return jax.shard_map(
            functools.partial(on_device, plan),
            mesh=mesh,
            in_specs=placed,
            out_specs=(P(("row", "col"), None), P(("row", "col"), None), P(), P()),
            check_vma=False,
        )(*args)

    return run
```

time: 132 us -> 118 us (0.89)
  Pallas kernels: 131 us -> 117 us
    pallas_call x1, Pallas kernels: 125 us -> 110 us  [call(): pl.pallas_call(functools.partial(body, plan, names), name=name, out_shape...]
where the time goes in v5:
time: 118 us
  Pallas kernels  117 us (99%)
    pallas_call x1, Pallas kernels, call(): pl.pallas_call(functools.partial(body, plan, names), name=name, out_shape...  110 us
    pallas_call x1, Pallas kernels, on_device(): pl.pallas_call(cast_kernel, name='cast', out_shape=[shaped(low.shape, F32...  6.47 us

profile of v5, /device:TPU:0, one launch (start us, length us, event | category | flops | bytes accessed | tf_op | source)
XLA Modules:
  0.0 117.7 jit_solution(17595158642286377637)
XLA Ops:
  0.6 110.4 %layer.1 = (bf16[128,2048]{1,0:T(8,128)(2,1)S(1)}, f32[128,2048]{1,0:T(8,128)S(1)}, bf16[2048,2048]{1,0:T(8,128)(2,1)S(1)}, f32[1,2048]{1,0:T(1,128)S(1)}) custom-call(bf16[128,2048]{1,0:T(8,128)(2,1)} %refs_0_.1, s32[16,512]{1,0:T(8,128)} %bitcast.4, s32[16,512]{1,0:T(8,128)} %bitcast.5, bf16[2048,2048]{1,0:T(8,128)(2,1)} %refs_3_.1, f32[1,2048]{1,0:T(1,128)} %bitcast.6, ...), custom_call_target="tpu_custom_call" | custom-call | tf_op jit(solution)/shard_map/layer/pallas_call | solution.py:1080
  111.1 6.5 %cast.1 = (f32[2048,2048]{1,0:T(8,128)}, bf16[128,2048]{1,0:T(8,128)(2,1)}, f32[128,2048]{1,0:T(8,128)}, f32[1,2048]{1,0:T(1,128)}) custom-call(bf16[2048,2048]{1,0:T(8,128)(2,1)S(1)} %get-tuple-element.12.low, bf16[128,2048]{1,0:T(8,128)(2,1)S(1)} %get-tuple-element.13.act_in, f32[128,2048]{1,0:T(8,128)S(1)} %get-tuple-element.14.fg_in, ...), custom_call_target="tpu_custom_call" | custom-call | tf_op jit(solution)/shard_map/cast/pallas_call | solution.py:1132

commit v6 on v5

--- a/solution.py
+++ b/solution.py
@@ -17,7 +17,7 @@
 FINE = (4, 4, 4, 4)
 WIDE = 4
 BACK = 4
-RING = 96
+RING = 32
 
 
 class Plan:
@@ -170,30 +170,33 @@
         plan, r, x, k = s.plan, s.r, s.x, s.k
         self.mates = s.to_x + [s.twin] + s.to_far
         self.mate_cols = [a * CORES + k for a in s.xs] + [x * CORES + 1 - k] + [a * CORES + 1 - k for a in s.xs]
-        self.start()
 
     def block_of(self, a, b):
         return at((b * self.s.plan.nz + a) * NODE, NODE)
 
-    def start(self):
-        s = self.s
-        plan, r, send, z, y, x, k = s.plan, s.r, s.send, s.z, s.y, s.x, s.k
-        fs = plan.slice
-        col, mine = x * CORES + k, self.block_of(z, y)
+    def send_codes(self):
+        s, r = self.s, self.s.r
         for device in s.to_z:
-            send(r.codes, r.line_codes.at[z], r.codes_sem.at[z], device)
-        for chunk, (start, size) in enumerate(plan.fine):
-            rows = pl.ds(start, size)
-            for a, device in zip(s.zs, s.to_z):
-                source = r.x_t.at[span(a * fs + start, size)]
-                send(source, r.gathered.at[rows, mine], r.slice_sem.at[chunk, z], device)
-            for i, device in enumerate(s.to_y):
-                source = r.x_t.at[span(z * fs + start, size)]
-                send(source, r.gathered.at[rows, mine], r.line_sem.at[chunk, seen(i, plan.ny)], device)
+            s.send(r.codes, r.line_codes.at[s.z], r.codes_sem.at[s.z], device)
+
+    def send_counts(self):
+        s, r = self.s, self.s.r
+        col = s.x * CORES + s.k
         for device, c in zip(self.mates, self.mate_cols):
-            send(r.count.at[c], r.degrees.at[col], r.degree_sem, device)
-        r.gathered[:, mine] = r.x_t[at(z * fs, fs), :]
+            s.send(r.count.at[c], r.degrees.at[col], r.degree_sem, device)
         r.degrees[col] = r.count[col]
+
+    def send_slices(self, chunk):
+        s, r, plan = self.s, self.s.r, self.s.plan
+        start, size = plan.fine[chunk]
+        rows, mine = pl.ds(start, size), self.block_of(s.z, s.y)
+        for a, device in zip(s.zs, s.to_z):
+            source = r.x_t.at[span(a * plan.slice + start, size)]
+            s.send(source, r.gathered.at[rows, mine], r.slice_sem.at[chunk, s.z], device)
+        own = span(s.z * plan.slice + start, size)
+        for i, device in enumerate(s.to_y):
+            s.send(r.x_t.at[own], r.gathered.at[rows, mine], r.line_sem.at[chunk, seen(i, plan.ny)], device)
+        r.gathered[rows, mine] = r.x_t[own, :]
 
     def build(self, i):
         s = self.s
@@ -728,27 +731,33 @@
 
 
 def schedule(f, b):
+    f.send_slices(0)
+    f.send_counts()
+    f.scale()
+    f.send_codes()
     f.build(0)
-    f.build(3)
+    f.pass_on(0, 0)
+    f.send_slices(1)
+    f.send_slices(2)
     f.pass_on(0, 2)
     f.pass_on(0, 1)
-    f.pass_on(0, 0)
+    f.build(3)
+    f.build(1)
+    f.pass_on(1, 2)
     f.build(2)
-    f.pass_on(1, 2)
-    f.build(1)
+    f.pass_on(1, 1)
     f.pass_on(1, 0)
-    f.pass_on(1, 1)
+    f.send_slices(3)
     f.first(0)
-    f.scale()
     f.pass_on(2, 2)
     f.own(0)
+    f.pass_on(2, 1)
     f.pass_on(2, 0)
-    f.pass_on(2, 1)
     f.second(0)
     f.first(1)
+    f.pass_on(3, 1)
+    f.own(1)
     f.pass_on(3, 0)
-    f.own(1)
-    f.pass_on(3, 1)
     f.second(1)
     f.pass_on(3, 2)
     f.first(2)
@@ -759,8 +768,8 @@
     f.last(1)
     f.own(3)
     f.second(3)
+    f.combine(0)
     f.last(2)
-    f.combine(0)
     b.agg_send(0)
     f.add(0)
     f.combine(1)
@@ -769,148 +778,148 @@
     f.add(1)
     b.pass_agg(0)
     f.combine(2)
+    b.pass_agg(1)
     b.agg_send(2)
     f.add(2)
     f.combine(3)
     b.agg_send(3)
     f.layer(0)
     b.pg_y(0)
+    f.layer(1)
     b.pg_x(0)
-    f.layer(1)
+    f.layer(2)
+    f.layer(3)
+    b.grads_start(3)
+    b.pg_x(2)
     b.pg_y(1)
-    f.layer(2)
-    b.pg_x(2)
-    f.layer(3)
+    b.grads_start(0)
+    b.pass_agg(2)
+    b.grads_start(2)
+    b.pg_x(1)
+    b.pass_agg(3)
+    b.pg_y(2)
+    b.pg_y(3)
+    b.pass_pg(0)
+    b.pass_pg(1)
+    b.grads_x(3)
+    b.grads_start(1)
+    b.await_agg()
+    b.tile_part(0)
+    b.tile_own(0)
+    b.grads_x(0)
     b.bias_start()
-    b.pass_agg(2)
-    b.grads_start(0)
-    b.pass_agg(3)
-    b.pass_agg(1)
-    b.pg_y(2)
-    b.pg_x(1)
-    b.grads_start(2)
-    b.grads_start(3)
-    b.pass_pg(0)
-    b.grads_start(1)
-    b.pass_pg(1)
-    b.grads_x(0)
-    b.await_agg()
+    b.sum_start(0)
     b.tile_part(1)
     b.tile_own(1)
+    b.pass_pg(2)
+    b.grads_twin(3)
+    b.bias_stage(0)
+    b.sum_start(1)
+    b.target(3)
+    b.grads_x(1)
+    b.sum_far(0)
+    b.pass_pg(3)
+    b.pg_x(3)
+    b.grads_twin(0)
+    b.bias_stage(1)
+    b.tile_part(2)
+    b.sum_other(0)
+    b.target(0)
+    b.sum_out(0)
+    b.sum_far(1)
+    b.tile_own(2)
     b.grads_x(2)
-    b.pg_y(3)
-    b.sum_start(1)
-    b.grads_twin(0)
-    b.pass_pg(2)
-    b.tile_part(0)
-    b.tile_own(0)
-    b.grads_x(3)
-    b.pass_pg(3)
-    b.sum_start(0)
-    b.target(0)
-    b.sum_far(1)
-    b.pg_x(3)
-    b.grads_x(1)
+    b.sum_start(2)
+    b.grads_twin(1)
+    b.sum_other(1)
+    b.sum_end(0)
+    b.target(1)
+    b.sum_out(1)
+    b.sum_far(2)
+    b.tile_part(3)
+    b.sum_other(2)
     b.grads_twin(2)
-    b.tile_part(2)
-    b.sum_other(1)
-    b.tile_own(2)
+    b.sum_end(1)
+    b.tile_own(3)
+    b.sum_start(3)
+    b.gather_line(0, 1)
+    b.sum_out(2)
     b.target(2)
-    b.sum_out(1)
-    b.sum_start(2)
-    b.grads_twin(3)
-    b.sum_far(0)
-    b.target(3)
-    b.bias_stage(0)
-    b.sum_other(0)
-    b.target_own(0)
-    b.sum_out(0)
-    b.sum_far(2)
-    b.sum_end(1)
-    b.tile_part(3)
-    b.tile_own(3)
-    b.grads_twin(1)
-    b.sum_other(2)
-    b.bias_stage(1)
-    b.sum_end(0)
-    b.sum_start(3)
-    b.sum_out(2)
-    b.target(1)
+    b.sum_end(2)
+    b.gather_x(1, 0)
     b.gather_line(1, 1)
-    b.gather_line(1, 2)
-    b.sum_end(2)
-    b.target_own(2)
-    b.gather_x(0, 0)
     b.gather_line(0, 2)
     b.sum_far(3)
+    b.gather_line(1, 2)
+    b.gather_x(0, 1)
+    b.gather_line(0, 3)
+    b.gather_y(0, 0)
+    b.gather_line(2, 2)
+    b.target_own(0)
     b.sum_other(3)
+    b.gather_line(2, 1)
+    b.gather_y(2, 0)
+    b.sum_out(3)
+    b.gather_y(0, 1)
+    b.sum_end(3)
+    b.twin_own(0)
+    b.gather_x(1, 1)
+    b.target_own(2)
+    b.gather_line(2, 3)
+    b.gather_x(0, 0)
+    b.gather_y(1, 1)
     b.gather_line(1, 3)
-    b.gather_line(0, 1)
-    b.gather_line(2, 2)
-    b.sum_out(3)
-    b.gather_y(1, 2)
-    b.gather_line(2, 1)
-    b.sum_end(3)
-    b.gather_x(1, 3)
-    b.gather_line(0, 3)
-    b.gather_y(1, 0)
-    b.gather_line(2, 3)
-    b.gather_y(0, 0)
+    b.gather_x(0, 3)
+    b.target_own(3)
+    b.gather_line(3, 2)
+    b.back(3)
+    b.target_own(1)
     b.back(0)
-    b.gather_line(3, 2)
-    b.gather_x(1, 0)
     b.gather_line(3, 1)
-    b.gather_x(1, 2)
-    b.gather_y(1, 1)
-    b.target_own(1)
-    b.gather_x(1, 1)
-    b.gather_x(0, 3)
-    b.gather_y(1, 3)
-    b.bias_stage(2)
-    b.back(2)
     b.back(1)
-    b.gather_y(2, 1)
-    b.gather_y(0, 1)
-    b.gather_y(0, 2)
-    b.target_own(3)
-    b.gather_line(3, 3)
-    b.gather_y(3, 0)
-    b.gather_x(0, 1)
-    b.twin_own(2)
-    b.gather_x(2, 2)
-    b.twin_own(1)
-    b.twin_own(3)
-    b.gather_x(2, 0)
     b.gather_y(0, 3)
     b.gather_x(0, 2)
+    b.gather_line(3, 3)
+    b.gather_x(3, 2)
+    b.gather_x(1, 2)
+    b.back(2)
+    b.gather_y(2, 1)
+    b.gather_y(1, 3)
+    b.gather_x(1, 3)
+    b.gather_y(0, 2)
+    b.gather_y(3, 0)
+    b.gather_x(3, 0)
+    b.gather_x(3, 3)
+    b.twin_own(1)
+    b.gather_y(1, 2)
+    b.gather_y(2, 2)
+    b.gather_x(2, 0)
+    b.gather_y(3, 2)
+    b.twin_corner(0)
+    b.twin_x(0)
+    b.gather_y(1, 0)
+    b.gather_x(2, 2)
+    b.gather_x(3, 1)
     b.gather_x(2, 3)
-    b.back(3)
+    b.twin_x(3)
+    b.twin_x(1)
+    b.twin_own(2)
+    b.twin_own(3)
+    b.twin_y(0)
+    b.gather_y(3, 3)
+    b.gather_y(3, 1)
     b.gather_x(2, 1)
-    b.gather_y(2, 0)
-    b.twin_x(0)
-    b.gather_x(3, 2)
-    b.gather_x(3, 0)
-    b.twin_x(1)
     b.gather_y(2, 3)
-    b.gather_y(2, 2)
-    b.twin_y(0)
-    b.gather_y(3, 2)
-    b.gather_y(3, 3)
-    b.twin_corner(1)
-    b.gather_x(3, 3)
+    b.bias_stage(2)
+    b.twin_x(2)
     b.twin_y(1)
     b.twin_y(2)
-    b.twin_x(2)
-    b.gather_y(3, 1)
+    b.through()
+    b.twin_corner(3)
     b.twin_y(3)
-    b.gather_x(3, 1)
-    b.through()
-    b.twin_x(3)
-    b.twin_corner(0)
+    b.bias_stage(3)
+    b.twin_corner(1)
     b.twin_corner(2)
-    b.twin_own(0)
-    b.twin_corner(3)
-    b.bias_stage(3)
     b.gather_twin()
 
 

time: 118 us -> 114 us (0.966)
  Pallas kernels: 117 us -> 113 us
    pallas_call x1, Pallas kernels: 110 us -> 106 us  [call(): pl.pallas_call(functools.partial(body, plan, names), name=name, out_shape...]
where the time goes in v6:
time: 114 us; the launch traced here: 113 us
  Pallas kernels  113 us (99%)
    pallas_call x1, Pallas kernels, call(): pl.pallas_call(functools.partial(body, plan, names), name=name, out_shape...  106 us
    pallas_call x1, Pallas kernels, on_device(): pl.pallas_call(cast_kernel, name='cast', out_shape=[shaped(low.shape, F32...  6.47 us

profile of v6, /device:TPU:0, one launch (start us, length us, event | category | flops | bytes accessed | tf_op | source)
XLA Modules:
  0.0 113.4 jit_solution(10571025146085724981)
XLA Ops:
  0.6 106.1 %layer.1 = (bf16[128,2048]{1,0:T(8,128)(2,1)S(1)}, f32[128,2048]{1,0:T(8,128)S(1)}, bf16[2048,2048]{1,0:T(8,128)(2,1)S(1)}, f32[1,2048]{1,0:T(1,128)S(1)}) custom-call(bf16[128,2048]{1,0:T(8,128)(2,1)} %refs_0_.1, s32[16,512]{1,0:T(8,128)} %bitcast.4, s32[16,512]{1,0:T(8,128)} %bitcast.5, bf16[2048,2048]{1,0:T(8,128)(2,1)} %refs_3_.1, f32[1,2048]{1,0:T(1,128)} %bitcast.6, ...), custom_call_target="tpu_custom_call" | custom-call | tf_op jit(solution)/shard_map/layer/pallas_call | solution.py:1089
  106.8 6.5 %cast.1 = (f32[2048,2048]{1,0:T(8,128)}, bf16[128,2048]{1,0:T(8,128)(2,1)}, f32[128,2048]{1,0:T(8,128)}, f32[1,2048]{1,0:T(1,128)}) custom-call(bf16[2048,2048]{1,0:T(8,128)(2,1)S(1)} %get-tuple-element.12.low, bf16[128,2048]{1,0:T(8,128)(2,1)S(1)} %get-tuple-element.13.act_in, f32[128,2048]{1,0:T(8,128)S(1)} %get-tuple-element.14.fg_in, ...), custom_call_target="tpu_custom_call" | custom-call | tf_op jit(solution)/shard_map/cast/pallas_call | solution.py:1141

commit v7 on v6

--- a/solution.py
+++ b/solution.py
@@ -732,42 +732,42 @@
 
 def schedule(f, b):
     f.send_slices(0)
+    f.build(0)
+    f.send_codes()
+    f.pass_on(0, 1)
+    f.send_slices(1)
+    f.pass_on(0, 0)
+    f.pass_on(0, 2)
+    f.build(2)
+    f.send_slices(2)
+    f.build(1)
+    f.send_slices(3)
+    f.pass_on(1, 0)
+    f.pass_on(1, 2)
+    f.pass_on(1, 1)
+    f.build(3)
+    f.first(0)
     f.send_counts()
-    f.scale()
-    f.send_codes()
-    f.build(0)
-    f.pass_on(0, 0)
-    f.send_slices(1)
-    f.send_slices(2)
-    f.pass_on(0, 2)
-    f.pass_on(0, 1)
-    f.build(3)
-    f.build(1)
-    f.pass_on(1, 2)
-    f.build(2)
-    f.pass_on(1, 1)
-    f.pass_on(1, 0)
-    f.send_slices(3)
-    f.first(0)
     f.pass_on(2, 2)
     f.own(0)
-    f.pass_on(2, 1)
     f.pass_on(2, 0)
     f.second(0)
+    f.pass_on(2, 1)
     f.first(1)
+    f.pass_on(3, 2)
+    f.pass_on(3, 0)
     f.pass_on(3, 1)
     f.own(1)
-    f.pass_on(3, 0)
     f.second(1)
-    f.pass_on(3, 2)
     f.first(2)
+    f.own(2)
     f.last(0)
-    f.own(2)
+    f.first(3)
     f.second(2)
-    f.first(3)
+    f.own(3)
     f.last(1)
-    f.own(3)
     f.second(3)
+    f.scale()
     f.combine(0)
     f.last(2)
     b.agg_send(0)
@@ -775,151 +775,151 @@
     f.combine(1)
     b.agg_send(1)
     f.last(3)
+    b.pass_agg(0)
     f.add(1)
-    b.pass_agg(0)
     f.combine(2)
-    b.pass_agg(1)
     b.agg_send(2)
     f.add(2)
+    b.pass_agg(1)
     f.combine(3)
     b.agg_send(3)
     f.layer(0)
-    b.pg_y(0)
     f.layer(1)
-    b.pg_x(0)
     f.layer(2)
+    b.pg_x(1)
     f.layer(3)
     b.grads_start(3)
+    b.pg_y(0)
+    b.pass_agg(2)
     b.pg_x(2)
+    b.pass_agg(3)
+    b.pg_x(0)
+    b.grads_start(0)
+    b.grads_start(2)
+    b.pass_pg(0)
     b.pg_y(1)
-    b.grads_start(0)
-    b.pass_agg(2)
-    b.grads_start(2)
-    b.pg_x(1)
-    b.pass_agg(3)
     b.pg_y(2)
+    b.grads_x(3)
+    b.await_agg()
+    b.grads_start(1)
+    b.bias_start()
+    b.tile_part(0)
+    b.pass_pg(1)
     b.pg_y(3)
-    b.pass_pg(0)
-    b.pass_pg(1)
-    b.grads_x(3)
-    b.grads_start(1)
-    b.await_agg()
-    b.tile_part(0)
+    b.grads_x(0)
     b.tile_own(0)
-    b.grads_x(0)
-    b.bias_start()
     b.sum_start(0)
+    b.grads_twin(3)
+    b.pass_pg(2)
+    b.grads_x(2)
     b.tile_part(1)
     b.tile_own(1)
-    b.pass_pg(2)
-    b.grads_twin(3)
     b.bias_stage(0)
+    b.pg_x(3)
+    b.target(3)
+    b.sum_far(0)
     b.sum_start(1)
-    b.target(3)
-    b.grads_x(1)
-    b.sum_far(0)
-    b.pass_pg(3)
-    b.pg_x(3)
     b.grads_twin(0)
-    b.bias_stage(1)
+    b.sum_other(0)
     b.tile_part(2)
-    b.sum_other(0)
     b.target(0)
     b.sum_out(0)
     b.sum_far(1)
+    b.pass_pg(3)
     b.tile_own(2)
-    b.grads_x(2)
     b.sum_start(2)
+    b.bias_stage(1)
+    b.grads_twin(2)
+    b.sum_other(1)
+    b.grads_x(1)
+    b.sum_end(0)
+    b.target(2)
+    b.sum_out(1)
+    b.tile_part(3)
+    b.sum_far(2)
+    b.tile_own(3)
+    b.sum_other(2)
+    b.sum_end(1)
+    b.gather_y(0, 0)
     b.grads_twin(1)
-    b.sum_other(1)
-    b.sum_end(0)
-    b.target(1)
-    b.sum_out(1)
-    b.sum_far(2)
-    b.tile_part(3)
-    b.sum_other(2)
-    b.grads_twin(2)
-    b.sum_end(1)
-    b.tile_own(3)
+    b.target_own(0)
     b.sum_start(3)
     b.gather_line(0, 1)
     b.sum_out(2)
-    b.target(2)
+    b.target(1)
     b.sum_end(2)
-    b.gather_x(1, 0)
     b.gather_line(1, 1)
     b.gather_line(0, 2)
+    b.gather_line(0, 3)
+    b.twin_own(0)
+    b.gather_x(0, 1)
     b.sum_far(3)
+    b.sum_other(3)
+    b.gather_x(0, 0)
+    b.gather_line(2, 2)
     b.gather_line(1, 2)
-    b.gather_x(0, 1)
-    b.gather_line(0, 3)
-    b.gather_y(0, 0)
-    b.gather_line(2, 2)
-    b.target_own(0)
-    b.sum_other(3)
     b.gather_line(2, 1)
-    b.gather_y(2, 0)
+    b.gather_line(1, 3)
     b.sum_out(3)
+    b.gather_x(0, 3)
+    b.sum_end(3)
+    b.gather_x(2, 0)
+    b.target_own(3)
+    b.gather_y(0, 2)
+    b.gather_line(2, 3)
+    b.gather_y(0, 3)
+    b.target_own(2)
+    b.gather_line(3, 2)
+    b.back(0)
     b.gather_y(0, 1)
-    b.sum_end(3)
-    b.twin_own(0)
+    b.target_own(1)
     b.gather_x(1, 1)
-    b.target_own(2)
-    b.gather_line(2, 3)
-    b.gather_x(0, 0)
+    b.back(3)
+    b.twin_own(1)
+    b.gather_x(0, 2)
+    b.bias_stage(2)
+    b.gather_line(3, 1)
+    b.gather_y(1, 3)
+    b.gather_y(1, 0)
+    b.back(1)
+    b.gather_line(3, 3)
+    b.gather_x(2, 1)
+    b.gather_x(1, 0)
     b.gather_y(1, 1)
-    b.gather_line(1, 3)
-    b.gather_x(0, 3)
-    b.target_own(3)
-    b.gather_line(3, 2)
-    b.back(3)
-    b.target_own(1)
-    b.back(0)
-    b.gather_line(3, 1)
-    b.back(1)
-    b.gather_y(0, 3)
-    b.gather_x(0, 2)
-    b.gather_line(3, 3)
-    b.gather_x(3, 2)
+    b.twin_y(0)
+    b.gather_y(1, 2)
     b.gather_x(1, 2)
     b.back(2)
+    b.gather_x(3, 1)
+    b.twin_corner(0)
+    b.gather_y(3, 1)
+    b.gather_x(1, 3)
     b.gather_y(2, 1)
-    b.gather_y(1, 3)
-    b.gather_x(1, 3)
-    b.gather_y(0, 2)
+    b.gather_x(2, 2)
     b.gather_y(3, 0)
+    b.bias_stage(3)
+    b.gather_x(2, 3)
+    b.twin_x(0)
+    b.twin_y(1)
+    b.twin_own(2)
+    b.gather_y(2, 2)
     b.gather_x(3, 0)
+    b.gather_x(3, 2)
+    b.gather_y(2, 3)
+    b.gather_y(2, 0)
     b.gather_x(3, 3)
-    b.twin_own(1)
-    b.gather_y(1, 2)
-    b.gather_y(2, 2)
-    b.gather_x(2, 0)
+    b.twin_y(2)
     b.gather_y(3, 2)
-    b.twin_corner(0)
-    b.twin_x(0)
-    b.gather_y(1, 0)
-    b.gather_x(2, 2)
-    b.gather_x(3, 1)
-    b.gather_x(2, 3)
+    b.gather_y(3, 3)
+    b.twin_y(3)
+    b.twin_own(3)
+    b.twin_x(2)
     b.twin_x(3)
     b.twin_x(1)
-    b.twin_own(2)
-    b.twin_own(3)
-    b.twin_y(0)
-    b.gather_y(3, 3)
-    b.gather_y(3, 1)
-    b.gather_x(2, 1)
-    b.gather_y(2, 3)
-    b.bias_stage(2)
-    b.twin_x(2)
-    b.twin_y(1)
-    b.twin_y(2)
     b.through()
+    b.twin_corner(2)
+    b.twin_corner(1)
     b.twin_corner(3)
-    b.twin_y(3)
-    b.bias_stage(3)
-    b.twin_corner(1)
-    b.twin_corner(2)
     b.gather_twin()
 
 

time: 114 us -> 113 us (level)
  no operation moved by 1% of the time
where the time goes in v7:
time: 113 us
  Pallas kernels  112 us (99%)
    pallas_call x1, Pallas kernels, call(): pl.pallas_call(functools.partial(body, plan, names), name=name, out_shape...  106 us
    pallas_call x1, Pallas kernels, on_device(): pl.pallas_call(cast_kernel, name='cast', out_shape=[shaped(low.shape, F32...  6.47 us

profile of v7, /device:TPU:0, one launch (start us, length us, event | category | flops | bytes accessed | tf_op | source)
XLA Modules:
  0.0 113.0 jit_solution(2307169944792227962)
XLA Ops:
  0.6 105.7 %layer.1 = (bf16[128,2048]{1,0:T(8,128)(2,1)S(1)}, f32[128,2048]{1,0:T(8,128)S(1)}, bf16[2048,2048]{1,0:T(8,128)(2,1)S(1)}, f32[1,2048]{1,0:T(1,128)S(1)}) custom-call(bf16[128,2048]{1,0:T(8,128)(2,1)} %refs_0_.1, s32[16,512]{1,0:T(8,128)} %bitcast.4, s32[16,512]{1,0:T(8,128)} %bitcast.5, bf16[2048,2048]{1,0:T(8,128)(2,1)} %refs_3_.1, f32[1,2048]{1,0:T(1,128)} %bitcast.6, ...), custom_call_target="tpu_custom_call" | custom-call | tf_op jit(solution)/shard_map/layer/pallas_call | solution.py:1089
  106.3 6.5 %cast.1 = (f32[2048,2048]{1,0:T(8,128)}, bf16[128,2048]{1,0:T(8,128)(2,1)}, f32[128,2048]{1,0:T(8,128)}, f32[1,2048]{1,0:T(1,128)}) custom-call(bf16[2048,2048]{1,0:T(8,128)(2,1)S(1)} %get-tuple-element.12.low, bf16[128,2048]{1,0:T(8,128)(2,1)S(1)} %get-tuple-element.13.act_in, f32[128,2048]{1,0:T(8,128)S(1)} %get-tuple-element.14.fg_in, ...), custom_call_target="tpu_custom_call" | custom-call | tf_op jit(solution)/shard_map/cast/pallas_call | solution.py:1141

commit v8 on v7

--- a/solution.py
+++ b/solution.py
@@ -1136,7 +1136,7 @@
             dict({name: (array, v) for name, array in zip(between, kept)}, w_hbm=(weight, far)),
             results, backward_scratch(plan),
         )
-    parts = 8
+    parts = 16
     vmem, hbm = pl.BlockSpec(memory_space=v), pl.BlockSpec(memory_space=far)
     weight_grad, activations, feature_grad, bias_grad = pl.pallas_call(
         cast_kernel,

time: 113 us -> 113 us (level)
  no operation moved by 1% of the time
where the time goes in v8:
time: 113 us
  Pallas kernels  112 us (99%)
    pallas_call x1, Pallas kernels, call(): pl.pallas_call(functools.partial(body, plan, names), name=name, out_shape...  106 us
    pallas_call x1, Pallas kernels, on_device(): pl.pallas_call(cast_kernel, name='cast', out_shape=[shaped(low.shape, F32...  6.48 us

profile of v8, /device:TPU:0, one launch (start us, length us, event | category | flops | bytes accessed | tf_op | source)
XLA Modules:
  0.0 113.0 jit_solution(13084482490261170752)
XLA Ops:
  0.6 105.7 %layer.1 = (bf16[128,2048]{1,0:T(8,128)(2,1)S(1)}, f32[128,2048]{1,0:T(8,128)S(1)}, bf16[2048,2048]{1,0:T(8,128)(2,1)S(1)}, f32[1,2048]{1,0:T(1,128)S(1)}) custom-call(bf16[128,2048]{1,0:T(8,128)(2,1)} %refs_0_.1, s32[16,512]{1,0:T(8,128)} %bitcast.4, s32[16,512]{1,0:T(8,128)} %bitcast.5, bf16[2048,2048]{1,0:T(8,128)(2,1)} %refs_3_.1, f32[1,2048]{1,0:T(1,128)} %bitcast.6, ...), custom_call_target="tpu_custom_call" | custom-call | tf_op jit(solution)/shard_map/layer/pallas_call | solution.py:1089
  106.3 6.5 %cast.1 = (f32[2048,2048]{1,0:T(8,128)}, bf16[128,2048]{1,0:T(8,128)(2,1)}, f32[128,2048]{1,0:T(8,128)}, f32[1,2048]{1,0:T(1,128)}) custom-call(bf16[2048,2048]{1,0:T(8,128)(2,1)S(1)} %get-tuple-element.12.low, bf16[128,2048]{1,0:T(8,128)(2,1)S(1)} %get-tuple-element.13.act_in, f32[128,2048]{1,0:T(8,128)S(1)} %get-tuple-element.14.fg_in, ...), custom_call_target="tpu_custom_call" | custom-call | tf_op jit(solution)/shard_map/cast/pallas_call | solution.py:1141
